TPU v7x, 128 devices: a whole 4x4x4 slice. The times are simulated.
128 devices in a mesh: fsdp: 128 (over x, z, y, core).
Axes of the slice: x: 4, y: 4, z: 4, core: 2. Of those that a mesh axis runs over, the one named last changes fastest.
Arguments:
- tokens: bfloat16 [16384, 1536], P('fsdp'), may hold values from -6 to 6
- expert_ids: int32 [16384, 6], P('fsdp'), may hold values from 0 to 7, all different within a row; in each aligned block of 128 rows (0 to 127, 128 to 255, ...) at most 128 rows name the same one
- attn_gain: bfloat16 [1536], P('fsdp'), may hold values from 0.099609375 to 1.8984375
- w_qkv: bfloat16 [1536, 2560], P('fsdp'), may hold values from -0.15625 to 0.15625
- w_out: bfloat16 [1536, 1536], P('fsdp'), may hold values from -0.625 to 0.625
- moe_gain: bfloat16 [1536], P('fsdp'), may hold values from 0.099609375 to 1.8984375
- w_router: bfloat16 [1536, 8], P('fsdp'), may hold values from -0.078125 to 0.078125
- w_shared_in: bfloat16 [1536, 2048], P('fsdp'), may hold values from -0.15625 to 0.15625
- w_shared_out: bfloat16 [1536, 1024], P('fsdp'), may hold values from -0.1875 to 0.1875
- w_expert_in: bfloat16 [12288, 1024], P('fsdp'), may hold values from -0.15625 to 0.15625
- w_expert_out: bfloat16 [12288, 512], P('fsdp'), may hold values from -0.25 to 0.25
- out_grad: bfloat16 [16384, 1536], P('fsdp'), may hold values from -6 to 6
Outputs:
- block_out: bfloat16 [16384, 1536], P('fsdp')
- tokens_grad: float32 [16384, 1536], P('fsdp')
- attn_gain_grad: float32 [1536], P('fsdp')
- w_qkv_grad: float32 [1536, 2560], P('fsdp')
- w_out_grad: float32 [1536, 1536], P('fsdp')
- moe_gain_grad: float32 [1536], P('fsdp')
- w_router_grad: float32 [1536, 8], P('fsdp')
- w_shared_in_grad: float32 [1536, 2048], P('fsdp')
- w_shared_out_grad: float32 [1536, 1024], P('fsdp')
- w_expert_in_grad: float32 [12288, 1024], P('fsdp')
- w_expert_out_grad: float32 [12288, 512], P('fsdp')
Inputs may be any that keep to these rules, and one draw needn't show every extreme that they name: `expert_ids`: each row names 6 different experts. Among the rows of one device no expert is named by more than 128 rows, and this bound is reached.
All inputs are finite; a program needn't handle non-finite values.
Results may differ from a plain program's by a relative error of at most 0.02.
Values may be sent and summed in bfloat16 or wider, within the bound.
A program may use at most 384 MiB of HBM per device.

v0:
```python
import jax
import jax.numpy as jnp
from jax import lax
from jax.sharding import PartitionSpec as P

D = 1536
HQ = 12
KV = 4
HD = 128
H = 512
SH = 1024
EXPERTS = 8
TOP = 6
CAP = 128


epsilon = 1e-05


def swish_parts(joined, width):
    gate_part = joined[..., :width].astype(jnp.float32)
    up_part = joined[..., width:].astype(jnp.float32)
    return (gate_part, up_part, jax.nn.sigmoid(gate_part))


def swish_forward(joined, width):
    gate_part, up_part, sig_gate = swish_parts(joined, width)
    return (gate_part * sig_gate * up_part).astype(jnp.bfloat16)


def swish_backward(joined, width, act_grad):
    gate_part, up_part, sig_gate = swish_parts(joined, width)
    gate_slope = sig_gate * (1.0 + gate_part * (1.0 - sig_gate))
    return jnp.concatenate(
        [act_grad * up_part * gate_slope, act_grad * gate_part * sig_gate], axis=-1
    ).astype(jnp.bfloat16)


def causal_scores(query_rows, key_rows, length):
    scores = jnp.einsum(
        "qkgd,skd->kgqs", query_rows, key_rows, preferred_element_type=jnp.float32
    ) * HD ** (-0.5)
    causal = jnp.arange(length)[:, None] >= jnp.arange(length)[None, :]
    return jnp.where(causal, scores, -1e30)


def slot_numbers(expert_ids):
    flat_ids = expert_ids.reshape(-1)
    one_hot = (flat_ids[:, None] == jnp.arange(EXPERTS, dtype=jnp.int32)[None, :]).astype(jnp.int32)
    before = jnp.cumsum(one_hot, axis=0) - one_hot
    return (flat_ids, jnp.sum(before * one_hot, axis=1))


def rms_backward(values, inverse, gain, grad_in):
    scaled = gain * grad_in
    gain_grad = jnp.sum(grad_in * values * inverse, axis=0)
    value_grad = inverse * scaled - values * inverse**3 * jnp.mean(
        scaled * values, axis=-1, keepdims=True
    )
    return (gain_grad, value_grad)


def local(
    tokens,
    expert_ids,
    attn_gain,
    w_qkv,
    w_out,
    moe_gain,
    w_router,
    w_shared_in,
    w_shared_out,
    w_expert_in,
    w_expert_out,
    out_grad,
):
    dense_full = (
        lax.all_gather(attn_gain, "fsdp", axis=0, tiled=True),
        lax.all_gather(w_qkv, "fsdp", axis=0, tiled=True),
        lax.all_gather(w_out, "fsdp", axis=0, tiled=True),
        lax.all_gather(moe_gain, "fsdp", axis=0, tiled=True),
        lax.all_gather(w_router, "fsdp", axis=0, tiled=True),
        lax.all_gather(w_shared_in, "fsdp", axis=0, tiled=True),
        lax.all_gather(w_shared_out, "fsdp", axis=0, tiled=True),
    )
    experts = (
        lax.all_gather(w_expert_in, "fsdp", axis=0, tiled=True),
        lax.all_gather(w_expert_out, "fsdp", axis=0, tiled=True),
    )
    length = tokens.shape[0]
    group_size = HQ // KV
    score_scale = HD ** (-0.5)
    inputs = tokens.astype(jnp.float32)
    gain_one = dense_full[0].astype(jnp.float32)
    inverse_one = lax.rsqrt(jnp.mean(inputs * inputs, axis=-1, keepdims=True) + epsilon)
    normed = (inputs * inverse_one * gain_one).astype(jnp.bfloat16)
    qkv_low = jnp.dot(normed, dense_full[1], preferred_element_type=jnp.float32).astype(
        jnp.bfloat16
    )
    query_rows = qkv_low[:, : HQ * HD].reshape(length, KV, group_size, HD)
    key_rows = qkv_low[:, HQ * HD : (HQ + KV) * HD].reshape(length, KV, HD)
    value_rows = qkv_low[:, (HQ + KV) * HD :].reshape(length, KV, HD)
    scores = causal_scores(query_rows, key_rows, length)
    row_peak = jnp.max(scores, axis=-1, keepdims=True)
    exponent = jnp.exp(scores - row_peak)
    totals = jnp.sum(exponent, axis=-1, keepdims=True)
    log_total = row_peak + jnp.log(totals)
    probs_low = (exponent / totals).astype(jnp.bfloat16)
    head_mix = jnp.einsum(
        "kgqs,skd->qkgd", probs_low, value_rows, preferred_element_type=jnp.float32
    )
    head_mix = head_mix.reshape(length, HQ * HD).astype(jnp.bfloat16)
    hidden = inputs + jnp.einsum(
        "sa,da->sd", head_mix, dense_full[2], preferred_element_type=jnp.float32
    )
    gain_two = dense_full[3].astype(jnp.float32)
    inverse_two = lax.rsqrt(jnp.mean(hidden * hidden, axis=-1, keepdims=True) + epsilon)
    moe_in = (hidden * inverse_two * gain_two).astype(jnp.bfloat16)
    logits = jnp.dot(moe_in, dense_full[4], preferred_element_type=jnp.float32)
    router_probs = jax.nn.softmax(logits, axis=-1)
    choose = (expert_ids[:, :, None] == jnp.arange(EXPERTS)[None, None, :]).astype(jnp.float32)
    gate_weights = jnp.sum(choose * router_probs[:, None, :], axis=-1)
    flat_ids, slot_index = slot_numbers(expert_ids)
    owner_row = jnp.arange(length * TOP) // TOP
    dispatched = (
        jnp.zeros((EXPERTS, CAP, D), jnp.bfloat16).at[flat_ids, slot_index].set(moe_in[owner_row])
    )
    expert_in = experts[0].reshape(EXPERTS, D, 2 * H)
    expert_back = experts[1].reshape(EXPERTS, D, H)
    gate_up = jnp.einsum(
        "ecd,edh->ech", dispatched, expert_in, preferred_element_type=jnp.float32
    ).astype(jnp.bfloat16)
    expert_act = swish_forward(gate_up, H)
    expert_out = jnp.einsum(
        "ech,edh->ecd", expert_act, expert_back, preferred_element_type=jnp.float32
    ).astype(jnp.bfloat16)
    picked = expert_out[flat_ids, slot_index].reshape(length, TOP, D)
    routed = jnp.sum(gate_weights[:, :, None] * picked, axis=1)
    shared_gate_up = jnp.dot(moe_in, dense_full[5], preferred_element_type=jnp.float32).astype(
        jnp.bfloat16
    )
    shared_act = swish_forward(shared_gate_up, SH)
    shared_branch = jnp.einsum(
        "sf,df->sd", shared_act, dense_full[6], preferred_element_type=jnp.float32
    )
    block_out = (hidden + shared_branch + routed).astype(jnp.bfloat16)
    dense_full = (
        lax.all_gather(attn_gain, "fsdp", axis=0, tiled=True),
        lax.all_gather(w_qkv, "fsdp", axis=0, tiled=True),
        lax.all_gather(w_out, "fsdp", axis=0, tiled=True),
        lax.all_gather(moe_gain, "fsdp", axis=0, tiled=True),
        lax.all_gather(w_router, "fsdp", axis=0, tiled=True),
        lax.all_gather(w_shared_in, "fsdp", axis=0, tiled=True),
        lax.all_gather(w_shared_out, "fsdp", axis=0, tiled=True),
    )
    experts = (
        lax.all_gather(w_expert_in, "fsdp", axis=0, tiled=True),
        lax.all_gather(w_expert_out, "fsdp", axis=0, tiled=True),
    )
    expert_in = experts[0].reshape(EXPERTS, D, 2 * H)
    expert_back = experts[1].reshape(EXPERTS, D, H)
    cotangent = out_grad.astype(jnp.float32)
    gate_grad = jnp.sum(picked * cotangent[:, None, :], axis=-1)
    placed_grad = (
        (gate_weights[:, :, None] * cotangent[:, None, :])
        .reshape(length * TOP, D)
        .astype(jnp.bfloat16)
    )
    expert_out_grad = (
        jnp.zeros((EXPERTS, CAP, D), jnp.bfloat16).at[flat_ids, slot_index].set(placed_grad)
    )
    expert_back_grad = jnp.einsum(
        "ecd,ech->edh", expert_out_grad, expert_act, preferred_element_type=jnp.float32
    )
    act_grad = jnp.einsum(
        "ecd,edh->ech", expert_out_grad, expert_back, preferred_element_type=jnp.float32
    )
    gate_up_grad = swish_backward(gate_up, H, act_grad)
    expert_in_grad = jnp.einsum(
        "ecd,ech->edh", dispatched, gate_up_grad, preferred_element_type=jnp.float32
    )
    dispatched_grad = jnp.einsum(
        "ech,edh->ecd", gate_up_grad, expert_in, preferred_element_type=jnp.float32
    )
    routed_in_grad = jnp.sum(dispatched_grad[flat_ids, slot_index].reshape(length, TOP, D), axis=1)
    shared_out_grad = jnp.einsum(
        "sd,sf->df", out_grad, shared_act, preferred_element_type=jnp.float32
    )
    shared_act_grad = jnp.dot(out_grad, dense_full[6], preferred_element_type=jnp.float32)
    shared_grad = swish_backward(shared_gate_up, SH, shared_act_grad)
    shared_in_grad = jnp.einsum(
        "sd,sf->df", moe_in, shared_grad, preferred_element_type=jnp.float32
    )
    shared_to_input = jnp.einsum(
        "sf,df->sd", shared_grad, dense_full[5], preferred_element_type=jnp.float32
    )
    prob_grad = jnp.sum(choose * gate_grad[:, :, None], axis=1)
    logit_grad = router_probs * (
        prob_grad - jnp.sum(router_probs * prob_grad, axis=-1, keepdims=True)
    )
    logit_grad = logit_grad.astype(jnp.bfloat16)
    router_grad = jnp.einsum("sd,se->de", moe_in, logit_grad, preferred_element_type=jnp.float32)
    router_to_input = jnp.einsum(
        "se,de->sd", logit_grad, dense_full[4], preferred_element_type=jnp.float32
    )
    moe_in_grad = routed_in_grad + shared_to_input + router_to_input
    gain_two_grad, hidden_part = rms_backward(hidden, inverse_two, gain_two, moe_in_grad)
    hidden_grad = cotangent + hidden_part
    hidden_low = hidden_grad.astype(jnp.bfloat16)
    out_proj_grad = jnp.einsum(
        "sd,sa->da", hidden_low, head_mix, preferred_element_type=jnp.float32
    )
    mix_grad = jnp.dot(hidden_low, dense_full[2], preferred_element_type=jnp.float32).astype(
        jnp.bfloat16
    )
    mix_grad = mix_grad.reshape(length, KV, group_size, HD)
    scores_again = causal_scores(query_rows, key_rows, length)
    probs = jnp.exp(scores_again - log_total)
    prob_att_grad = jnp.einsum(
        "qkgd,skd->kgqs", mix_grad, value_rows, preferred_element_type=jnp.float32
    )
    value_grad = jnp.einsum(
        "kgqs,qkgd->skd", probs.astype(jnp.bfloat16), mix_grad, preferred_element_type=jnp.float32
    )
    row_delta = jnp.sum(probs * prob_att_grad, axis=-1, keepdims=True)
    score_grad = (probs * (prob_att_grad - row_delta)).astype(jnp.bfloat16)
    query_grad = (
        jnp.einsum("kgqs,skd->qkgd", score_grad, key_rows, preferred_element_type=jnp.float32)
        * score_scale
    )
    key_grad = (
        jnp.einsum("kgqs,qkgd->skd", score_grad, query_rows, preferred_element_type=jnp.float32)
        * score_scale
    )
    qkv_grad = jnp.concatenate(
        [
            query_grad.reshape(length, HQ * HD),
            key_grad.reshape(length, KV * HD),
            value_grad.reshape(length, KV * HD),
        ],
        axis=1,
    ).astype(jnp.bfloat16)
    qkv_weight_grad = jnp.einsum("sd,sc->dc", normed, qkv_grad, preferred_element_type=jnp.float32)
    normed_grad = jnp.einsum(
        "sc,dc->sd", qkv_grad, dense_full[1], preferred_element_type=jnp.float32
    )
    gain_one_grad, input_part = rms_backward(inputs, inverse_one, gain_one, normed_grad)
    tokens_grad = hidden_grad + input_part
    summed = (
        lax.psum_scatter(gain_one_grad, "fsdp", scatter_dimension=0, tiled=True),
        lax.psum_scatter(qkv_weight_grad, "fsdp", scatter_dimension=0, tiled=True),
        lax.psum_scatter(out_proj_grad, "fsdp", scatter_dimension=0, tiled=True),
        lax.psum_scatter(gain_two_grad, "fsdp", scatter_dimension=0, tiled=True),
        lax.psum_scatter(router_grad, "fsdp", scatter_dimension=0, tiled=True),
        lax.psum_scatter(shared_in_grad, "fsdp", scatter_dimension=0, tiled=True),
        lax.psum_scatter(shared_out_grad, "fsdp", scatter_dimension=0, tiled=True),
        lax.psum_scatter(
            expert_in_grad.reshape(EXPERTS * D, 2 * H), "fsdp", scatter_dimension=0, tiled=True
        ),
        lax.psum_scatter(
            expert_back_grad.reshape(EXPERTS * D, H), "fsdp", scatter_dimension=0, tiled=True
        ),
    )
    return (
        block_out,
        tokens_grad,
        summed[0],
        summed[1],
        summed[2],
        summed[3],
        summed[4],
        summed[5],
        summed[6],
        summed[7],
        summed[8],
    )


def solution(mesh):
    return jax.shard_map(
        local,
        mesh=mesh,
        in_specs=(
            P("fsdp", None),
            P("fsdp", None),
            P("fsdp"),
            P("fsdp", None),
            P("fsdp", None),
            P("fsdp"),
            P("fsdp", None),
            P("fsdp", None),
            P("fsdp", None),
            P("fsdp", None),
            P("fsdp", None),
            P("fsdp", None),
        ),
        out_specs=(
            P("fsdp", None),
            P("fsdp", None),
            P("fsdp"),
            P("fsdp", None),
            P("fsdp", None),
            P("fsdp"),
            P("fsdp", None),
            P("fsdp", None),
            P("fsdp", None),
            P("fsdp", None),
            P("fsdp", None),
        ),
        check_vma=False,
    )
```

profile of v0, /device:TPU:8, one launch (start us, length us, event | category | flops | bytes accessed | tf_op | source)
XLA Modules:
  0.0 1694.1 jit_solution(5245008209324685165)
XLA Ops:
  14.1 67.7 %all-reduce.13 = (bf16[1536]{0:T(1024)(128)(2,1)S(1)}, bf16[1536]{0:T(1024)(128)(2,1)S(1)}) all-reduce(bf16[1536]{0:T(1024)(128)(2,1)S(1)} %dynamic-update-slice, bf16[1536]{0:T(1024)(128)(2,1)S(1)} %dynamic-update-slice.1), channel_id=1, replica_groups=mesh['fsdp'=128] {'fsdp'}, use_global_device_ids=true, to_apply=%add | all-reduce | flops 3072 | bytes 12288
  84.1 33.2 %all-gather.4 = bf16[128,12,8]{1,2,0:T(8,128)(2,1)S(1)} all-gather(bf16[1,12,8]{1,2,0:T(8,128)(2,1)} %bitcast.130), channel_id=1, replica_groups=mesh['fsdp'=128] {'fsdp'}, dimensions={0}, use_global_device_ids=true | all-gather | bytes 24768 | tf_op jit(solution)/shard_map/all_gather | solution.py:82
  117.6 4.5 mul.281
  122.1 6.6 mul.282
  129.6 8.4 reshape.297
  138.0 13.3 all-gather.20.cloned.1.call-done
  151.3 10.7 reshape.299
  162.0 62.1 %all-gather.16.cloned.1.call-done = bf16[128,12,2560]{2,1,0:T(8,128)(2,1)} async-done(((bf16[1,12,2560]{2,1,0:T(8,128)(2,1)}), bf16[128,12,2560]{2,1,0:T(8,128)(2,1)}) %all-gather.16.cloned.1.call-update) | async-done | bytes 7864336 | tf_op jit(solution)/shard_map/all_gather | solution.py:79
  224.1 12.8 reshape.295
  236.9 4.5 convolution_convert_fusion.1
  243.6 4.6 multiply_reduce_fusion.5
  260.0 87.2 %scatter_fusion = bf16[8,128,1536]{2,1,0:T(8,128)(2,1)S(1)} fusion(bf16[8,128,1536]{2,1,0:T(8,128)(2,1)S(1)} %broadcast.198.clone, s32[768]{0:T(1024)S(1)} %get-tuple-element.73, bf16[768,1536]{1,0:T(8,128)(2,1)} %gather_fusion), kind=kCustom, calls=%fused_computation.3 | custom fusion | bytes 7084032 | tf_op jit(solution)/shard_map/scatter | solution.py:126
  353.2 123.5 %scatter_fusion.1 = bf16[8,128,1536]{2,1,0:T(8,128)(2,1)} fusion(bf16[8,128,1536]{2,1,0:T(8,128)(2,1)} %broadcast.198.clone.1, s32[768]{0:T(1024)S(1)} %get-tuple-element.73, bf16[768,1536]{1,0:T(8,128)(2,1)} %multiply_convert_fusion), kind=kCustom, calls=%fused_computation.4 | custom fusion | bytes 7084032 | tf_op jit(solution)/shard_map/scatter | solution.py:170
  476.7 12.2 convolution_convert_fusion.4
  488.9 10.6 fusion.72
  499.6 10.0 fusion.7
  509.6 21.4 %fusion.15 = f32[8,1536,1024]{2,1,0:T(8,128)} fusion(bf16[8,128,1536]{2,1,0:T(8,128)(2,1)S(1)} %scatter_fusion, bf16[8,128,512]{2,1,0:T(8,128)(2,1)} %get-tuple-element.86, bf16[8,128,512]{2,1,0:T(8,128)(2,1)} %get-tuple-element.85), kind=kOutput, calls=%fused_computation.42 | convolution fusion | flops 3225419776 | bytes 55574528 | tf_op jit(solution)/shard_map/ecd,ech->edh/dot_general | solution.py:179
  533.0 6.2 reshape.301
  542.7 6.4 fusion.46
  549.2 9.5 convolution_convert_fusion
  558.7 12.4 gather_fusion.1
  571.1 5.4 reshape.257
  576.6 5.7 multiply_reduce_fusion
  582.4 15.1 fusion.16
  597.5 13.3 gather_fusion.2
  610.7 6.3 reshape.250
  617.2 4.9 reduce_sum.154
  622.2 5.1 convolution_add_fusion.3
  634.0 5.1 fusion.49
  639.1 8.1 fusion.47
  647.2 436.7 %fusion.76 = (f32[16,2560]{1,0:T(8,128)S(1)}, f32[16,1536]{1,0:T(8,128)S(1)}, f32[16,2048]{1,0:T(8,128)}) fusion(f32[1536,2560]{1,0:T(8,128)} %fusion.47, f32[1536,1536]{1,0:T(8,128)} %fusion.49, f32[1536,2048]{1,0:T(8,128)} %fusion.46), kind=kCustom, calls=%all-reduce-scatter.3 | all-reduce-scatter fusion | flops 12582913 | bytes 38141952
  1095.7 16.6 collective-permute-start.54
  1112.4 7.2 collective-permute-start.53
  1119.7 5.0 collective-permute-start.52
  1130.9 5.8 collective-permute-start.49
  1150.6 9.6 collective-permute-start.43
  1161.8 4.9 collective-permute-start.41
  1175.4 4.6 collective-permute-start.37
  1181.3 5.2 collective-permute-start.35
  1194.7 5.2 collective-permute-start.93
  1211.9 20.6 %collective-permute-start.92 = (f32[16,2048]{1,0:T(8,128)}, f32[16,2048]{1,0:T(8,128)}, u32[]{:S(2)}, u32[]{:S(2)}) collective-permute-start(f32[16,2048]{1,0:T(8,128)} %get-tuple-element.84), channel_id=1, source_target_pairs={{0,29},{1,30},{2,31},{3,32},{4,33},{5,34},{6,35},{7,36},{8,37},{9,... | collective-permute-start | bytes 393224
  1242.1 9.2 collective-permute-start.86
  1251.3 5.3 collective-permute-start.85
  1267.0 14.6 collective-permute-start.80
  1283.6 5.8 collective-permute-start.78
  1295.1 7.8 collective-permute-start.75
  1310.2 6.2 collective-permute-start.71
  1318.4 5.8 collective-permute-start.69
  1324.1 6.8 collective-permute-start.68
  1347.4 6.2 fusion.31
  1355.0 4.7 collective-permute-start.28
  1373.2 6.2 collective-permute-start.21
  1387.2 4.5 collective-permute-start.18
  1391.7 4.6 collective-permute-start.17
  1396.3 8.0 collective-permute-start.16
  1404.4 4.4 collective-permute-start.15
  1410.8 5.9 collective-permute-start.14
  1419.0 8.5 collective-permute-start.12
  1433.6 69.5 %all-reduce.12 = (f32[1536]{0:T(1024)S(1)}, f32[1536]{0:T(1024)S(1)}, f32[1536,8]{0,1:T(8,128)S(1)}) all-reduce(f32[1536]{0:T(1024)S(1)} %get-tuple-element.70, f32[1536]{0:T(1024)S(1)} %copy-done.122, f32[1536,8]{0,1:T(8,128)S(1)} %fusion.80), channel_id=2, replica_groups=mesh['fsdp'=128] {'fsdp'}, use_global_device_ids=true, to_apply=%region_21.22.clone | all-reduce | flops 15360 | bytes 122880
  1504.8 31.7 %concatenate.31 = f32[524,1536]{1,0:T(8,128)S(1)} concatenate(f32[12,1536]{1,0:T(8,128)} %copy-done.84, f32[16,1536]{1,0:T(8,128)} %copy-done.85, f32[16,1536]{1,0:T(8,128)} %copy-done.86, f32[16,1536]{1,0:T(8,128)} %copy-done.87, f32[16,1536]{1,0:T(8,128)} %copy-done.88, f32[16,1536]{1,0:T(8,128)} %copy-done.89, f32[16,1536]{1,0:T(8,128)} %copy-done.90, f32[16,1536]{1,0:T(8,128)} %copy-done.91, ...), dimensions={0} | concatenate | bytes 6438912
  1545.1 4.9 collective-permute-start.6
  1554.0 55.5 %concatenate.32 = f32[524,2048]{1,0:T(8,128)} concatenate(f32[12,2048]{1,0:T(8,128)} %copy-done.76, f32[16,2048]{1,0:T(8,128)} %copy-done.75, f32[16,2048]{1,0:T(8,128)} %collective-permute-done.93, f32[16,2048]{1,0:T(8,128)} %collective-permute-done.92, f32[16,2048]{1,0:T(8,128)} %collective-permute-done.91, f32[16,2048]{1,0:T(8,128)} %copy-done.77, ...), dimensions={0} | concatenate | bytes 8585216
  1614.7 4.4 collective-permute-start.2
  1630.5 55.0 %concatenate.30 = f32[524,2560]{1,0:T(8,128)} concatenate(f32[12,2560]{1,0:T(8,128)S(1)} %copy-done.41, f32[16,2560]{1,0:T(8,128)S(1)} %copy-done.43, f32[16,2560]{1,0:T(8,128)S(1)} %copy-done.45, f32[16,2560]{1,0:T(8,128)S(1)} %copy-done.47, f32[16,2560]{1,0:T(8,128)S(1)} %copy-done.49, f32[16,2560]{1,0:T(8,128)S(1)} %copy-done.51, f32[16,2560]{1,0:T(8,128)S(1)} %copy-done.53, ...), dimensions={0} | concatenate | bytes 10731520
  (545 shorter events, 223.0 us)
Async XLA Ops:
  7.2 122.4 %all-gather.18.cloned.1.call-start = ((), (), s32[]{:S(2)}) async-start(), calls=%async_computation.7 | async-start | bytes 6340608 | tf_op jit(solution)/shard_map/all_gather | solution.py:80
  7.9 143.4 %all-gather.20.cloned.1.call-start = ((), (), s32[]{:S(2)}) async-start(), calls=%async_computation.8 | async-start | bytes 8454144 | tf_op jit(solution)/shard_map/all_gather | solution.py:83
  8.7 215.5 %all-gather.16.cloned.1.call-start = ((), (), s32[]{:S(2)}) async-start(), calls=%async_computation.6 | async-start | bytes 10567680 | tf_op jit(solution)/shard_map/all_gather | solution.py:79
  9.4 467.3 %all-gather.12.cloned.1.call-start = ((), (), s32[]{:S(2)}) async-start(), calls=%async_computation.2 | async-start | bytes 25362432 | tf_op jit(solution)/shard_map/all_gather | solution.py:87
  10.0 489.6 %all-gather.14.cloned.1.call-start = ((), (), s32[]{:S(2)}) async-start(), calls=%async_computation.3 | async-start | bytes 12681216 | tf_op jit(solution)/shard_map/all_gather | solution.py:88
  10.6 522.4 %all-gather.22.cloned.1.call-start = ((), (), s32[]{:S(2)}) async-start(), calls=%async_computation.9 | async-start | bytes 4227072 | tf_op jit(solution)/shard_map/all_gather | solution.py:84
  11.1 1319.8 %all-reduce.17.cloned.1.call-start = ((), (), s32[]{:S(2)}) async-start(), calls=%async_computation.10 | async-start | bytes 12582912
  254.9 1432.3 %reduce-scatter.13.cloned.1.call-start = ((), (), s32[]{:S(2)}) async-start(), calls=%async_computation.5 | async-start | bytes 25362432 | tf_op jit(solution)/shard_map/reduce_scatter | solution.py:260
  499.5 1187.6 %reduce-scatter.11.cloned.1.call-start = ((), (), s32[]{:S(2)}) async-start(), calls=%async_computation.4 | async-start | bytes 50724864 | tf_op jit(solution)/shard_map/reduce_scatter | solution.py:257
  1090.5 22.0 %collective-permute-start.58 = (f32[16,1536]{1,0:T(8,128)S(1)}, f32[16,1536]{1,0:T(8,128)S(1)}, u32[]{:S(2)}, u32[]{:S(2)}) collective-permute-start(f32[16,1536]{1,0:T(8,128)S(1)} %get-tuple-element.83), channel_id=1, source_target_pairs={{0,27},{1,28},{2,29},{3,30},{4,31},{5,32},{6,33},{7,34},{8,35},{9,... | collective-permute-start | bytes 294920
  1091.8 27.9 %collective-permute-start.57 = (f32[16,1536]{1,0:T(8,128)S(1)}, f32[16,1536]{1,0:T(8,128)S(1)}, u32[]{:S(2)}, u32[]{:S(2)}) collective-permute-start(f32[16,1536]{1,0:T(8,128)S(1)} %get-tuple-element.83), channel_id=1, source_target_pairs={{0,26},{1,27},{2,28},{3,29},{4,30},{5,31},{6,32},{7,33},{8,34},{9,... | collective-permute-start | bytes 294920
  1093.1 31.6 %collective-permute-start.56 = (f32[16,1536]{1,0:T(8,128)S(1)}, f32[16,1536]{1,0:T(8,128)S(1)}, u32[]{:S(2)}, u32[]{:S(2)}) collective-permute-start(f32[16,1536]{1,0:T(8,128)S(1)} %get-tuple-element.83), channel_id=1, source_target_pairs={{0,25},{1,26},{2,27},{3,28},{4,29},{5,30},{6,31},{7,32},{8,33},{9,... | collective-permute-start | bytes 294920
  1094.4 33.2 %collective-permute-start.55 = (f32[16,1536]{1,0:T(8,128)S(1)}, f32[16,1536]{1,0:T(8,128)S(1)}, u32[]{:S(2)}, u32[]{:S(2)}) collective-permute-start(f32[16,1536]{1,0:T(8,128)S(1)} %get-tuple-element.83), channel_id=1, source_target_pairs={{0,24},{1,25},{2,26},{3,27},{4,28},{5,29},{6,30},{7,31},{8,32},{9,... | collective-permute-start | bytes 294920
  1095.7 35.1 %collective-permute-start.54 = (f32[16,1536]{1,0:T(8,128)S(1)}, f32[16,1536]{1,0:T(8,128)S(1)}, u32[]{:S(2)}, u32[]{:S(2)}) collective-permute-start(f32[16,1536]{1,0:T(8,128)S(1)} %get-tuple-element.83), channel_id=1, source_target_pairs={{0,23},{1,24},{2,25},{3,26},{4,27},{5,28},{6,29},{7,30},{8,31},{9,... | collective-permute-start | bytes 294920
  1112.4 24.3 %collective-permute-start.53 = (f32[16,1536]{1,0:T(8,128)S(1)}, f32[16,1536]{1,0:T(8,128)S(1)}, u32[]{:S(2)}, u32[]{:S(2)}) collective-permute-start(f32[16,1536]{1,0:T(8,128)S(1)} %get-tuple-element.83), channel_id=1, source_target_pairs={{0,22},{1,23},{2,24},{3,25},{4,26},{5,27},{6,28},{7,29},{8,30},{9,... | collective-permute-start | bytes 294920
  1119.7 19.6 %collective-permute-start.52 = (f32[16,1536]{1,0:T(8,128)S(1)}, f32[16,1536]{1,0:T(8,128)S(1)}, u32[]{:S(2)}, u32[]{:S(2)}) collective-permute-start(f32[16,1536]{1,0:T(8,128)S(1)} %get-tuple-element.83), channel_id=1, source_target_pairs={{0,21},{1,22},{2,23},{3,24},{4,25},{5,26},{6,27},{7,28},{8,29},{9,... | collective-permute-start | bytes 294920
  1139.3 20.9 %collective-permute-start.47 = (f32[16,1536]{1,0:T(8,128)S(1)}, f32[16,1536]{1,0:T(8,128)S(1)}, u32[]{:S(2)}, u32[]{:S(2)}) collective-permute-start(f32[16,1536]{1,0:T(8,128)S(1)} %get-tuple-element.83), channel_id=1, source_target_pairs={{0,16},{1,17},{2,18},{3,19},{4,20},{5,21},{6,22},{7,23},{8,24},{9,... | collective-permute-start | bytes 294920
  1146.2 20.5 %collective-permute-start.45 = (f32[16,1536]{1,0:T(8,128)S(1)}, f32[16,1536]{1,0:T(8,128)S(1)}, u32[]{:S(2)}, u32[]{:S(2)}) collective-permute-start(f32[16,1536]{1,0:T(8,128)S(1)} %get-tuple-element.83), channel_id=1, source_target_pairs={{0,14},{1,15},{2,16},{3,17},{4,18},{5,19},{6,20},{7,21},{8,22},{9,... | collective-permute-start | bytes 294920
  1149.2 19.5 %collective-permute-start.44 = (f32[16,1536]{1,0:T(8,128)S(1)}, f32[16,1536]{1,0:T(8,128)S(1)}, u32[]{:S(2)}, u32[]{:S(2)}) collective-permute-start(f32[16,1536]{1,0:T(8,128)S(1)} %get-tuple-element.83), channel_id=1, source_target_pairs={{0,13},{1,14},{2,15},{3,16},{4,17},{5,18},{6,19},{7,20},{8,21},{9,... | collective-permute-start | bytes 294920
  1150.6 20.4 %collective-permute-start.43 = (f32[16,1536]{1,0:T(8,128)S(1)}, f32[16,1536]{1,0:T(8,128)S(1)}, u32[]{:S(2)}, u32[]{:S(2)}) collective-permute-start(f32[16,1536]{1,0:T(8,128)S(1)} %get-tuple-element.83), channel_id=1, source_target_pairs={{0,12},{1,13},{2,14},{3,15},{4,16},{5,17},{6,18},{7,19},{8,20},{9,... | collective-permute-start | bytes 294920
  1193.4 42.8 %collective-permute-start.94 = (f32[16,2048]{1,0:T(8,128)}, f32[16,2048]{1,0:T(8,128)S(1)}, u32[]{:S(2)}, u32[]{:S(2)}) collective-permute-start(f32[16,2048]{1,0:T(8,128)} %get-tuple-element.84), channel_id=1, source_target_pairs={{0,31},{1,32},{2,33},{3,34},{4,35},{5,36},{6,37},{7,38},{8,39},{9,... | collective-permute-start | bytes 393224
  1194.7 43.5 %collective-permute-start.93 = (f32[16,2048]{1,0:T(8,128)}, f32[16,2048]{1,0:T(8,128)}, u32[]{:S(2)}, u32[]{:S(2)}) collective-permute-start(f32[16,2048]{1,0:T(8,128)} %get-tuple-element.84), channel_id=1, source_target_pairs={{0,30},{1,31},{2,32},{3,33},{4,34},{5,35},{6,36},{7,37},{8,38},{9,... | collective-permute-start | bytes 393224
  1200.9 34.1 %collective-permute-start.31 = (f32[12,2560]{1,0:T(8,128)S(1)}, f32[12,2560]{1,0:T(8,128)S(1)}, u32[]{:S(2)}, u32[]{:S(2)}) collective-permute-start(f32[12,2560]{1,0:T(8,128)S(1)} %slice.58), channel_id=1, source_target_pairs={{0,32},{1,33},{2,34},{3,35},{4,36},{5,37},{6,38},{7,39},{8,40},{9,... | collective-permute-start | bytes 368648
  1207.5 25.0 %collective-permute-start.95 = (f32[12,2048]{1,0:T(8,128)S(1)}, f32[12,2048]{1,0:T(8,128)S(1)}, u32[]{:S(2)}, u32[]{:S(2)}) collective-permute-start(f32[12,2048]{1,0:T(8,128)S(1)} %slice.60), channel_id=1, source_target_pairs={{0,32},{1,33},{2,34},{3,35},{4,36},{5,37},{6,38},{7,39},{8,40},{9,... | collective-permute-start | bytes 294920
  1211.9 28.3 %collective-permute-start.92 = (f32[16,2048]{1,0:T(8,128)}, f32[16,2048]{1,0:T(8,128)}, u32[]{:S(2)}, u32[]{:S(2)}) collective-permute-start(f32[16,2048]{1,0:T(8,128)} %get-tuple-element.84), channel_id=1, source_target_pairs={{0,29},{1,30},{2,31},{3,32},{4,33},{5,34},{6,35},{7,36},{8,37},{9,... | collective-permute-start | bytes 393224
  1236.3 20.3 %collective-permute-start.89 = (f32[16,2048]{1,0:T(8,128)}, f32[16,2048]{1,0:T(8,128)}, u32[]{:S(2)}, u32[]{:S(2)}) collective-permute-start(f32[16,2048]{1,0:T(8,128)} %get-tuple-element.84), channel_id=1, source_target_pairs={{0,26},{1,27},{2,28},{3,29},{4,30},{5,31},{6,32},{7,33},{8,34},{9,... | collective-permute-start | bytes 393224
  1238.2 20.3 %collective-permute-start.88 = (f32[16,2048]{1,0:T(8,128)}, f32[16,2048]{1,0:T(8,128)}, u32[]{:S(2)}, u32[]{:S(2)}) collective-permute-start(f32[16,2048]{1,0:T(8,128)} %get-tuple-element.84), channel_id=1, source_target_pairs={{0,25},{1,26},{2,27},{3,28},{4,29},{5,30},{6,31},{7,32},{8,33},{9,... | collective-permute-start | bytes 393224
  1240.2 21.7 %collective-permute-start.87 = (f32[16,2048]{1,0:T(8,128)}, f32[16,2048]{1,0:T(8,128)}, u32[]{:S(2)}, u32[]{:S(2)}) collective-permute-start(f32[16,2048]{1,0:T(8,128)} %get-tuple-element.84), channel_id=1, source_target_pairs={{0,24},{1,25},{2,26},{3,27},{4,28},{5,29},{6,30},{7,31},{8,32},{9,... | collective-permute-start | bytes 393224
  1242.1 21.9 %collective-permute-start.86 = (f32[16,2048]{1,0:T(8,128)}, f32[16,2048]{1,0:T(8,128)}, u32[]{:S(2)}, u32[]{:S(2)}) collective-permute-start(f32[16,2048]{1,0:T(8,128)} %get-tuple-element.84), channel_id=1, source_target_pairs={{0,23},{1,24},{2,25},{3,26},{4,27},{5,28},{6,29},{7,30},{8,31},{9,... | collective-permute-start | bytes 393224
  1256.6 25.1 %collective-permute-start.84 = (f32[16,2048]{1,0:T(8,128)}, f32[16,2048]{1,0:T(8,128)}, u32[]{:S(2)}, u32[]{:S(2)}) collective-permute-start(f32[16,2048]{1,0:T(8,128)} %get-tuple-element.84), channel_id=1, source_target_pairs={{0,21},{1,22},{2,23},{3,24},{4,25},{5,26},{6,27},{7,28},{8,29},{9,... | collective-permute-start | bytes 393224
  1258.5 25.1 %collective-permute-start.83 = (f32[16,2048]{1,0:T(8,128)}, f32[16,2048]{1,0:T(8,128)}, u32[]{:S(2)}, u32[]{:S(2)}) collective-permute-start(f32[16,2048]{1,0:T(8,128)} %get-tuple-element.84), channel_id=1, source_target_pairs={{0,20},{1,21},{2,22},{3,23},{4,24},{5,25},{6,26},{7,27},{8,28},{9,... | collective-permute-start | bytes 393224
  1261.9 27.5 %collective-permute-start.82 = (f32[16,2048]{1,0:T(8,128)}, f32[16,2048]{1,0:T(8,128)}, u32[]{:S(2)}, u32[]{:S(2)}) collective-permute-start(f32[16,2048]{1,0:T(8,128)} %get-tuple-element.84), channel_id=1, source_target_pairs={{0,19},{1,20},{2,21},{3,22},{4,23},{5,24},{6,25},{7,26},{8,27},{9,... | collective-permute-start | bytes 393224
  1264.1 28.1 %collective-permute-start.81 = (f32[16,2048]{1,0:T(8,128)}, f32[16,2048]{1,0:T(8,128)}, u32[]{:S(2)}, u32[]{:S(2)}) collective-permute-start(f32[16,2048]{1,0:T(8,128)} %get-tuple-element.84), channel_id=1, source_target_pairs={{0,18},{1,19},{2,20},{3,21},{4,22},{5,23},{6,24},{7,25},{8,26},{9,... | collective-permute-start | bytes 393224
  1267.0 28.1 %collective-permute-start.80 = (f32[16,2048]{1,0:T(8,128)}, f32[16,2048]{1,0:T(8,128)}, u32[]{:S(2)}, u32[]{:S(2)}) collective-permute-start(f32[16,2048]{1,0:T(8,128)} %get-tuple-element.84), channel_id=1, source_target_pairs={{0,17},{1,18},{2,19},{3,20},{4,21},{5,22},{6,23},{7,24},{8,25},{9,... | collective-permute-start | bytes 393224
  1281.6 21.3 %collective-permute-start.79 = (f32[16,2048]{1,0:T(8,128)}, f32[16,2048]{1,0:T(8,128)}, u32[]{:S(2)}, u32[]{:S(2)}) collective-permute-start(f32[16,2048]{1,0:T(8,128)} %get-tuple-element.84), channel_id=1, source_target_pairs={{0,16},{1,17},{2,18},{3,19},{4,20},{5,21},{6,22},{7,23},{8,24},{9,... | collective-permute-start | bytes 393224
  1283.6 21.3 %collective-permute-start.78 = (f32[16,2048]{1,0:T(8,128)}, f32[16,2048]{1,0:T(8,128)}, u32[]{:S(2)}, u32[]{:S(2)}) collective-permute-start(f32[16,2048]{1,0:T(8,128)} %get-tuple-element.84), channel_id=1, source_target_pairs={{0,15},{1,16},{2,17},{3,18},{4,19},{5,20},{6,21},{7,22},{8,23},{9,... | collective-permute-start | bytes 393224
  1295.1 21.3 %collective-permute-start.75 = (f32[16,2048]{1,0:T(8,128)}, f32[16,2048]{1,0:T(8,128)}, u32[]{:S(2)}, u32[]{:S(2)}) collective-permute-start(f32[16,2048]{1,0:T(8,128)} %get-tuple-element.84), channel_id=1, source_target_pairs={{0,12},{1,13},{2,14},{3,15},{4,16},{5,17},{6,18},{7,19},{8,20},{9,... | collective-permute-start | bytes 393224
  1308.3 24.9 %collective-permute-start.72 = (f32[16,2048]{1,0:T(8,128)}, f32[16,2048]{1,0:T(8,128)}, u32[]{:S(2)}, u32[]{:S(2)}) collective-permute-start(f32[16,2048]{1,0:T(8,128)} %get-tuple-element.84), channel_id=1, source_target_pairs={{0,9},{1,10},{2,11},{3,12},{4,13},{5,14},{6,15},{7,16},{8,17},{9,1... | collective-permute-start | bytes 393224
  1310.2 25.2 %collective-permute-start.71 = (f32[16,2048]{1,0:T(8,128)}, f32[16,2048]{1,0:T(8,128)}, u32[]{:S(2)}, u32[]{:S(2)}) collective-permute-start(f32[16,2048]{1,0:T(8,128)} %get-tuple-element.84), channel_id=1, source_target_pairs={{0,8},{1,9},{2,10},{3,11},{4,12},{5,13},{6,14},{7,15},{8,16},{9,17... | collective-permute-start | bytes 393224
  1316.4 23.0 %collective-permute-start.70 = (f32[16,2048]{1,0:T(8,128)}, f32[16,2048]{1,0:T(8,128)}, u32[]{:S(2)}, u32[]{:S(2)}) collective-permute-start(f32[16,2048]{1,0:T(8,128)} %get-tuple-element.84), channel_id=1, source_target_pairs={{0,7},{1,8},{2,9},{3,10},{4,11},{5,12},{6,13},{7,14},{8,15},{9,16}... | collective-permute-start | bytes 393224
  1318.4 24.6 %collective-permute-start.69 = (f32[16,2048]{1,0:T(8,128)}, f32[16,2048]{1,0:T(8,128)}, u32[]{:S(2)}, u32[]{:S(2)}) collective-permute-start(f32[16,2048]{1,0:T(8,128)} %get-tuple-element.84), channel_id=1, source_target_pairs={{0,6},{1,7},{2,8},{3,9},{4,10},{5,11},{6,12},{7,13},{8,14},{9,15},... | collective-permute-start | bytes 393224
  1324.1 20.9 %collective-permute-start.68 = (f32[16,2048]{1,0:T(8,128)}, f32[16,2048]{1,0:T(8,128)}, u32[]{:S(2)}, u32[]{:S(2)}) collective-permute-start(f32[16,2048]{1,0:T(8,128)} %get-tuple-element.84), channel_id=1, source_target_pairs={{0,5},{1,6},{2,7},{3,8},{4,9},{5,10},{6,11},{7,12},{8,13},{9,14},{... | collective-permute-start | bytes 393224
  1333.2 20.4 %collective-permute-start.67 = (f32[16,2048]{1,0:T(8,128)}, f32[16,2048]{1,0:T(8,128)}, u32[]{:S(2)}, u32[]{:S(2)}) collective-permute-start(f32[16,2048]{1,0:T(8,128)} %get-tuple-element.84), channel_id=1, source_target_pairs={{0,4},{1,5},{2,6},{3,7},{4,8},{5,9},{6,10},{7,11},{8,12},{9,13},{1... | collective-permute-start | bytes 393224
  1339.5 20.3 %collective-permute-start.65 = (f32[16,2048]{1,0:T(8,128)}, f32[16,2048]{1,0:T(8,128)S(1)}, u32[]{:S(2)}, u32[]{:S(2)}) collective-permute-start(f32[16,2048]{1,0:T(8,128)} %get-tuple-element.84), channel_id=1, source_target_pairs={{0,2},{1,3},{2,4},{3,5},{4,6},{5,7},{6,8},{7,9},{8,10},{9,11},{10,... | collective-permute-start | bytes 393224
  1364.2 19.9 %collective-permute-start.24 = (f32[16,2560]{1,0:T(8,128)S(1)}, f32[16,2560]{1,0:T(8,128)S(1)}, u32[]{:S(2)}, u32[]{:S(2)}) collective-permute-start(f32[16,2560]{1,0:T(8,128)S(1)} %get-tuple-element.82), channel_id=1, source_target_pairs={{0,25},{1,26},{2,27},{3,28},{4,29},{5,30},{6,31},{7,32},{8,33},{9,... | collective-permute-start | bytes 491528
  1365.6 21.5 %collective-permute-start.23 = (f32[16,2560]{1,0:T(8,128)S(1)}, f32[16,2560]{1,0:T(8,128)S(1)}, u32[]{:S(2)}, u32[]{:S(2)}) collective-permute-start(f32[16,2560]{1,0:T(8,128)S(1)} %get-tuple-element.82), channel_id=1, source_target_pairs={{0,24},{1,25},{2,26},{3,27},{4,28},{5,29},{6,30},{7,31},{8,32},{9,... | collective-permute-start | bytes 491528
  1370.0 21.7 %collective-permute-start.22 = (f32[16,2560]{1,0:T(8,128)S(1)}, f32[16,2560]{1,0:T(8,128)S(1)}, u32[]{:S(2)}, u32[]{:S(2)}) collective-permute-start(f32[16,2560]{1,0:T(8,128)S(1)} %get-tuple-element.82), channel_id=1, source_target_pairs={{0,23},{1,24},{2,25},{3,26},{4,27},{5,28},{6,29},{7,30},{8,31},{9,... | collective-permute-start | bytes 491528
  1373.2 23.1 %collective-permute-start.21 = (f32[16,2560]{1,0:T(8,128)S(1)}, f32[16,2560]{1,0:T(8,128)S(1)}, u32[]{:S(2)}, u32[]{:S(2)}) collective-permute-start(f32[16,2560]{1,0:T(8,128)S(1)} %get-tuple-element.82), channel_id=1, source_target_pairs={{0,22},{1,23},{2,24},{3,25},{4,26},{5,27},{6,28},{7,29},{8,30},{9,... | collective-permute-start | bytes 491528
  1379.4 24.9 %collective-permute-start.20 = (f32[16,2560]{1,0:T(8,128)S(1)}, f32[16,2560]{1,0:T(8,128)S(1)}, u32[]{:S(2)}, u32[]{:S(2)}) collective-permute-start(f32[16,2560]{1,0:T(8,128)S(1)} %get-tuple-element.82), channel_id=1, source_target_pairs={{0,21},{1,22},{2,23},{3,24},{4,25},{5,26},{6,27},{7,28},{8,29},{9,... | collective-permute-start | bytes 491528
  1384.1 26.7 %collective-permute-start.19 = (f32[16,2560]{1,0:T(8,128)S(1)}, f32[16,2560]{1,0:T(8,128)S(1)}, u32[]{:S(2)}, u32[]{:S(2)}) collective-permute-start(f32[16,2560]{1,0:T(8,128)S(1)} %get-tuple-element.82), channel_id=1, source_target_pairs={{0,20},{1,21},{2,22},{3,23},{4,24},{5,25},{6,26},{7,27},{8,28},{9,... | collective-permute-start | bytes 491528
  1387.2 29.6 %collective-permute-start.18 = (f32[16,2560]{1,0:T(8,128)S(1)}, f32[16,2560]{1,0:T(8,128)S(1)}, u32[]{:S(2)}, u32[]{:S(2)}) collective-permute-start(f32[16,2560]{1,0:T(8,128)S(1)} %get-tuple-element.82), channel_id=1, source_target_pairs={{0,19},{1,20},{2,21},{3,22},{4,23},{5,24},{6,25},{7,26},{8,27},{9,... | collective-permute-start | bytes 491528
  1391.7 27.4 %collective-permute-start.17 = (f32[16,2560]{1,0:T(8,128)S(1)}, f32[16,2560]{1,0:T(8,128)S(1)}, u32[]{:S(2)}, u32[]{:S(2)}) collective-permute-start(f32[16,2560]{1,0:T(8,128)S(1)} %get-tuple-element.82), channel_id=1, source_target_pairs={{0,18},{1,19},{2,20},{3,21},{4,22},{5,23},{6,24},{7,25},{8,26},{9,... | collective-permute-start | bytes 491528
  1396.3 31.2 %collective-permute-start.16 = (f32[16,2560]{1,0:T(8,128)S(1)}, f32[16,2560]{1,0:T(8,128)S(1)}, u32[]{:S(2)}, u32[]{:S(2)}) collective-permute-start(f32[16,2560]{1,0:T(8,128)S(1)} %get-tuple-element.82), channel_id=1, source_target_pairs={{0,17},{1,18},{2,19},{3,20},{4,21},{5,22},{6,23},{7,24},{8,25},{9,... | collective-permute-start | bytes 491528
  1404.4 25.4 %collective-permute-start.15 = (f32[16,2560]{1,0:T(8,128)S(1)}, f32[16,2560]{1,0:T(8,128)S(1)}, u32[]{:S(2)}, u32[]{:S(2)}) collective-permute-start(f32[16,2560]{1,0:T(8,128)S(1)} %get-tuple-element.82), channel_id=1, source_target_pairs={{0,16},{1,17},{2,18},{3,19},{4,20},{5,21},{6,22},{7,23},{8,24},{9,... | collective-permute-start | bytes 491528
  1410.8 125.7 %collective-permute-start.14 = (f32[16,2560]{1,0:T(8,128)S(1)}, f32[16,2560]{1,0:T(8,128)}, u32[]{:S(2)}, u32[]{:S(2)}) collective-permute-start(f32[16,2560]{1,0:T(8,128)S(1)} %get-tuple-element.82), channel_id=1, source_target_pairs={{0,15},{1,16},{2,17},{3,18},{4,19},{5,20},{6,21},{7,22},{8,23},{9,... | collective-permute-start | bytes 491528
  1416.7 123.1 %collective-permute-start.13 = (f32[16,2560]{1,0:T(8,128)S(1)}, f32[16,2560]{1,0:T(8,128)}, u32[]{:S(2)}, u32[]{:S(2)}) collective-permute-start(f32[16,2560]{1,0:T(8,128)S(1)} %get-tuple-element.82), channel_id=1, source_target_pairs={{0,14},{1,15},{2,16},{3,17},{4,18},{5,19},{6,20},{7,21},{8,22},{9,... | collective-permute-start | bytes 491528
  1419.0 122.7 %collective-permute-start.12 = (f32[16,2560]{1,0:T(8,128)S(1)}, f32[16,2560]{1,0:T(8,128)}, u32[]{:S(2)}, u32[]{:S(2)}) collective-permute-start(f32[16,2560]{1,0:T(8,128)S(1)} %get-tuple-element.82), channel_id=1, source_target_pairs={{0,13},{1,14},{2,15},{3,16},{4,17},{5,18},{6,19},{7,20},{8,21},{9,... | collective-permute-start | bytes 491528
  1427.5 117.6 %collective-permute-start.11 = (f32[16,2560]{1,0:T(8,128)S(1)}, f32[16,2560]{1,0:T(8,128)}, u32[]{:S(2)}, u32[]{:S(2)}) collective-permute-start(f32[16,2560]{1,0:T(8,128)S(1)} %get-tuple-element.82), channel_id=1, source_target_pairs={{0,12},{1,13},{2,14},{3,15},{4,16},{5,17},{6,18},{7,19},{8,20},{9,... | collective-permute-start | bytes 491528
  1429.7 120.3 %collective-permute-start.10 = (f32[16,2560]{1,0:T(8,128)S(1)}, f32[16,2560]{1,0:T(8,128)}, u32[]{:S(2)}, u32[]{:S(2)}) collective-permute-start(f32[16,2560]{1,0:T(8,128)S(1)} %get-tuple-element.82), channel_id=1, source_target_pairs={{0,11},{1,12},{2,13},{3,14},{4,15},{5,16},{6,17},{7,18},{8,19},{9,... | collective-permute-start | bytes 491528
  1536.6 72.9 %collective-permute-start.9 = (f32[16,2560]{1,0:T(8,128)S(1)}, f32[16,2560]{1,0:T(8,128)}, u32[]{:S(2)}, u32[]{:S(2)}) collective-permute-start(f32[16,2560]{1,0:T(8,128)S(1)} %get-tuple-element.82), channel_id=1, source_target_pairs={{0,10},{1,11},{2,12},{3,13},{4,14},{5,15},{6,16},{7,17},{8,18},{9,... | collective-permute-start | bytes 491528
  1539.8 71.2 %collective-permute-start.8 = (f32[16,2560]{1,0:T(8,128)S(1)}, f32[16,2560]{1,0:T(8,128)}, u32[]{:S(2)}, u32[]{:S(2)}) collective-permute-start(f32[16,2560]{1,0:T(8,128)S(1)} %get-tuple-element.82), channel_id=1, source_target_pairs={{0,9},{1,10},{2,11},{3,12},{4,13},{5,14},{6,15},{7,16},{8,17},{9,1... | collective-permute-start | bytes 491528
  1541.8 72.9 %collective-permute-start.7 = (f32[16,2560]{1,0:T(8,128)S(1)}, f32[16,2560]{1,0:T(8,128)}, u32[]{:S(2)}, u32[]{:S(2)}) collective-permute-start(f32[16,2560]{1,0:T(8,128)S(1)} %get-tuple-element.82), channel_id=1, source_target_pairs={{0,8},{1,9},{2,10},{3,11},{4,12},{5,13},{6,14},{7,15},{8,16},{9,17... | collective-permute-start | bytes 491528
  1545.1 73.9 %collective-permute-start.6 = (f32[16,2560]{1,0:T(8,128)S(1)}, f32[16,2560]{1,0:T(8,128)}, u32[]{:S(2)}, u32[]{:S(2)}) collective-permute-start(f32[16,2560]{1,0:T(8,128)S(1)} %get-tuple-element.82), channel_id=1, source_target_pairs={{0,7},{1,8},{2,9},{3,10},{4,11},{5,12},{6,13},{7,14},{8,15},{9,16}... | collective-permute-start | bytes 491528
  1550.0 73.3 %collective-permute-start.5 = (f32[16,2560]{1,0:T(8,128)S(1)}, f32[16,2560]{1,0:T(8,128)}, u32[]{:S(2)}, u32[]{:S(2)}) collective-permute-start(f32[16,2560]{1,0:T(8,128)S(1)} %get-tuple-element.82), channel_id=1, source_target_pairs={{0,6},{1,7},{2,8},{3,9},{4,10},{5,11},{6,12},{7,13},{8,14},{9,15},... | collective-permute-start | bytes 491528
  (178 other events, 6218.8 us)
Sparse Core Ops, SparseCore 0:
  11.1 69.5 all-gather.17
  83.6 67.6 all-gather.19
  154.5 69.6 all-gather.15
  227.1 91.9 all-gather.11
  322.1 72.7 all-gather.13
  397.8 65.1 all-gather.21
  467.8 157.2 all-reduce.16
  631.1 272.3 reduce-scatter.12
  909.4 433.0 reduce-scatter.10
where the time goes:
time: 1720 us; the launch traced here: 1690 us
  blocking collectives  607 us (35%)
  local copies, waits for them, and re-layouts  466 us (27%)
  starting transfers between devices  367 us (21%)
  matrix products  134 us (8%)
  waiting for transfers between devices  82.6 us (5%)
  other arithmetic  21 us (1%)
  between operations  17.2 us (1%)
    unnamed x3, blocking collectives  574 us
    unnamed x97, starting transfers between devices  366 us
    scatter x2, local copies, waits for them, and re-layouts, local(): jnp.zeros((EXPERTS, CAP, D), jnp.bfloat16).at[flat_ids, slot_index]  211 us
    unnamed x298, local copies, waits for them, and re-layouts  198 us
    all_gather x1, waiting for transfers between devices, local(): lax.all_gather(w_qkv, 'fsdp', axis=0, tiled=True)  62.1 us
  transfers between devices with their start and end apart: 105, of which 5 were waited for; matrix products, arithmetic and copies ran while one was open for 62% of the time, Pallas kernels for 0%

commit v1 on v0

v1 whole, which is shorter than its diff:
```python
import jax
import jax.numpy as jnp
from jax import lax
from jax.experimental import pallas as pl
from jax.experimental.pallas import tpu as pltpu
from jax.sharding import PartitionSpec as P

D = 1536
HD = 128
SH = 1024
EXPERTS = 8
TOP = 6
ROWS = 12
SEQ = 128
W_ATT = 1152
W_SHARED = 768
W_ALL = W_ATT + W_SHARED
WIDE = D + 128
epsilon = 1e-05
MESH = pl.DeviceIdType.MESH
F32 = jnp.float32
BF16 = jnp.bfloat16
STRIDE = {"x": (32, 4), "z": (8, 4), "y": (2, 4), "c": (1, 2)}
FAR_FIRST = (2, 1, 3)
NEAR_FIRST = (1, 3, 2)


def place(me, axis):
    stride, size = STRIDE[axis]
    return lax.rem(lax.div(me, stride), size)


def peer(me, axis, step):
    stride, size = STRIDE[axis]
    here = place(me, axis)
    return me + (lax.rem(here + step, size) - here) * stride


class Links:
    def __init__(self, send_sem, recv_sem):
        self.me = lax.axis_index("fsdp")
        self.send_sem, self.recv_sem = send_sem, recv_sem
        self.count = 0
        self.x, self.y, self.z, self.c = (place(self.me, axis) for axis in "xyzc")

    def take(self, number):
        first = self.count
        self.count += number
        return first

    def copy(self, src, dst, axis, step, sem):
        return pltpu.make_async_remote_copy(
            src_ref=src,
            dst_ref=dst,
            send_sem=self.send_sem.at[sem],
            recv_sem=self.recv_sem.at[sem],
            device_id=(peer(self.me, axis, step),),
            device_id_type=MESH,
        )

    def send(self, src, dst, axis, step):
        copy = self.copy(src, dst, axis, step, self.take(1))
        copy.start()
        return copy

    def local(self, src, dst):
        copy = pltpu.make_async_copy(src, dst, self.send_sem.at[self.take(1)])
        copy.start()
        return copy

    def greet(self, axes):
        barrier = pltpu.get_barrier_semaphore()
        total = 0
        for axis in axes:
            for step in range(1, STRIDE[axis][1]):
                pl.semaphore_signal(
                    barrier, inc=1, device_id=(peer(self.me, axis, step),), device_id_type=MESH
                )
                total += 1
        return lambda: pl.semaphore_wait(barrier, total)


def finish(copies):
    for copy in copies:
        copy.wait()


def received(copies):
    for copy in copies:
        copy.wait_recv()


def sent(copies):
    for copy in copies:
        copy.wait_send()


def dot(a, b):
    return jnp.dot(a, b, preferred_element_type=F32)


def dot_nt(a, b):
    return lax.dot_general(a, b, (((1,), (1,)), ((), ())), preferred_element_type=F32)


def dot_tn(a, b):
    return lax.dot_general(a, b, (((0,), (0,)), ((), ())), preferred_element_type=F32)


def pick_matrix(shape, source):
    row = lax.broadcasted_iota(jnp.int32, shape, 0)
    col = lax.broadcasted_iota(jnp.int32, shape, 1)
    return (col == source(row)).astype(BF16)


def moved(pick, rows):
    return dot(pick, rows).astype(BF16)


def gather_first(links, own, part, here, cut):
    first = []
    for axis, half in (("y", cut[0]), ("z", cut[1])):
        for step in FAR_FIRST:
            first.append(links.send(own.at[half], part(here, half), axis, step))
    return first


def gather_second(links, first, part, cut):
    received(first[:3])
    second = []
    for step in FAR_FIRST:
        piece = part(pl.ds(links.z * 4, 4), cut[0])
        second.append(links.send(piece, piece, "z", step))
    received(first[3:])
    for step in FAR_FIRST:
        for z in range(4):
            piece = part(z * 4 + links.y, cut[1])
            second.append(links.send(piece, piece, "y", step))
    return second


def scatter_first(links, part, got, cut):
    first = []
    for step in FAR_FIRST:
        to = lax.rem(links.z + step, 4) * 4
        first.append(links.send(part(pl.ds(to, 4), cut[0]), got[0].at[step - 1], "z", step))
    for step in FAR_FIRST:
        to = lax.rem(links.y + step, 4)
        for z in range(4):
            first.append(
                links.send(part(z * 4 + to, cut[1]), got[1].at[step - 1, z], "y", step)
            )
    return first


def scatter_second(links, first, part, got, last, cut):
    second = []
    for half, axis in ((0, "y"), (1, "z")):
        received(first[3:] if half else first[:3])
        here = links.z if half else links.y

        @pl.loop(0, 4)
        def _(k):
            slot = k * 4 + links.y if half else links.z * 4 + k
            total = part(slot, cut[half])[...].astype(F32)
            for step in range(3):
                total = total + got[half][step, k].astype(F32)
            got[half][0, k] = total.astype(BF16)

        for step in FAR_FIRST:
            second.append(
                links.send(
                    got[half].at[0, lax.rem(here + step, 4)], last[half].at[step - 1], axis, step
                )
            )
    return second


def scatter_end(links, got, last, half):
    here = links.z if half else links.y
    total = got[half][0, here].astype(F32)
    for step in range(3):
        total = total + last[half][step].astype(F32)
    return total


INS = (
    "tokens",
    "ids",
    "gain_one",
    "w_qkv",
    "w_out",
    "w_router",
    "gain_two",
    "w_sin",
    "w_sout",
    "e_in",
    "e_out",
    "out_grad",
)
OUTS = {
    "block_out": ((SEQ, D), BF16),
    "tokens_grad": ((SEQ, D), F32),
    "g_gain": ((ROWS, 128), F32),
    "g_qkv": ((ROWS, 2560), F32),
    "g_out": ((ROWS, D), F32),
    "g_misc": ((ROWS, 128), F32),
    "g_sin": ((ROWS, 2 * SH), F32),
    "g_sout": ((ROWS, SH), F32),
    "g_ein": ((96, 1024), F32),
    "g_eout": ((96, 512), F32),
}
SCRATCH = {
    "pack": ((4, 16, W_ALL), BF16),
    "arrived": ((4, 16, W_ALL), BF16),
    "dense": ((16, 2, 48, W_ATT), BF16),
    "shared": ((16, 2, 48, W_SHARED), BF16),
    "got": ((16, 96, D), BF16),
    "full": ((8, 2, 96, D), BF16),
    "nat": ((D, D), BF16),
    "normed": ((4, SEQ, D), BF16),
    "qkv": ((4, SEQ, 640), BF16),
    "mix": ((4, SEQ, 384), BF16),
    "send_y": ((4, 2, SEQ, D), BF16),
    "send_x": ((4, 2, SEQ, WIDE), BF16),
    "pair_y": ((4, SEQ, D), BF16),
    "pair_x": ((4, SEQ, WIDE), BF16),
    "got_y": ((3, SEQ, D), BF16),
    "got_x": ((3, SEQ, WIDE), BF16),
    "hidden": ((SEQ, D), F32),
    "probs": ((SEQ, 128), F32),
    "rows": ((4, 2, SEQ, WIDE), BF16),
    "cot": ((4, 2, SEQ, D), BF16),
    "gated": ((4, 256, 640), BF16),
    "joint": ((4, 256, 1280), BF16),
    "low": ((4, SEQ, D), BF16),
    "dsh": ((16, 2, 48, 384), BF16),
    "dgot": ((16, 48, W_ATT), BF16),
    "back": ((48, W_ALL), BF16),
    "e_got0": ((3, 4, 48, D), BF16),
    "e_got1": ((3, 4, 48, D), BF16),
    "e_last0": ((3, 48, D), BF16),
    "e_last1": ((3, 48, D), BF16),
    "d_got0": ((3, 4, 48, 640), BF16),
    "d_got1": ((3, 4, 48, 512), BF16),
    "d_last0": ((3, 48, 640), BF16),
    "d_last1": ((3, 48, 512), BF16),
    "s_got0": ((3, 4, 48, 384), BF16),
    "s_got1": ((3, 4, 48, 384), BF16),
    "s_last0": ((3, 48, 384), BF16),
    "s_last1": ((3, 48, 384), BF16),
}
SEMS = 256


class Bag:
    pass


def near(i):
    return jnp.where(i == 2, 3, jnp.where(i == 3, 2, i))


def far(i):
    return jnp.where(i == 0, 2, jnp.where(i == 3, 0, jnp.where(i == 2, 3, 1)))


def causal_probs(q, k):
    scores = dot_nt(q, k) * HD**-0.5
    row = lax.broadcasted_iota(jnp.int32, (SEQ, SEQ), 0)
    col = lax.broadcasted_iota(jnp.int32, (SEQ, SEQ), 1)
    scores = jnp.where(col <= row, scores, -1e30)
    exponent = jnp.exp(scores - jnp.max(scores, axis=1, keepdims=True))
    return exponent / jnp.sum(exponent, axis=1, keepdims=True)


def kernel(*refs):
    b = Bag()
    names = [*INS, *OUTS, *SCRATCH]
    for name, ref in zip(names, refs):
        setattr(b, name, ref)
    links = Links(*refs[len(names) :])
    x, y, z, c = links.x, links.y, links.z, links.c
    other = 1 - c
    here = z * 4 + y
    mine = 2 * x + c
    every = pl.ds(0, 48)
    e_cut = ((pl.ds(0, 48),), (pl.ds(48, 48),))
    d_cut = ((every, pl.ds(0, 640)), (every, pl.ds(640, 512)))
    s_cut = ((every, pl.ds(0, 384)), (every, pl.ds(384, 384)))
    d_part = lambda slots, half: b.dense.at[(slots, c, *half)]
    s_part = lambda slots, half: b.shared.at[(slots, c, *half)]
    e_part = lambda slots, half: b.got.at[(slots, *half)]

    greeted = links.greet("xyzc")
    b.got[here, :, 0:1024] = b.e_in[...]
    b.got[here, :, 1024:1536] = b.e_out[...]
    b.pack[...] = jnp.zeros_like(b.pack)
    gain_one = b.gain_one[...].astype(F32)
    for k in range(4):
        for start, width, at in ((k * 384, 384, 0), (D + k * 128, 128, 384), (2048 + k * 128, 128, 512)):
            b.pack[k, 0:ROWS, at : at + width] = (
                b.w_qkv[:, start : start + width].astype(F32) * gain_one
            ).astype(BF16)
        b.pack[k, 0:ROWS, 640:1024] = b.w_out[:, k * 384 : k * 384 + 384]
        b.pack[k, 0:ROWS, 1024:1032] = b.w_router[...]
        b.pack[k, 0:ROWS, 1032:1033] = b.gain_two[...]
        for core in range(2):
            at, unit = W_ATT + 384 * core, (2 * k + core) * 128
            b.pack[k, 0:ROWS, at : at + 128] = b.w_sin[:, unit : unit + 128]
            b.pack[k, 0:ROWS, at + 128 : at + 256] = b.w_sin[:, SH + unit : SH + unit + 128]
            b.pack[k, 0:ROWS, at + 256 : at + 384] = b.w_sout[:, unit : unit + 128]
    greeted()
    exchange = [
        links.send(b.pack.at[lax.rem(x + step, 4)], b.arrived.at[x], "x", step)
        for step in FAR_FIRST
    ]
    e_first = gather_first(links, b.got.at[here], e_part, here, e_cut)
    inputs = b.tokens[...].astype(F32)
    inverse_one = lax.rsqrt(jnp.mean(inputs * inputs, axis=1, keepdims=True) + epsilon)
    b.normed[x] = (inputs * inverse_one).astype(BF16)
    b.cot[x, c] = b.out_grad[...]
    normed_sends = [
        links.send(b.normed.at[x], b.normed.at[x], "x", step) for step in FAR_FIRST
    ]
    cot_pair = links.send(b.cot.at[x, c], b.cot.at[x, c], "c", 1)
    b.arrived[x] = b.pack[x]
    finish(exchange)
    pick = pick_matrix((48, 64), lambda row: row // ROWS * 16 + row % ROWS)
    for col in range(0, W_ALL, 384):
        block = moved(pick, b.arrived[:, :, col : col + 384].reshape(64, 384))
        if col < W_ATT:
            b.dense[here, c, :, col : col + 384] = block
        else:
            b.shared[here, c, :, col - W_ATT : col - W_ATT + 384] = block

    d_first = gather_first(links, b.dense.at[here, c], d_part, here, d_cut)
    d_second = gather_second(links, d_first, d_part, d_cut)
    s_first = gather_first(links, b.shared.at[here, c], s_part, here, s_cut)
    received(d_second)
    sent(d_first + d_second)
    d_pair = links.send(b.dense.at[:, c], b.dense.at[:, c], "c", 1)
    e_second = gather_second(links, e_first, e_part, e_cut)
    s_second = gather_second(links, s_first, s_part, s_cut)
    received(normed_sends)
    cot_base = links.take(4)
    cot_copy = lambda step: links.copy(
        b.cot.at[x, c], b.cot.at[x, c], "x", step, cot_base + step
    )
    for step in NEAR_FIRST:
        cot_copy(step).start()
    d_pair.wait()

    order = pick_matrix(
        (192, 192), lambda row: row % 48 // ROWS * 48 + row // 48 * ROWS + row % ROWS
    )

    def to_rows(j, source, start, at):
        piece = source[pl.ds(2 * j, 2), :, :, start].reshape(192, 384)
        piece = moved(order, piece)
        for k in range(4):
            row = pl.multiple_of(k * 384 + j * 48, 16)
            b.nat[pl.ds(row, 48), at : at + 384] = piece[k * 48 : k * 48 + 48]

    def to_blocks(j, target, start, at):
        pieces = [
            b.nat[pl.ds(pl.multiple_of(k * 384 + j * 48, 16), 48), at : at + 384] for k in range(4)
        ]
        piece = moved(order, jnp.concatenate(pieces, axis=0))
        target[pl.ds(2 * j, 2), :, :, start] = piece.reshape(2, 2, 48, 384)

    @pl.loop(0, 8)
    def _(j):
        for part in range(3):
            to_rows(j, b.dense, pl.ds(part * 384, 384), part * 384)

    for at, width in ((0, 256), (256, 256), (512, 128)):
        result = dot(b.normed[...].reshape(512, D), b.nat[:, at : at + width])
        b.qkv[:, :, at : at + width] = result.astype(BF16).reshape(4, SEQ, width)
    mix_base = links.take(4)

    def mix_copy(step):
        return links.copy(
            b.send_y.at[lax.rem(x + step, 4), 0], b.got_y.at[step - 1], "x", step, mix_base + step
        )

    @pl.loop(0, 4)
    def _(i):
        step = far(i)
        s = lax.rem(x + step, 4)
        key, value = b.qkv[s, :, 384:512], b.qkv[s, :, 512:640]
        for h in range(3):
            head = slice(h * HD, (h + 1) * HD)
            probs = causal_probs(b.qkv[s, :, head], key)
            b.mix[s, :, head] = dot(probs.astype(BF16), value).astype(BF16)
        for n in range(2):
            rows = slice(n * 768, (n + 1) * 768)
            b.send_y[s, 0, :, rows] = dot_nt(b.mix[s], b.nat[rows, 640:1024]).astype(BF16)

        @pl.when(i < 3)
        def _():
            mix_copy(step).start()

    received(e_second)
    received(s_second)
    sent(e_first + e_second + s_first + s_second)
    half = pl.ds(pl.multiple_of(other * 384, 128), 384)
    s_pair = links.send(b.shared.at[:, c, :, half], b.shared.at[:, c, :, half], "c", 1)
    e_pair = links.send(b.got.at[pl.ds(8 * other, 8)], b.full.at[:, c], "c", 1)
    e_own = links.local(b.got.at[pl.ds(8 * c, 8)], b.full.at[:, c])

    for step in FAR_FIRST:
        mix_copy(step).wait()
    hidden = b.tokens[...].astype(F32) + b.send_y[x, 0].astype(F32)
    for step in range(3):
        hidden = hidden + b.got_y[step].astype(F32)
    b.hidden[...] = hidden
    inverse_two = lax.rsqrt(jnp.mean(hidden * hidden, axis=1, keepdims=True) + epsilon)
    lane8 = lax.broadcasted_iota(jnp.int32, (8, 128), 1)
    gain_two = dot_nt((lane8 == 8).astype(BF16), b.nat[:, 1024:1152])[0:1]
    moe_in = (hidden * inverse_two * gain_two).astype(BF16)
    b.rows[x, c, :, 0:D] = moe_in
    lane = lax.broadcasted_iota(jnp.int32, (SEQ, 128), 1)
    logits = jnp.where(lane < EXPERTS, dot(moe_in, b.nat[:, 1024:1152]), -1e30)
    exponent = jnp.exp(logits - jnp.max(logits, axis=1, keepdims=True))
    router_probs = exponent / jnp.sum(exponent, axis=1, keepdims=True)
    b.probs[...] = router_probs
    chosen = jnp.zeros((SEQ, 128), F32)
    for k in range(TOP):
        chosen = chosen + (b.ids[:, k : k + 1] == lane).astype(F32)
    gates = chosen * router_probs
    high = gates.astype(BF16).astype(F32)
    b.rows[x, c, :, D:WIDE] = (high + pltpu.roll(gates - high, 8, 1)).astype(BF16)
    rows_base = links.take(4)
    rows_copy = lambda step: links.copy(
        b.rows.at[x, c], b.rows.at[x, c], "x", step, rows_base + step
    )
    for step in NEAR_FIRST:
        rows_copy(step).start()
    pair_rows = links.take(4)
    pair_cot = links.take(4)
    forward_rows = lambda s, d: links.copy(
        b.rows.at[s, c], b.rows.at[s, c], "c", 1, pair_rows + d
    )
    forward_cot = lambda s, d: links.copy(b.cot.at[s, c], b.cot.at[s, c], "c", 1, pair_cot + d)
    forward_rows(x, 0).start()

    s_pair.wait()
    e_pair.wait()
    e_own.wait()

    @pl.loop(0, 8)
    def _(j):
        to_rows(j, b.shared, pl.ds(pl.multiple_of(c * 384, 128), 384), W_ATT)

    back_pair = links.take(4)
    back_base = links.take(4)
    sum_pair = links.take(4)
    sum_base = links.take(4)
    back_forward = lambda s, d: links.copy(
        b.send_x.at[s, other], b.pair_x.at[s], "c", 1, back_pair + d
    )
    sum_forward = lambda s, d: links.copy(
        b.send_y.at[s, other], b.pair_y.at[s], "c", 1, sum_pair + d
    )
    back_copy = lambda step: links.copy(
        b.send_x.at[lax.rem(x + step, 4), c], b.got_x.at[step - 1], "x", step, back_base + step
    )
    sum_copy = lambda step: links.copy(
        b.send_y.at[lax.rem(x + step, 4), c], b.got_y.at[step - 1], "x", step, sum_base + step
    )
    cot_pair.wait()

    @pl.loop(0, 4)
    def _(i):
        d = near(i)
        s = lax.rem(x + d, 4)

        @pl.when(i > 0)
        def _():
            rows_copy(4 - d).wait_recv()
            forward_rows(s, d).start()
            cot_copy(4 - d).wait_recv()
            forward_cot(s, d).start()
            forward_cot(s, d).wait_recv()

        forward_rows(s, d).wait_recv()
        tokens = b.rows[s, :, :, 0:D].reshape(256, D)
        grads = b.cot[s].reshape(256, D)
        lanes = lax.broadcasted_iota(jnp.int32, (256, 128), 1)
        gate = b.rows[s, :, :, D:WIDE].reshape(256, 128).astype(F32)
        gate = jnp.where((lanes == mine) | (lanes == mine + 8), gate, 0.0)
        gate = jnp.sum(gate, axis=1, keepdims=True)
        gate_grad = jnp.zeros((256, 1), F32)
        for part in range(3):
            if part < 2:
                at, width = part * 256, 256
                g = dot(tokens, b.full[:, :, :, at : at + 256].reshape(D, 256))
                u = dot(tokens, b.full[:, :, :, at + 512 : at + 768].reshape(D, 256))
                a = dot(grads, b.full[:, :, :, at + 1024 : at + 1280].reshape(D, 256))
                first, second, scale = at, at + 512, gate
            else:
                at, width = 512, 128
                gu = dot(tokens, b.nat[:, 1152:1408])
                g, u = gu[:, 0:128], gu[:, 128:256]
                a = dot(grads, b.nat[:, 1408:1536])
                first, second, scale = 1024, 1152, None
            g = g.astype(BF16).astype(F32)
            u = u.astype(BF16).astype(F32)
            sg = jax.nn.sigmoid(g)
            act = (g * sg * u).astype(BF16)
            if scale is not None:
                gate_grad = gate_grad + jnp.sum(act.astype(F32) * a, axis=1, keepdims=True)
                act = (act.astype(F32) * scale).astype(BF16)
                a = a * scale
            b.gated[s, :, at : at + width] = act
            b.joint[s, :, first : first + width] = (
                a * u * (sg * (1.0 + g * (1.0 - sg)))
            ).astype(BF16)
            b.joint[s, :, second : second + width] = (a * g * sg).astype(BF16)
        gate_high = gate_grad.astype(BF16).astype(F32)
        spread = jnp.where(lanes == mine, gate_high, 0.0)
        spread = spread + jnp.where(lanes == mine + 8, gate_grad - gate_high, 0.0)
        b.send_x[s, :, :, D:WIDE] = spread.astype(BF16).reshape(2, SEQ, 128)
        for n in range(2):
            rows = slice(n * 768, (n + 1) * 768)
            result = dot_nt(
                b.joint[s, :, 0:1024], b.full[4 * n : 4 * n + 4, :, :, 0:1024].reshape(768, 1024)
            ) + dot_nt(b.joint[s, :, 1024:1280], b.nat[rows, 1152:1408])
            b.send_x[s, :, :, rows] = result.astype(BF16).reshape(2, SEQ, 768)
        back_forward(s, d).start()

        for n in range(2):
            rows = slice(n * 768, (n + 1) * 768)
            result = dot_nt(
                b.gated[s, :, 0:512], b.full[4 * n : 4 * n + 4, :, :, 1024:1536].reshape(768, 512)
            ) + dot_nt(b.gated[s, :, 512:640], b.nat[rows, 1408:1536])
            b.send_y[s, :, :, rows] = result.astype(BF16).reshape(2, SEQ, 768)
        sum_forward(s, d).start()
        back_forward(s, d).wait_recv()
        b.send_x[s, c] = (b.send_x[s, c].astype(F32) + b.pair_x[s].astype(F32)).astype(BF16)

        @pl.when(i > 0)
        def _():
            back_copy(d).start()

    for n in range(4):
        cols = slice(n * 384, (n + 1) * 384)
        tokens = b.rows[:, :, :, cols].reshape(1024, 384)
        for at in (0, 512):
            result = dot_tn(tokens, b.joint[:, :, at : at + 512].reshape(1024, 512))
            b.full[2 * n : 2 * n + 2, :, :, at : at + 512] = result.astype(BF16).reshape(
                2, 2, 96, 512
            )
        result = dot_tn(tokens, b.joint[:, :, 1024:1280].reshape(1024, 256))
        b.nat[cols, 1152:1408] = result.astype(BF16)
        grads = b.cot[:, :, :, cols].reshape(1024, 384)
        result = dot_tn(grads, b.gated[:, :, 0:512].reshape(1024, 512))
        b.full[2 * n : 2 * n + 2, :, :, 1024:1536] = result.astype(BF16).reshape(2, 2, 96, 512)
        result = dot_tn(grads, b.gated[:, :, 512:640].reshape(1024, 128))
        b.nat[cols, 1408:1536] = result.astype(BF16)
    e_give = links.send(b.full.at[:, other], b.got.at[pl.ds(8 * c, 8)], "c", 1)
    e_keep = links.local(b.full.at[:, c], b.got.at[pl.ds(8 * c, 8)])

    @pl.loop(0, 8)
    def _(j):
        to_blocks(j, b.dsh, pl.ds(0, 384), W_ATT)

    half = pl.ds(pl.multiple_of(c * 384, 128), 384)
    s_give = links.send(b.dsh.at[:, other], b.shared.at[:, 0, :, half], "c", 1)
    s_keep = links.local(b.dsh.at[:, c], b.shared.at[:, 0, :, half])
    s_sum = lambda slots, half: b.shared.at[(slots, 0, *half)]
    e_give.wait()
    e_keep.wait()
    e_first = scatter_first(links, e_part, (b.e_got0, b.e_got1), e_cut)
    s_give.wait()
    s_keep.wait()
    s_first = scatter_first(links, s_sum, (b.s_got0, b.s_got1), s_cut)

    for step in NEAR_FIRST:
        back_copy(step).wait()
    moe_back = b.send_x[x, c].astype(F32)
    for step in range(3):
        moe_back = moe_back + b.got_x[step].astype(F32)
    raw = moe_back[:, D:WIDE]
    router_probs = b.probs[...]
    chosen = jnp.zeros((SEQ, 128), F32)
    for k in range(TOP):
        chosen = chosen + (b.ids[:, k : k + 1] == lane).astype(F32)
    prob_grad = chosen * (raw + pltpu.roll(raw, 120, 1))
    logit_grad = router_probs * (
        prob_grad - jnp.sum(router_probs * prob_grad, axis=1, keepdims=True)
    )
    logit_grad = logit_grad.astype(BF16)
    gain_two = dot_nt((lane8 == 8).astype(BF16), b.nat[:, 1024:1152])[0:1]
    moe_in_grad = moe_back[:, 0:D] + dot_nt(logit_grad, b.nat[:, 1024:1152])
    hidden = b.hidden[...]
    inverse_two = lax.rsqrt(jnp.mean(hidden * hidden, axis=1, keepdims=True) + epsilon)
    misc_grad = dot_tn(b.rows[x, c, :, 0:D], logit_grad) + dot_tn(
        (moe_in_grad * hidden * inverse_two).astype(BF16), (lane == 8).astype(BF16)
    )
    b.nat[:, 1024:1152] = misc_grad.astype(BF16)
    scaled = gain_two * moe_in_grad
    hidden_grad = (
        b.out_grad[...].astype(F32)
        + inverse_two * scaled
        - hidden
        * (inverse_two * inverse_two * inverse_two)
        * jnp.mean(scaled * hidden, axis=1, keepdims=True)
    )
    b.tokens_grad[...] = hidden_grad
    b.low[x] = hidden_grad.astype(BF16)
    low_base = links.take(4)
    low_copy = lambda step: links.copy(b.low.at[x], b.low.at[x], "x", step, low_base + step)
    for step in NEAR_FIRST:
        low_copy(step).start()

    norm_base = links.take(4)
    norm_copy = lambda step: links.copy(
        b.send_x.at[lax.rem(x + step, 4), 0, :, pl.ds(0, D)],
        b.got_x.at[step - 1, :, pl.ds(0, D)],
        "x",
        step,
        norm_base + step,
    )
    for d in range(4):
        back_forward(lax.rem(x + d, 4), d).wait_send()

    @pl.loop(0, 4)
    def _(i):
        d = near(i)
        s = lax.rem(x + d, 4)

        @pl.when(i > 0)
        def _():
            low_copy(4 - d).wait_recv()

        mix_grad = dot(b.low[s], b.nat[:, 640:1024]).astype(BF16)
        key, value = b.qkv[s, :, 384:512], b.qkv[s, :, 512:640]
        key_grad = jnp.zeros((SEQ, HD), F32)
        value_grad = jnp.zeros((SEQ, HD), F32)
        for h in range(3):
            head = slice(h * HD, (h + 1) * HD)
            query = b.qkv[s, :, head]
            mixed = mix_grad[:, head]
            probs = causal_probs(query, key)
            dprob = dot_nt(mixed, value)
            value_grad = value_grad + dot_tn(probs.astype(BF16), mixed)
            delta = jnp.sum(probs * dprob, axis=1, keepdims=True)
            score_grad = (probs * (dprob - delta)).astype(BF16)
            b.qkv[s, :, head] = (dot(score_grad, key) * HD**-0.5).astype(BF16)
            key_grad = key_grad + dot_tn(score_grad, query)
        b.qkv[s, :, 384:512] = (key_grad * HD**-0.5).astype(BF16)
        b.qkv[s, :, 512:640] = value_grad.astype(BF16)
        for n in range(2):
            rows = slice(n * 768, (n + 1) * 768)
            b.send_x[s, 0, :, rows] = dot_nt(b.qkv[s], b.nat[rows, 0:640]).astype(BF16)

        @pl.when(i > 0)
        def _():
            norm_copy(d).start()

    for d in range(4):
        s = lax.rem(x + d, 4)
        sum_forward(s, d).wait()
        b.send_y[s, c] = (b.send_y[s, c].astype(F32) + b.pair_y[s].astype(F32)).astype(BF16)
        if d:
            sum_copy(d).start()

    for n in range(4):
        cols = slice(n * 384, (n + 1) * 384)
        result = dot_tn(b.normed[:, :, cols].reshape(512, 384), b.qkv[...].reshape(512, 640))
        b.nat[cols, 0:640] = result.astype(BF16)
        result = dot_tn(b.low[:, :, cols].reshape(512, 384), b.mix[...].reshape(512, 384))
        b.nat[cols, 640:1024] = result.astype(BF16)

    @pl.loop(0, 8)
    def _(j):
        for part in range(3):
            to_blocks(j, b.dense, pl.ds(part * 384, 384), part * 384)

    d_give = links.send(b.dense.at[:, other], b.dgot, "c", 1)
    e_next = scatter_second(
        links, e_first, e_part, (b.e_got0, b.e_got1), (b.e_last0, b.e_last1), e_cut
    )
    d_give.wait()

    @pl.loop(0, 16)
    def _(block):
        b.dense[block, c] = (b.dense[block, c].astype(F32) + b.dgot[block].astype(F32)).astype(BF16)

    d_first = scatter_first(links, d_part, (b.d_got0, b.d_got1), d_cut)
    s_next = scatter_second(
        links, s_first, s_sum, (b.s_got0, b.s_got1), (b.s_last0, b.s_last1), s_cut
    )

    for step in NEAR_FIRST:
        norm_copy(step).wait()
    scaled = b.send_x[x, 0, :, 0:D].astype(F32)
    for step in range(3):
        scaled = scaled + b.got_x[step, :, 0:D].astype(F32)
    inputs = b.tokens[...].astype(F32)
    inverse_one = lax.rsqrt(jnp.mean(inputs * inputs, axis=1, keepdims=True) + epsilon)
    b.tokens_grad[...] = (
        b.tokens_grad[...]
        + inverse_one * scaled
        - inputs
        * (inverse_one * inverse_one * inverse_one)
        * jnp.mean(scaled * inputs, axis=1, keepdims=True)
    )
    for step in NEAR_FIRST:
        sum_copy(step).wait()
    result = b.hidden[...] + b.send_y[x, c].astype(F32)
    for step in range(3):
        result = result + b.got_y[step].astype(F32)
    b.block_out[...] = result.astype(BF16)

    received(e_next)
    for part in range(2):
        rows = slice(48 * part, 48 * part + 48)
        total = scatter_end(links, (b.e_got0, b.e_got1), (b.e_last0, b.e_last1), part)
        b.g_ein[rows] = total[:, 0:1024]
        b.g_eout[rows] = total[:, 1024:1536]
    received(s_next)
    for part in range(2):
        total = scatter_end(links, (b.s_got0, b.s_got1), (b.s_last0, b.s_last1), part)
        b.back[:, W_ATT + 384 * part : W_ATT + 384 * part + 384] = total.astype(BF16)
    d_next = scatter_second(
        links, d_first, d_part, (b.d_got0, b.d_got1), (b.d_last0, b.d_last1), d_cut
    )
    received(d_next)
    for part, cols in ((0, slice(0, 640)), (1, slice(640, 1152))):
        total = scatter_end(links, (b.d_got0, b.d_got1), (b.d_last0, b.d_last1), part)
        b.back[:, cols] = total.astype(BF16)
    pick = pick_matrix((64, 48), lambda row: jnp.where(row % 16 < ROWS, row // 16 * ROWS + row % 16, -1))
    for col in range(0, W_ALL, 384):
        b.pack[:, :, col : col + 384] = moved(pick, b.back[:, col : col + 384]).reshape(4, 16, 384)
    exchange = [
        links.send(b.pack.at[lax.rem(x + step, 4)], b.arrived.at[x], "x", step)
        for step in FAR_FIRST
    ]
    b.arrived[x] = b.pack[x]

    sent(normed_sends + e_first + s_first + d_first)
    for step in NEAR_FIRST:
        rows_copy(step).wait_send()
        cot_copy(step).wait_send()
        low_copy(step).wait_send()
    for d in range(4):
        forward_rows(lax.rem(x + d, 4), d).wait_send()
        if d:
            forward_cot(lax.rem(x + d, 4), d).wait_send()
    sent(e_next + s_next + d_next)
    received(exchange)
    gain_grad = jnp.zeros((ROWS, 1), F32)
    misc = jnp.zeros((ROWS, 128), F32)
    for k in range(4):
        piece = b.arrived[k].astype(F32)[0:ROWS]
        for start, width, at in ((k * 384, 384, 0), (D + k * 128, 128, 384), (2048 + k * 128, 128, 512)):
            raw = piece[:, at : at + width]
            gain_grad = gain_grad + jnp.sum(
                raw * b.w_qkv[:, start : start + width].astype(F32), axis=1, keepdims=True
            )
            b.g_qkv[:, start : start + width] = raw * gain_one
        b.g_out[:, k * 384 : k * 384 + 384] = piece[:, 640:1024]
        misc = misc + piece[:, 1024:1152]
        for core in range(2):
            at, unit = W_ATT + 384 * core, (2 * k + core) * 128
            b.g_sin[:, unit : unit + 128] = piece[:, at : at + 128]
            b.g_sin[:, SH + unit : SH + unit + 128] = piece[:, at + 128 : at + 256]
            b.g_sout[:, unit : unit + 128] = piece[:, at + 256 : at + 384]
    b.g_misc[...] = misc
    b.g_gain[...] = jnp.broadcast_to(gain_grad, (ROWS, 128))
    sent(exchange)


def local(
    tokens,
    expert_ids,
    attn_gain,
    w_qkv,
    w_out,
    moe_gain,
    w_router,
    w_shared_in,
    w_shared_out,
    w_expert_in,
    w_expert_out,
    out_grad,
):
    results = pl.pallas_call(
        kernel,
        out_shape=[jax.ShapeDtypeStruct(shape, dtype) for shape, dtype in OUTS.values()],
        in_specs=[pl.BlockSpec(memory_space=pltpu.VMEM)] * len(INS),
        out_specs=[pl.BlockSpec(memory_space=pltpu.VMEM)] * len(OUTS),
        scratch_shapes=[
            *[pltpu.VMEM(shape, dtype) for shape, dtype in SCRATCH.values()],
            pltpu.SemaphoreType.DMA((SEMS,)),
            pltpu.SemaphoreType.DMA((SEMS,)),
        ],
        compiler_params=pltpu.CompilerParams(
            collective_id=1, has_side_effects=True, vmem_limit_bytes=(64 << 20) - (1 << 16)
        ),
        cost_estimate=pl.CostEstimate(
            flops=23_000_000_000, bytes_accessed=10_000_000, transcendentals=2_000_000
        ),
        name="block",
    )(
        tokens,
        expert_ids,
        attn_gain[:, None],
        w_qkv,
        w_out,
        w_router,
        moe_gain[:, None],
        w_shared_in,
        w_shared_out,
        w_expert_in,
        w_expert_out,
        out_grad,
    )
    block_out, tokens_grad, gain, qkv, out, misc, sin, sout, ein, eout = results
    return (
        block_out,
        tokens_grad,
        gain[:, 0],
        qkv,
        out,
        misc[:, 8],
        misc[:, 0:EXPERTS],
        sin,
        sout,
        ein,
        eout,
    )


def solution(mesh):
    wide, flat = P("fsdp", None), P("fsdp")
    return jax.shard_map(
        local,
        mesh=mesh,
        in_specs=(wide, wide, flat, wide, wide, flat, wide, wide, wide, wide, wide, wide),
        out_specs=(wide, wide, flat, wide, wide, flat, wide, wide, wide, wide, wide),
        check_vma=False,
    )
```

time: 1720 us -> 215 us (0.12); the launches traced: 1690 us -> 214 us
  blocking collectives: 607 us -> 0 us
  local copies, waits for them, and re-layouts: 466 us -> 14 us
  starting transfers between devices: 367 us -> 0 us
  Pallas kernels: 0 us -> 200 us
  matrix products: 134 us -> 0 us
  waiting for transfers between devices: 82.6 us -> 0 us
  other arithmetic: 21 us -> 0 us
    unnamed x3 -> x0, blocking collectives: 574 us -> none
    unnamed x97 -> x0, starting transfers between devices: 366 us -> none
    scatter x2 -> x0, local copies, waits for them, and re-layouts: 211 us -> none  [local(): jnp.zeros((EXPERTS, CAP, D), jnp.bfloat16).at[flat_ids, slot_index]]
    pallas_call x0 -> x1, Pallas kernels: none -> 200 us  [local(): pl.pallas_call(kernel, out_shape=[jax.ShapeDtypeStruct(shape, dtype) for...]
    unnamed x298 -> x33, local copies, waits for them, and re-layouts: 198 us -> 11.1 us
    dot_general x27 -> x0, matrix products: 134 us -> none  [the longest x1 21.4 us: local(): jnp.einsum('ecd,ech->edh', dispatched, gate_up_grad, preferred_element_ty...]
    all_gather x6 -> x0, waiting for transfers between devices: 75.5 us -> none  [the longest x1 62.1 us: local(): lax.all_gather(w_qkv, 'fsdp', axis=0, tiled=True)]
    all_gather x1 -> x0, blocking collectives: 33.2 us -> none  [local(): lax.all_gather(w_router, 'fsdp', axis=0, tiled=True)]
  transfers between devices with their start and end apart: 105 -> 0, of which waited for: 5 -> 0; matrix products, arithmetic and copies ran while one was open for 62% -> 0% of each run, Pallas kernels for 0% -> 0%
where the time goes in v1:
time: 215 us; the launch traced here: 214 us
  Pallas kernels  200 us (93%)
  local copies, waits for them, and re-layouts  14 us (7%)
    pallas_call x1, Pallas kernels, local(): pl.pallas_call(kernel, out_shape=[jax.ShapeDtypeStruct(shape, dtype) for...  200 us
    unnamed x33, local copies, waits for them, and re-layouts  11.1 us

profile of v1, /device:TPU:8, one launch (start us, length us, event | category | flops | bytes accessed | tf_op | source)
XLA Modules:
  0.0 214.3 jit_solution(10353851810904090492)
XLA Ops:
  0.6 0.0 copy-start.9
  0.7 0.6 copy-done.9
  1.3 0.0 copy-start.10
  1.3 0.7 copy.29.refs_2_
  2.0 0.0 copy-done.10
  2.0 0.0 copy-start.8
  2.0 0.7 copy.31.refs_6_
  2.7 0.0 copy-done.8
  2.7 0.0 copy-start.7
  2.7 0.7 copy.30.refs_5_
  3.4 0.0 copy-done.7
  3.4 0.7 copy.28.refs_1_
  4.1 199.7 %block.1 = (bf16[128,1536]{1,0:T(8,128)(2,1)}, f32[128,1536]{1,0:T(8,128)}, f32[12,128]{1,0:T(8,128)}, f32[12,2560]{1,0:T(8,128)}, f32[12,1536]{1,0:T(8,128)}, /...) custom-call(bf16[128,1536]{1,0:T(8,128)(2,1)} %refs_0_.1, ...), custom_call_target="tpu_custom_call" | custom-call | flops 23000000512 | bytes 10000000 | tf_op jit(solution)/shard_map/block/pallas_call | solution.py:791
  203.8 0.0 copy-start
  203.8 1.5 slice_reduce_fusion
  205.3 1.4 copy.32
  206.6 1.8 copy.41
  208.4 0.0 copy-done
  208.4 0.0 copy-start.3
  208.4 0.0 copy-start.5
  208.4 0.9 copy.42
  209.3 0.2 copy-done.3
  209.5 0.0 copy-start.1
  209.5 0.7 copy.43
  210.1 0.0 copy-done.5
  210.1 0.0 copy-start.4
  210.1 0.6 copy.44
  210.8 0.3 copy-done.4
  211.1 0.0 copy-start.6
  211.1 0.7 copy.45
  211.7 0.2 copy-done.6
  211.9 0.6 copy.46
  212.6 0.0 copy-done.1
  212.6 0.0 copy-start.2
  212.6 0.7 copy.47
  213.3 0.3 copy-done.2
  213.7 0.7 copy.48
Async XLA Ops:
  0.6 0.7 copy-start.9
  1.3 0.7 copy-start.10
  2.0 0.7 copy-start.8
  2.7 0.7 copy-start.7
  203.8 4.6 %copy-start = (f32[128,1536]{1,0:T(8,128)S(1)}, f32[128,1536]{1,0:T(8,128)}, u32[]{:S(2)}) copy-start(f32[128,1536]{1,0:T(8,128)} %get-tuple-element.67) | copy-start | bytes 2359300
  208.4 1.1 copy-start.3
  208.4 1.7 copy-start.5
  209.5 3.1 %copy-start.1 = (f32[96,1024]{1,0:T(8,128)S(1)}, f32[96,1024]{1,0:T(8,128)}, u32[]{:S(2)}) copy-start(f32[96,1024]{1,0:T(8,128)} %get-tuple-element.75) | copy-start | bytes 1179652
  210.1 0.9 copy-start.4
  211.1 0.9 copy-start.6
  212.6 1.1 copy-start.2

commit v2 on v1

--- a/solution.py
+++ b/solution.py
@@ -139,6 +139,56 @@
     return second
 
 
+class PlaneRing:
+    def __init__(self, links, first, part, cut):
+        self.links, self.part, self.cut = links, part, cut
+        received(first)
+        self.near, self.far = {}, []
+        for step, order in ((1, (0, 1)), (3, (1, 0))):
+            for h in order:
+                piece = part(pl.ds(links.z * 4 + 2 * h, 2), cut[0])
+                self.near["z", step, h] = links.send(piece, piece, "z", step)
+        for step, order in ((1, (0, 1, 2, 3)), (3, (2, 3, 0, 1))):
+            for z in order:
+                piece = part(z * 4 + links.y, cut[1])
+                self.near["y", step, z] = links.send(piece, piece, "y", step)
+
+    def pass_on(self):
+        links, part, cut = self.links, self.part, self.cut
+        for step, h in ((1, 0), (3, 1)):
+            self.near["z", step, h].wait_recv()
+            piece = part(pl.ds(lax.rem(links.z + 4 - step, 4) * 4 + 2 * h, 2), cut[0])
+            self.far.append(links.send(piece, piece, "z", step))
+        for step, z in ((1, 0), (1, 1), (3, 2), (3, 3)):
+            self.near["y", step, z].wait_recv()
+            piece = part(z * 4 + lax.rem(links.y + 4 - step, 4), cut[1])
+            self.far.append(links.send(piece, piece, "y", step))
+
+    def arrive(self):
+        passed = (("z", 1, 0), ("z", 3, 1), ("y", 1, 0), ("y", 1, 1), ("y", 3, 2), ("y", 3, 3))
+        for key, copy in self.near.items():
+            if key not in passed:
+                copy.wait_recv()
+        received(self.far)
+        sent(self.near.values())
+        sent(self.far)
+
+
+class RowRing:
+    def __init__(self, links, part):
+        self.links, self.part = links, part
+        self.first = links.take(4)
+
+    def near(self, step):
+        piece = self.part(self.links.x, pl.ds(0, SEQ))
+        return self.links.copy(piece, piece, "x", step, self.first + step)
+
+    def far(self, h):
+        step = 3 if h else 1
+        piece = self.part(lax.rem(self.links.x + 4 - step, 4), pl.ds(64 * h, 64))
+        return self.links.copy(piece, piece, "x", step, self.first + 2 * h)
+
+
 def scatter_first(links, part, got, cut):
     first = []
     for step in FAR_FIRST:
@@ -201,16 +251,18 @@
 OUTS = {
     "block_out": ((SEQ, D), BF16),
     "tokens_grad": ((SEQ, D), F32),
-    "g_gain": ((ROWS, 128), F32),
+    "g_gain_one": ((1, ROWS), F32),
     "g_qkv": ((ROWS, 2560), F32),
     "g_out": ((ROWS, D), F32),
-    "g_misc": ((ROWS, 128), F32),
+    "g_gain_two": ((1, ROWS), F32),
+    "g_router": ((EXPERTS, ROWS), F32),
     "g_sin": ((ROWS, 2 * SH), F32),
     "g_sout": ((ROWS, SH), F32),
     "g_ein": ((96, 1024), F32),
     "g_eout": ((96, 512), F32),
 }
 SCRATCH = {
+    "small": ((128, 128), F32),
     "pack": ((4, 16, W_ALL), BF16),
     "arrived": ((4, 16, W_ALL), BF16),
     "dense": ((16, 2, 48, W_ATT), BF16),
@@ -229,13 +281,13 @@
     "got_x": ((3, SEQ, WIDE), BF16),
     "hidden": ((SEQ, D), F32),
     "probs": ((SEQ, 128), F32),
+    "chosen": ((SEQ, 128), F32),
     "rows": ((4, 2, SEQ, WIDE), BF16),
     "cot": ((4, 2, SEQ, D), BF16),
     "gated": ((4, 256, 640), BF16),
     "joint": ((4, 256, 1280), BF16),
     "low": ((4, SEQ, D), BF16),
     "dsh": ((16, 2, 48, 384), BF16),
-    "dgot": ((16, 48, W_ATT), BF16),
     "back": ((48, W_ALL), BF16),
     "e_got0": ((3, 4, 48, D), BF16),
     "e_got1": ((3, 4, 48, D), BF16),
@@ -250,7 +302,7 @@
     "s_last0": ((3, 48, 384), BF16),
     "s_last1": ((3, 48, 384), BF16),
 }
-SEMS = 256
+SEMS = 320
 
 
 class Bag:
@@ -296,15 +348,25 @@
     b.got[here, :, 0:1024] = b.e_in[...]
     b.got[here, :, 1024:1536] = b.e_out[...]
     b.pack[...] = jnp.zeros_like(b.pack)
-    gain_one = b.gain_one[...].astype(F32)
+    b.small[...] = jnp.zeros_like(b.small)
+    b.small[0:EXPERTS, 0:ROWS] = b.w_router[...].astype(F32)
+    b.small[8:9, 0:ROWS] = b.gain_two[...].astype(F32)
+    b.small[9:10, 0:ROWS] = b.gain_one[...].astype(F32)
+    small = b.small[...].T
+    lane = lax.broadcasted_iota(jnp.int32, (SEQ, 128), 1)
+    row = lax.broadcasted_iota(jnp.int32, (SEQ, 128), 0)
+    named = jnp.zeros((SEQ, 128), F32)
+    for k in range(TOP):
+        named = named + (b.ids[k : k + 1, :] == row).astype(F32)
+    b.chosen[...] = named.T
+    gain_one = small[0:ROWS, 9:10]
     for k in range(4):
         for start, width, at in ((k * 384, 384, 0), (D + k * 128, 128, 384), (2048 + k * 128, 128, 512)):
             b.pack[k, 0:ROWS, at : at + width] = (
                 b.w_qkv[:, start : start + width].astype(F32) * gain_one
             ).astype(BF16)
         b.pack[k, 0:ROWS, 640:1024] = b.w_out[:, k * 384 : k * 384 + 384]
-        b.pack[k, 0:ROWS, 1024:1032] = b.w_router[...]
-        b.pack[k, 0:ROWS, 1032:1033] = b.gain_two[...]
+        b.pack[k, 0:ROWS, 1024:1152] = small[0:ROWS].astype(BF16)
         for core in range(2):
             at, unit = W_ATT + 384 * core, (2 * k + core) * 128
             b.pack[k, 0:ROWS, at : at + 128] = b.w_sin[:, unit : unit + 128]
@@ -320,12 +382,12 @@
     inverse_one = lax.rsqrt(jnp.mean(inputs * inputs, axis=1, keepdims=True) + epsilon)
     b.normed[x] = (inputs * inverse_one).astype(BF16)
     b.cot[x, c] = b.out_grad[...]
+    cot_pair = links.send(b.cot.at[x, c], b.cot.at[x, c], "c", 1)
+    b.arrived[x] = b.pack[x]
+    finish(exchange)
     normed_sends = [
         links.send(b.normed.at[x], b.normed.at[x], "x", step) for step in FAR_FIRST
     ]
-    cot_pair = links.send(b.cot.at[x, c], b.cot.at[x, c], "c", 1)
-    b.arrived[x] = b.pack[x]
-    finish(exchange)
     pick = pick_matrix((48, 64), lambda row: row // ROWS * 16 + row % ROWS)
     for col in range(0, W_ALL, 384):
         block = moved(pick, b.arrived[:, :, col : col + 384].reshape(64, 384))
@@ -340,16 +402,13 @@
     received(d_second)
     sent(d_first + d_second)
     d_pair = links.send(b.dense.at[:, c], b.dense.at[:, c], "c", 1)
-    e_second = gather_second(links, e_first, e_part, e_cut)
-    s_second = gather_second(links, s_first, s_part, s_cut)
+    d_pair.wait()
+    e_ring = PlaneRing(links, e_first, e_part, e_cut)
+    s_ring = PlaneRing(links, s_first, s_part, s_cut)
     received(normed_sends)
-    cot_base = links.take(4)
-    cot_copy = lambda step: links.copy(
-        b.cot.at[x, c], b.cot.at[x, c], "x", step, cot_base + step
-    )
-    for step in NEAR_FIRST:
-        cot_copy(step).start()
-    d_pair.wait()
+    cot_ring = RowRing(links, lambda s, rows: b.cot.at[s, c, rows])
+    for step in (1, 3):
+        cot_ring.near(step).start()
 
     order = pick_matrix(
         (192, 192), lambda row: row % 48 // ROWS * 48 + row // 48 * ROWS + row % ROWS
@@ -401,11 +460,10 @@
         def _():
             mix_copy(step).start()
 
-    received(e_second)
-    received(s_second)
-    sent(e_first + e_second + s_first + s_second)
-    half = pl.ds(pl.multiple_of(other * 384, 128), 384)
-    s_pair = links.send(b.shared.at[:, c, :, half], b.shared.at[:, c, :, half], "c", 1)
+    e_ring.pass_on()
+    s_ring.pass_on()
+    e_ring.arrive()
+    sent(e_first + s_first)
     e_pair = links.send(b.got.at[pl.ds(8 * other, 8)], b.full.at[:, c], "c", 1)
     e_own = links.local(b.got.at[pl.ds(8 * c, 8)], b.full.at[:, c])
 
@@ -420,23 +478,16 @@
     gain_two = dot_nt((lane8 == 8).astype(BF16), b.nat[:, 1024:1152])[0:1]
     moe_in = (hidden * inverse_two * gain_two).astype(BF16)
     b.rows[x, c, :, 0:D] = moe_in
-    lane = lax.broadcasted_iota(jnp.int32, (SEQ, 128), 1)
     logits = jnp.where(lane < EXPERTS, dot(moe_in, b.nat[:, 1024:1152]), -1e30)
     exponent = jnp.exp(logits - jnp.max(logits, axis=1, keepdims=True))
     router_probs = exponent / jnp.sum(exponent, axis=1, keepdims=True)
     b.probs[...] = router_probs
-    chosen = jnp.zeros((SEQ, 128), F32)
-    for k in range(TOP):
-        chosen = chosen + (b.ids[:, k : k + 1] == lane).astype(F32)
-    gates = chosen * router_probs
+    gates = b.chosen[...] * router_probs
     high = gates.astype(BF16).astype(F32)
     b.rows[x, c, :, D:WIDE] = (high + pltpu.roll(gates - high, 8, 1)).astype(BF16)
-    rows_base = links.take(4)
-    rows_copy = lambda step: links.copy(
-        b.rows.at[x, c], b.rows.at[x, c], "x", step, rows_base + step
-    )
-    for step in NEAR_FIRST:
-        rows_copy(step).start()
+    rows_ring = RowRing(links, lambda s, rows: b.rows.at[s, c, rows])
+    for step in (1, 3):
+        rows_ring.near(step).start()
     pair_rows = links.take(4)
     pair_cot = links.take(4)
     forward_rows = lambda s, d: links.copy(
@@ -444,7 +495,9 @@
     )
     forward_cot = lambda s, d: links.copy(b.cot.at[s, c], b.cot.at[s, c], "c", 1, pair_cot + d)
     forward_rows(x, 0).start()
-
+    s_ring.arrive()
+    half = pl.ds(pl.multiple_of(other * 384, 128), 384)
+    s_pair = links.send(b.shared.at[:, c, :, half], b.shared.at[:, c, :, half], "c", 1)
     s_pair.wait()
     e_pair.wait()
     e_own.wait()
@@ -453,35 +506,57 @@
     def _(j):
         to_rows(j, b.shared, pl.ds(pl.multiple_of(c * 384, 128), 384), W_ATT)
 
-    back_pair = links.take(4)
-    back_base = links.take(4)
+    back_pair = links.take(8)
+    back_base = links.take(8)
     sum_pair = links.take(4)
     sum_base = links.take(4)
-    back_forward = lambda s, d: links.copy(
-        b.send_x.at[s, other], b.pair_x.at[s], "c", 1, back_pair + d
+    parts = (pl.ds(0, 768), pl.ds(768, WIDE - 768))
+    back_forward = lambda s, d, n: links.copy(
+        b.send_x.at[s, other, :, parts[n]], b.pair_x.at[s, :, parts[n]], "c", 1, back_pair + 2 * d + n
     )
     sum_forward = lambda s, d: links.copy(
         b.send_y.at[s, other], b.pair_y.at[s], "c", 1, sum_pair + d
     )
-    back_copy = lambda step: links.copy(
-        b.send_x.at[lax.rem(x + step, 4), c], b.got_x.at[step - 1], "x", step, back_base + step
+    back_copy = lambda step, n: links.copy(
+        b.send_x.at[lax.rem(x + step, 4), c, :, parts[n]],
+        b.got_x.at[step - 1, :, parts[n]],
+        "x",
+        step,
+        back_base + 2 * step + n,
     )
     sum_copy = lambda step: links.copy(
         b.send_y.at[lax.rem(x + step, 4), c], b.got_y.at[step - 1], "x", step, sum_base + step
     )
     cot_pair.wait()
+
+    def forward(d):
+        s = lax.rem(x + d, 4)
+        for ring in (rows_ring, cot_ring):
+            if d == 2:
+                ring.far(0).wait_recv()
+                ring.far(1).wait_recv()
+            else:
+                ring.near(4 - d).wait_recv()
+                ring.far(0 if d == 3 else 1).start()
+        forward_rows(s, d).start()
+        forward_cot(s, d).start()
 
     @pl.loop(0, 4)
     def _(i):
         d = near(i)
         s = lax.rem(x + d, 4)
 
+        @pl.when(i == 1)
+        def _():
+            forward(1)
+            forward(3)
+
+        @pl.when(i == 3)
+        def _():
+            forward(2)
+
         @pl.when(i > 0)
         def _():
-            rows_copy(4 - d).wait_recv()
-            forward_rows(s, d).start()
-            cot_copy(4 - d).wait_recv()
-            forward_cot(s, d).start()
             forward_cot(s, d).wait_recv()
 
         forward_rows(s, d).wait_recv()
@@ -528,8 +603,118 @@
                 b.joint[s, :, 0:1024], b.full[4 * n : 4 * n + 4, :, :, 0:1024].reshape(768, 1024)
             ) + dot_nt(b.joint[s, :, 1024:1280], b.nat[rows, 1152:1408])
             b.send_x[s, :, :, rows] = result.astype(BF16).reshape(2, SEQ, 768)
-        back_forward(s, d).start()
-
+            back_forward(s, d, n).start()
+        for n in range(2):
+            back_forward(s, d, n).wait_recv()
+            b.send_x[s, c, :, parts[n]] = (
+                b.send_x[s, c, :, parts[n]].astype(F32) + b.pair_x[s, :, parts[n]].astype(F32)
+            ).astype(BF16)
+
+            @pl.when(i > 0)
+            def _():
+                back_copy(d, n).start()
+
+    e_got, e_last = (b.e_got0, b.e_got1), (b.e_last0, b.e_last1)
+    e_z = links.take(4)
+    e_y = links.take(16)
+    e_z_copy = lambda step: links.copy(
+        b.got.at[pl.ds(lax.rem(z + step, 4) * 4, 4), pl.ds(0, 48)],
+        b.e_got0.at[step - 1],
+        "z",
+        step,
+        e_z + step,
+    )
+    e_y_copy = lambda step, to: links.copy(
+        b.got.at[to * 4 + lax.rem(y + step, 4), pl.ds(48, 48)],
+        b.e_got1.at[step - 1, to],
+        "y",
+        step,
+        e_y + 4 * step + to,
+    )
+    e_moves = []
+    for low in range(2):
+        for n in (2 * low, 2 * low + 1):
+            cols = slice(n * 384, (n + 1) * 384)
+            tokens = b.rows[:, :, :, cols].reshape(1024, 384)
+            for at in (0, 512):
+                result = dot_tn(tokens, b.joint[:, :, at : at + 512].reshape(1024, 512))
+                b.full[2 * n : 2 * n + 2, :, :, at : at + 512] = result.astype(BF16).reshape(
+                    2, 2, 96, 512
+                )
+            grads = b.cot[:, :, :, cols].reshape(1024, 384)
+            result = dot_tn(grads, b.gated[:, :, 0:512].reshape(1024, 512))
+            result = result.astype(BF16).reshape(2, 2, 2, 48, 512)
+            for h in range(2):
+                b.dense[8 * h + 2 * n : 8 * h + 2 * n + 2, :, :, 0:512] = result[:, :, h]
+        four = pl.ds(4 * low, 4)
+        target = pl.ds(8 * c + 4 * low, 4)
+        wide, slim = pl.ds(0, 1024), pl.ds(1024, 512)
+        moves = [
+            links.send(b.full.at[four, other, :, wide], b.got.at[target, :, wide], "c", 1),
+            links.local(b.full.at[four, c, :, wide], b.got.at[target, :, wide]),
+        ]
+        for h in range(2):
+            rows, slots = pl.ds(48 * h, 48), pl.ds(8 * h + 4 * low, 4)
+            moves += [
+                links.send(
+                    b.dense.at[slots, other, :, pl.ds(0, 512)], b.got.at[target, rows, slim], "c", 1
+                ),
+                links.local(b.dense.at[slots, c, :, pl.ds(0, 512)], b.got.at[target, rows, slim]),
+            ]
+        e_moves.append(moves)
+
+    def e_start(low):
+        finish(e_moves[low])
+        for step in FAR_FIRST:
+
+            @pl.when(lax.rem(z + step, 2) == low)
+            def _():
+                e_z_copy(step).start()
+
+            for to in (low, low + 2):
+                e_y_copy(step, to).start()
+
+    e_start(0)
+
+    for step in NEAR_FIRST:
+        back_copy(step, 0).wait()
+        back_copy(step, 1).wait()
+    moe_back = b.send_x[x, c].astype(F32)
+    for step in range(3):
+        moe_back = moe_back + b.got_x[step].astype(F32)
+    raw = moe_back[:, D:WIDE]
+    router_probs = b.probs[...]
+    prob_grad = b.chosen[...] * (raw + pltpu.roll(raw, 120, 1))
+    logit_grad = router_probs * (
+        prob_grad - jnp.sum(router_probs * prob_grad, axis=1, keepdims=True)
+    )
+    logit_grad = logit_grad.astype(BF16)
+    gain_two = dot_nt((lane8 == 8).astype(BF16), b.nat[:, 1024:1152])[0:1]
+    moe_in_grad = moe_back[:, 0:D] + dot_nt(logit_grad, b.nat[:, 1024:1152])
+    hidden = b.hidden[...]
+    inverse_two = lax.rsqrt(jnp.mean(hidden * hidden, axis=1, keepdims=True) + epsilon)
+    scaled = gain_two * moe_in_grad
+    hidden_grad = (
+        b.out_grad[...].astype(F32)
+        + inverse_two * scaled
+        - hidden
+        * (inverse_two * inverse_two * inverse_two)
+        * jnp.mean(scaled * hidden, axis=1, keepdims=True)
+    )
+    b.tokens_grad[...] = hidden_grad
+    b.low[x] = hidden_grad.astype(BF16)
+    low_ring = RowRing(links, lambda s, rows: b.low.at[s, rows])
+    for step in (1, 3):
+        low_ring.near(step).start()
+    e_start(1)
+    misc_grad = dot_tn(b.rows[x, c, :, 0:D], logit_grad) + dot_tn(
+        (moe_in_grad * hidden * inverse_two).astype(BF16), (lane == 8).astype(BF16)
+    )
+    b.nat[:, 1024:1152] = misc_grad.astype(BF16)
+
+    @pl.loop(0, 4)
+    def _(d):
+        s = lax.rem(x + d, 4)
         for n in range(2):
             rows = slice(n * 768, (n + 1) * 768)
             result = dot_nt(
@@ -537,84 +722,37 @@
             ) + dot_nt(b.gated[s, :, 512:640], b.nat[rows, 1408:1536])
             b.send_y[s, :, :, rows] = result.astype(BF16).reshape(2, SEQ, 768)
         sum_forward(s, d).start()
-        back_forward(s, d).wait_recv()
-        b.send_x[s, c] = (b.send_x[s, c].astype(F32) + b.pair_x[s].astype(F32)).astype(BF16)
-
-        @pl.when(i > 0)
-        def _():
-            back_copy(d).start()
 
     for n in range(4):
         cols = slice(n * 384, (n + 1) * 384)
         tokens = b.rows[:, :, :, cols].reshape(1024, 384)
-        for at in (0, 512):
-            result = dot_tn(tokens, b.joint[:, :, at : at + 512].reshape(1024, 512))
-            b.full[2 * n : 2 * n + 2, :, :, at : at + 512] = result.astype(BF16).reshape(
-                2, 2, 96, 512
-            )
         result = dot_tn(tokens, b.joint[:, :, 1024:1280].reshape(1024, 256))
         b.nat[cols, 1152:1408] = result.astype(BF16)
         grads = b.cot[:, :, :, cols].reshape(1024, 384)
-        result = dot_tn(grads, b.gated[:, :, 0:512].reshape(1024, 512))
-        b.full[2 * n : 2 * n + 2, :, :, 1024:1536] = result.astype(BF16).reshape(2, 2, 96, 512)
         result = dot_tn(grads, b.gated[:, :, 512:640].reshape(1024, 128))
         b.nat[cols, 1408:1536] = result.astype(BF16)
-    e_give = links.send(b.full.at[:, other], b.got.at[pl.ds(8 * c, 8)], "c", 1)
-    e_keep = links.local(b.full.at[:, c], b.got.at[pl.ds(8 * c, 8)])
 
     @pl.loop(0, 8)
     def _(j):
         to_blocks(j, b.dsh, pl.ds(0, 384), W_ATT)
 
     half = pl.ds(pl.multiple_of(c * 384, 128), 384)
+    for k in range(2):
+        cot_ring.near(2 * k + 1).wait_send()
+        cot_ring.far(k).wait_send()
+    for d in range(1, 4):
+        forward_cot(lax.rem(x + d, 4), d).wait_send()
     s_give = links.send(b.dsh.at[:, other], b.shared.at[:, 0, :, half], "c", 1)
     s_keep = links.local(b.dsh.at[:, c], b.shared.at[:, 0, :, half])
     s_sum = lambda slots, half: b.shared.at[(slots, 0, *half)]
-    e_give.wait()
-    e_keep.wait()
-    e_first = scatter_first(links, e_part, (b.e_got0, b.e_got1), e_cut)
     s_give.wait()
     s_keep.wait()
     s_first = scatter_first(links, s_sum, (b.s_got0, b.s_got1), s_cut)
 
-    for step in NEAR_FIRST:
-        back_copy(step).wait()
-    moe_back = b.send_x[x, c].astype(F32)
-    for step in range(3):
-        moe_back = moe_back + b.got_x[step].astype(F32)
-    raw = moe_back[:, D:WIDE]
-    router_probs = b.probs[...]
-    chosen = jnp.zeros((SEQ, 128), F32)
-    for k in range(TOP):
-        chosen = chosen + (b.ids[:, k : k + 1] == lane).astype(F32)
-    prob_grad = chosen * (raw + pltpu.roll(raw, 120, 1))
-    logit_grad = router_probs * (
-        prob_grad - jnp.sum(router_probs * prob_grad, axis=1, keepdims=True)
-    )
-    logit_grad = logit_grad.astype(BF16)
-    gain_two = dot_nt((lane8 == 8).astype(BF16), b.nat[:, 1024:1152])[0:1]
-    moe_in_grad = moe_back[:, 0:D] + dot_nt(logit_grad, b.nat[:, 1024:1152])
-    hidden = b.hidden[...]
-    inverse_two = lax.rsqrt(jnp.mean(hidden * hidden, axis=1, keepdims=True) + epsilon)
-    misc_grad = dot_tn(b.rows[x, c, :, 0:D], logit_grad) + dot_tn(
-        (moe_in_grad * hidden * inverse_two).astype(BF16), (lane == 8).astype(BF16)
-    )
-    b.nat[:, 1024:1152] = misc_grad.astype(BF16)
-    scaled = gain_two * moe_in_grad
-    hidden_grad = (
-        b.out_grad[...].astype(F32)
-        + inverse_two * scaled
-        - hidden
-        * (inverse_two * inverse_two * inverse_two)
-        * jnp.mean(scaled * hidden, axis=1, keepdims=True)
-    )
-    b.tokens_grad[...] = hidden_grad
-    b.low[x] = hidden_grad.astype(BF16)
-    low_base = links.take(4)
-    low_copy = lambda step: links.copy(b.low.at[x], b.low.at[x], "x", step, low_base + step)
-    for step in NEAR_FIRST:
-        low_copy(step).start()
-
+    low_ring.near(1).wait_recv()
+    low_ring.far(0).start()
+    low_ring.near(3).wait_recv()
+    low_ring.far(1).start()
     norm_base = links.take(4)
     norm_copy = lambda step: links.copy(
         b.send_x.at[lax.rem(x + step, 4), 0, :, pl.ds(0, D)],
@@ -624,16 +762,18 @@
         norm_base + step,
     )
     for d in range(4):
-        back_forward(lax.rem(x + d, 4), d).wait_send()
+        for n in range(2):
+            back_forward(lax.rem(x + d, 4), d, n).wait_send()
 
     @pl.loop(0, 4)
     def _(i):
         d = near(i)
         s = lax.rem(x + d, 4)
 
-        @pl.when(i > 0)
+        @pl.when(i == 3)
         def _():
-            low_copy(4 - d).wait_recv()
+            low_ring.far(0).wait_recv()
+            low_ring.far(1).wait_recv()
 
         mix_grad = dot(b.low[s], b.nat[:, 640:1024]).astype(BF16)
         key, value = b.qkv[s, :, 384:512], b.qkv[s, :, 512:640]
@@ -667,6 +807,20 @@
         if d:
             sum_copy(d).start()
 
+    e_first = [e_z_copy(step) for step in FAR_FIRST]
+    e_first += [e_y_copy(step, to) for step in FAR_FIRST for to in range(4)]
+    e_next = scatter_second(links, e_first, e_part, e_got, e_last, e_cut)
+
+    d_base = links.take(8)
+
+    def d_landing(j):
+        rows = pl.ds(pl.multiple_of(lax.div(j, 4) * 48, 16), 48)
+        return b.cot.at[lax.rem(j, 4), :, rows, pl.ds(0, W_ATT)]
+
+    d_give = lambda j: links.copy(
+        b.dense.at[pl.ds(2 * j, 2), other], d_landing(j), "c", 1, d_base + j
+    )
+
     for n in range(4):
         cols = slice(n * 384, (n + 1) * 384)
         result = dot_tn(b.normed[:, :, cols].reshape(512, 384), b.qkv[...].reshape(512, 640))
@@ -678,16 +832,13 @@
     def _(j):
         for part in range(3):
             to_blocks(j, b.dense, pl.ds(part * 384, 384), part * 384)
-
-    d_give = links.send(b.dense.at[:, other], b.dgot, "c", 1)
-    e_next = scatter_second(
-        links, e_first, e_part, (b.e_got0, b.e_got1), (b.e_last0, b.e_last1), e_cut
-    )
-    d_give.wait()
-
-    @pl.loop(0, 16)
-    def _(block):
-        b.dense[block, c] = (b.dense[block, c].astype(F32) + b.dgot[block].astype(F32)).astype(BF16)
+        d_give(j).start()
+
+    @pl.loop(0, 8)
+    def _(j):
+        d_give(j).wait()
+        total = b.dense[pl.ds(2 * j, 2), c].astype(F32) + d_landing(j)[...].astype(F32)
+        b.dense[pl.ds(2 * j, 2), c] = total.astype(BF16)
 
     d_first = scatter_first(links, d_part, (b.d_got0, b.d_got1), d_cut)
     s_next = scatter_second(
@@ -718,7 +869,7 @@
     received(e_next)
     for part in range(2):
         rows = slice(48 * part, 48 * part + 48)
-        total = scatter_end(links, (b.e_got0, b.e_got1), (b.e_last0, b.e_last1), part)
+        total = scatter_end(links, e_got, e_last, part)
         b.g_ein[rows] = total[:, 0:1024]
         b.g_eout[rows] = total[:, 1024:1536]
     received(s_next)
@@ -742,14 +893,13 @@
     b.arrived[x] = b.pack[x]
 
     sent(normed_sends + e_first + s_first + d_first)
-    for step in NEAR_FIRST:
-        rows_copy(step).wait_send()
-        cot_copy(step).wait_send()
-        low_copy(step).wait_send()
+    for ring in (rows_ring, low_ring):
+        for step in (1, 3):
+            ring.near(step).wait_send()
+        for h in range(2):
+            ring.far(h).wait_send()
     for d in range(4):
         forward_rows(lax.rem(x + d, 4), d).wait_send()
-        if d:
-            forward_cot(lax.rem(x + d, 4), d).wait_send()
     sent(e_next + s_next + d_next)
     received(exchange)
     gain_grad = jnp.zeros((ROWS, 1), F32)
@@ -769,9 +919,18 @@
             b.g_sin[:, unit : unit + 128] = piece[:, at : at + 128]
             b.g_sin[:, SH + unit : SH + unit + 128] = piece[:, at + 128 : at + 256]
             b.g_sout[:, unit : unit + 128] = piece[:, at + 256 : at + 384]
-    b.g_misc[...] = misc
-    b.g_gain[...] = jnp.broadcast_to(gain_grad, (ROWS, 128))
+    b.small[0:ROWS] = jnp.where(lane[0:ROWS] == 9, gain_grad, misc)
+    small = b.small[...].T
+    b.g_router[...] = small[0:EXPERTS, 0:ROWS]
+    b.g_gain_two[...] = small[8:9, 0:ROWS]
+    b.g_gain_one[...] = small[9:10, 0:ROWS]
     sent(exchange)
+
+
+def hand_over(*refs):
+    n = len(OUTS)
+    for source, target in zip(refs[:n], refs[n:]):
+        target[...] = source[...]
 
 
 def local(
@@ -807,27 +966,34 @@
         name="block",
     )(
         tokens,
-        expert_ids,
-        attn_gain[:, None],
+        expert_ids.T,
+        attn_gain[None],
         w_qkv,
         w_out,
-        w_router,
-        moe_gain[:, None],
+        w_router.T,
+        moe_gain[None],
         w_shared_in,
         w_shared_out,
         w_expert_in,
         w_expert_out,
         out_grad,
     )
-    block_out, tokens_grad, gain, qkv, out, misc, sin, sout, ein, eout = results
+    results = pl.pallas_call(
+        hand_over,
+        out_shape=[jax.ShapeDtypeStruct(shape, dtype) for shape, dtype in OUTS.values()],
+        in_specs=[pl.BlockSpec(memory_space=pltpu.VMEM)] * len(OUTS),
+        out_specs=[pl.BlockSpec(memory_space=pltpu.VMEM)] * len(OUTS),
+        name="hand_over",
+    )(*results)
+    block_out, tokens_grad, gain_one, qkv, out, gain_two, router, sin, sout, ein, eout = results
     return (
         block_out,
         tokens_grad,
-        gain[:, 0],
+        gain_one[0],
         qkv,
         out,
-        misc[:, 8],
-        misc[:, 0:EXPERTS],
+        gain_two[0],
+        router.T,
         sin,
         sout,
         ein,

time: 215 us -> 182 us (0.85)
  Pallas kernels: 200 us -> 180 us
  local copies, waits for them, and re-layouts: 14 us -> 0 us
    pallas_call x1, Pallas kernels: 200 us -> 177 us  [local(): pl.pallas_call(kernel, out_shape=[jax.ShapeDtypeStruct(shape, dtype) for...]
    unnamed x33 -> x0, local copies, waits for them, and re-layouts: 11.1 us -> none
    pallas_call x0 -> x1, Pallas kernels: none -> 2.98 us  [local(): pl.pallas_call(hand_over, out_shape=[jax.ShapeDtypeStruct(shape, dtype) f...]
where the time goes in v2:
time: 182 us; the launch traced here: 181 us
  Pallas kernels  180 us (99%)
    pallas_call x1, Pallas kernels, local(): pl.pallas_call(kernel, out_shape=[jax.ShapeDtypeStruct(shape, dtype) for...  177 us

profile of v2, /device:TPU:8, one launch (start us, length us, event | category | flops | bytes accessed | tf_op | source)
XLA Modules:
  0.0 180.6 jit_solution(11124468953098391102)
XLA Ops:
  0.6 176.9 %block.1 = (bf16[128,1536]{1,0:T(8,128)(2,1)}, f32[128,1536]{1,0:T(8,128)}, f32[1,12]{1,0:T(1,128)}, f32[12,2560]{1,0:T(8,128)}, f32[12,1536]{1,0:T(8,128)}, /*i...) custom-call(bf16[128,1536]{1,0:T(8,128)(2,1)} %refs_0_.1, ...), custom_call_target="tpu_custom_call" | custom-call | flops 23000000512 | bytes 10000000 | tf_op jit(solution)/shard_map/block/pallas_call | solution.py:950
  177.5 3.0 %hand_over.1 = (bf16[128,1536]{1,0:T(8,128)(2,1)}, f32[128,1536]{1,0:T(8,128)}, f32[1,12]{1,0:T(1,128)}, f32[12,2560]{1,0:T(8,128)}, f32[12,1536]{1,0:T(8,128)},...) custom-call(bf16[128,1536]{1,0:T(8,128)(2,1)} %get-tuple-element.33., ...), custom_call_target="tpu_custom_call" | custom-call | tf_op jit(solution)/shard_map/hand_over/pallas_call | solution.py:981

commit v3 on v2

--- a/solution.py
+++ b/solution.py
@@ -125,20 +125,6 @@
     return first
 
 
-def gather_second(links, first, part, cut):
-    received(first[:3])
-    second = []
-    for step in FAR_FIRST:
-        piece = part(pl.ds(links.z * 4, 4), cut[0])
-        second.append(links.send(piece, piece, "z", step))
-    received(first[3:])
-    for step in FAR_FIRST:
-        for z in range(4):
-            piece = part(z * 4 + links.y, cut[1])
-            second.append(links.send(piece, piece, "y", step))
-    return second
-
-
 class PlaneRing:
     def __init__(self, links, first, part, cut):
         self.links, self.part, self.cut = links, part, cut
@@ -183,10 +169,76 @@
         piece = self.part(self.links.x, pl.ds(0, SEQ))
         return self.links.copy(piece, piece, "x", step, self.first + step)
 
+    def start(self):
+        self.near(1).start()
+        self.near(3).start()
+
+    def pass_on(self):
+        for step, h in ((1, 0), (3, 1)):
+            self.near(step).wait_recv()
+            self.far(h).start()
+
+    def arrive(self):
+        self.far(0).wait_recv()
+        self.far(1).wait_recv()
+
+    def sent(self):
+        for k in range(2):
+            self.near(2 * k + 1).wait_send()
+            self.far(k).wait_send()
+
     def far(self, h):
         step = 3 if h else 1
         piece = self.part(lax.rem(self.links.x + 4 - step, 4), pl.ds(64 * h, 64))
         return self.links.copy(piece, piece, "x", step, self.first + 2 * h)
+
+
+class SumRing:
+    def __init__(self, links, part, got):
+        self.links, self.part, self.got = links, part, got
+        self.first = links.take(6)
+
+    def block(self, step):
+        return lax.rem(self.links.x + step, 4)
+
+    def far(self, h):
+        rows = pl.ds(64 * h, 64)
+        return self.links.copy(
+            self.part(self.block(2), rows), self.got.at[1, rows], "x", 2 * h + 1, self.first + h
+        )
+
+    def near(self, step, early):
+        h = 1 if (step == 1) == early else 0
+        rows = pl.ds(64 * h, 64)
+        return self.links.copy(
+            self.part(self.block(step), rows),
+            self.got.at[step - 1, rows],
+            "x",
+            step,
+            self.first + 2 + (step - 1) + (0 if early else 1),
+        )
+
+    def start_far(self):
+        self.far(0).start()
+        self.far(1).start()
+
+    def pass_on(self):
+        for h, step in ((0, 1), (1, 3)):
+            self.far(h).wait_recv()
+            rows = pl.ds(64 * h, 64)
+            target = self.part(self.block(step), rows)
+            target[...] = (
+                target[...].astype(F32) + self.got[1, rows].astype(F32)
+            ).astype(BF16)
+            self.near(step, False).start()
+
+    def total(self, own):
+        for step in (1, 3):
+            for early in (True, False):
+                self.near(step, early).wait()
+        self.far(0).wait_send()
+        self.far(1).wait_send()
+        return own + self.got[0].astype(F32) + self.got[2].astype(F32)
 
 
 def scatter_first(links, part, got, cut):
@@ -385,9 +437,9 @@
     cot_pair = links.send(b.cot.at[x, c], b.cot.at[x, c], "c", 1)
     b.arrived[x] = b.pack[x]
     finish(exchange)
-    normed_sends = [
-        links.send(b.normed.at[x], b.normed.at[x], "x", step) for step in FAR_FIRST
-    ]
+    normed_ring = RowRing(links, lambda s, rows: b.normed.at[s, rows])
+    cot_ring = RowRing(links, lambda s, rows: b.cot.at[s, c, rows])
+    normed_ring.start()
     pick = pick_matrix((48, 64), lambda row: row // ROWS * 16 + row % ROWS)
     for col in range(0, W_ALL, 384):
         block = moved(pick, b.arrived[:, :, col : col + 384].reshape(64, 384))
@@ -397,18 +449,24 @@
             b.shared[here, c, :, col - W_ATT : col - W_ATT + 384] = block
 
     d_first = gather_first(links, b.dense.at[here, c], d_part, here, d_cut)
-    d_second = gather_second(links, d_first, d_part, d_cut)
+    d_ring = PlaneRing(links, d_first, d_part, d_cut)
     s_first = gather_first(links, b.shared.at[here, c], s_part, here, s_cut)
-    received(d_second)
-    sent(d_first + d_second)
-    d_pair = links.send(b.dense.at[:, c], b.dense.at[:, c], "c", 1)
-    d_pair.wait()
+    normed_ring.pass_on()
+    cot_ring.start()
+    d_ring.pass_on()
+    d_ring.arrive()
+    sent(d_first)
+    d_pair = links.take(8)
+
+    def d_forward(j):
+        piece = b.dense.at[pl.ds(2 * j, 2), c]
+        return links.copy(piece, piece, "c", 1, d_pair + j)
+
+    for j in range(8):
+        d_forward(j).start()
     e_ring = PlaneRing(links, e_first, e_part, e_cut)
     s_ring = PlaneRing(links, s_first, s_part, s_cut)
-    received(normed_sends)
-    cot_ring = RowRing(links, lambda s, rows: b.cot.at[s, c, rows])
-    for step in (1, 3):
-        cot_ring.near(step).start()
+    normed_ring.arrive()
 
     order = pick_matrix(
         (192, 192), lambda row: row % 48 // ROWS * 48 + row // 48 * ROWS + row % ROWS
@@ -430,23 +488,16 @@
 
     @pl.loop(0, 8)
     def _(j):
+        d_forward(j).wait()
         for part in range(3):
             to_rows(j, b.dense, pl.ds(part * 384, 384), part * 384)
 
     for at, width in ((0, 256), (256, 256), (512, 128)):
         result = dot(b.normed[...].reshape(512, D), b.nat[:, at : at + width])
         b.qkv[:, :, at : at + width] = result.astype(BF16).reshape(4, SEQ, width)
-    mix_base = links.take(4)
-
-    def mix_copy(step):
-        return links.copy(
-            b.send_y.at[lax.rem(x + step, 4), 0], b.got_y.at[step - 1], "x", step, mix_base + step
-        )
-
-    @pl.loop(0, 4)
-    def _(i):
-        step = far(i)
-        s = lax.rem(x + step, 4)
+    mix_ring = SumRing(links, lambda s, rows: b.send_y.at[s, 0, rows], b.got_y)
+
+    def attend(s):
         key, value = b.qkv[s, :, 384:512], b.qkv[s, :, 512:640]
         for h in range(3):
             head = slice(h * HD, (h + 1) * HD)
@@ -456,22 +507,29 @@
             rows = slice(n * 768, (n + 1) * 768)
             b.send_y[s, 0, :, rows] = dot_nt(b.mix[s], b.nat[rows, 640:1024]).astype(BF16)
 
-        @pl.when(i < 3)
+    @pl.loop(0, 4)
+    def _(i):
+        @pl.when(i == 3)
         def _():
-            mix_copy(step).start()
+            mix_ring.pass_on()
+
+        attend(lax.rem(x + far(i), 4))
+
+        @pl.when(i == 0)
+        def _():
+            mix_ring.start_far()
+
+        for k, step in ((1, 1), (2, 3)):
+
+            @pl.when(i == k)
+            def _():
+                mix_ring.near(step, True).start()
 
     e_ring.pass_on()
     s_ring.pass_on()
-    e_ring.arrive()
-    sent(e_first + s_first)
-    e_pair = links.send(b.got.at[pl.ds(8 * other, 8)], b.full.at[:, c], "c", 1)
-    e_own = links.local(b.got.at[pl.ds(8 * c, 8)], b.full.at[:, c])
-
-    for step in FAR_FIRST:
-        mix_copy(step).wait()
-    hidden = b.tokens[...].astype(F32) + b.send_y[x, 0].astype(F32)
-    for step in range(3):
-        hidden = hidden + b.got_y[step].astype(F32)
+    cot_ring.pass_on()
+
+    hidden = mix_ring.total(b.tokens[...].astype(F32) + b.send_y[x, 0].astype(F32))
     b.hidden[...] = hidden
     inverse_two = lax.rsqrt(jnp.mean(hidden * hidden, axis=1, keepdims=True) + epsilon)
     lane8 = lax.broadcasted_iota(jnp.int32, (8, 128), 1)
@@ -486,8 +544,7 @@
     high = gates.astype(BF16).astype(F32)
     b.rows[x, c, :, D:WIDE] = (high + pltpu.roll(gates - high, 8, 1)).astype(BF16)
     rows_ring = RowRing(links, lambda s, rows: b.rows.at[s, c, rows])
-    for step in (1, 3):
-        rows_ring.near(step).start()
+    rows_ring.start()
     pair_rows = links.take(4)
     pair_cot = links.take(4)
     forward_rows = lambda s, d: links.copy(
@@ -495,9 +552,14 @@
     )
     forward_cot = lambda s, d: links.copy(b.cot.at[s, c], b.cot.at[s, c], "c", 1, pair_cot + d)
     forward_rows(x, 0).start()
+    e_ring.arrive()
+    sent(e_first + s_first)
+    e_pair = links.send(b.got.at[pl.ds(8 * other, 8)], b.full.at[:, c], "c", 1)
+    e_own = links.local(b.got.at[pl.ds(8 * c, 8)], b.full.at[:, c])
     s_ring.arrive()
     half = pl.ds(pl.multiple_of(other * 384, 128), 384)
     s_pair = links.send(b.shared.at[:, c, :, half], b.shared.at[:, c, :, half], "c", 1)
+
     s_pair.wait()
     e_pair.wait()
     e_own.wait()
@@ -509,7 +571,6 @@
     back_pair = links.take(8)
     back_base = links.take(8)
     sum_pair = links.take(4)
-    sum_base = links.take(4)
     parts = (pl.ds(0, 768), pl.ds(768, WIDE - 768))
     back_forward = lambda s, d, n: links.copy(
         b.send_x.at[s, other, :, parts[n]], b.pair_x.at[s, :, parts[n]], "c", 1, back_pair + 2 * d + n
@@ -524,36 +585,33 @@
         step,
         back_base + 2 * step + n,
     )
-    sum_copy = lambda step: links.copy(
-        b.send_y.at[lax.rem(x + step, 4), c], b.got_y.at[step - 1], "x", step, sum_base + step
-    )
+    sum_ring = SumRing(links, lambda s, rows: b.send_y.at[s, c, rows], b.got_y)
     cot_pair.wait()
 
-    def forward(d):
+    rows_ring.pass_on()
+    for d in (1, 3):
+        forward_rows(lax.rem(x + d, 4), d).start()
+    cot_ring.arrive()
+    for d in range(1, 4):
+        forward_cot(lax.rem(x + d, 4), d).start()
+
+    def add_pair(i):
+        d = near(i)
         s = lax.rem(x + d, 4)
-        for ring in (rows_ring, cot_ring):
-            if d == 2:
-                ring.far(0).wait_recv()
-                ring.far(1).wait_recv()
-            else:
-                ring.near(4 - d).wait_recv()
-                ring.far(0 if d == 3 else 1).start()
-        forward_rows(s, d).start()
-        forward_cot(s, d).start()
+        for n in range(2):
+            back_forward(s, d, n).wait_recv()
+            b.send_x[s, c, :, parts[n]] = (
+                b.send_x[s, c, :, parts[n]].astype(F32) + b.pair_x[s, :, parts[n]].astype(F32)
+            ).astype(BF16)
+
+            @pl.when(i > 0)
+            def _():
+                back_copy(d, n).start()
 
     @pl.loop(0, 4)
     def _(i):
         d = near(i)
         s = lax.rem(x + d, 4)
-
-        @pl.when(i == 1)
-        def _():
-            forward(1)
-            forward(3)
-
-        @pl.when(i == 3)
-        def _():
-            forward(2)
 
         @pl.when(i > 0)
         def _():
@@ -593,6 +651,17 @@
                 a * u * (sg * (1.0 + g * (1.0 - sg)))
             ).astype(BF16)
             b.joint[s, :, second : second + width] = (a * g * sg).astype(BF16)
+            if part == 0:
+
+                @pl.when(i > 0)
+                def _():
+                    add_pair(i - 1)
+
+                @pl.when(i == 1)
+                def _():
+                    rows_ring.arrive()
+                    forward_rows(lax.rem(x + 2, 4), 2).start()
+
         gate_high = gate_grad.astype(BF16).astype(F32)
         spread = jnp.where(lanes == mine, gate_high, 0.0)
         spread = spread + jnp.where(lanes == mine + 8, gate_grad - gate_high, 0.0)
@@ -604,15 +673,8 @@
             ) + dot_nt(b.joint[s, :, 1024:1280], b.nat[rows, 1152:1408])
             b.send_x[s, :, :, rows] = result.astype(BF16).reshape(2, SEQ, 768)
             back_forward(s, d, n).start()
-        for n in range(2):
-            back_forward(s, d, n).wait_recv()
-            b.send_x[s, c, :, parts[n]] = (
-                b.send_x[s, c, :, parts[n]].astype(F32) + b.pair_x[s, :, parts[n]].astype(F32)
-            ).astype(BF16)
-
-            @pl.when(i > 0)
-            def _():
-                back_copy(d, n).start()
+
+    add_pair(jnp.int32(3))
 
     e_got, e_last = (b.e_got0, b.e_got1), (b.e_last0, b.e_last1)
     e_z = links.take(4)
@@ -675,6 +737,7 @@
                 e_y_copy(step, to).start()
 
     e_start(0)
+    e_start(1)
 
     for step in NEAR_FIRST:
         back_copy(step, 0).wait()
@@ -704,9 +767,7 @@
     b.tokens_grad[...] = hidden_grad
     b.low[x] = hidden_grad.astype(BF16)
     low_ring = RowRing(links, lambda s, rows: b.low.at[s, rows])
-    for step in (1, 3):
-        low_ring.near(step).start()
-    e_start(1)
+    low_ring.start()
     misc_grad = dot_tn(b.rows[x, c, :, 0:D], logit_grad) + dot_tn(
         (moe_in_grad * hidden * inverse_two).astype(BF16), (lane == 8).astype(BF16)
     )
@@ -737,22 +798,17 @@
         to_blocks(j, b.dsh, pl.ds(0, 384), W_ATT)
 
     half = pl.ds(pl.multiple_of(c * 384, 128), 384)
-    for k in range(2):
-        cot_ring.near(2 * k + 1).wait_send()
-        cot_ring.far(k).wait_send()
+    cot_ring.sent()
     for d in range(1, 4):
         forward_cot(lax.rem(x + d, 4), d).wait_send()
     s_give = links.send(b.dsh.at[:, other], b.shared.at[:, 0, :, half], "c", 1)
     s_keep = links.local(b.dsh.at[:, c], b.shared.at[:, 0, :, half])
     s_sum = lambda slots, half: b.shared.at[(slots, 0, *half)]
+
     s_give.wait()
     s_keep.wait()
     s_first = scatter_first(links, s_sum, (b.s_got0, b.s_got1), s_cut)
-
-    low_ring.near(1).wait_recv()
-    low_ring.far(0).start()
-    low_ring.near(3).wait_recv()
-    low_ring.far(1).start()
+    low_ring.pass_on()
     norm_base = links.take(4)
     norm_copy = lambda step: links.copy(
         b.send_x.at[lax.rem(x + step, 4), 0, :, pl.ds(0, D)],
@@ -772,8 +828,7 @@
 
         @pl.when(i == 3)
         def _():
-            low_ring.far(0).wait_recv()
-            low_ring.far(1).wait_recv()
+            low_ring.arrive()
 
         mix_grad = dot(b.low[s], b.nat[:, 640:1024]).astype(BF16)
         key, value = b.qkv[s, :, 384:512], b.qkv[s, :, 512:640]
@@ -800,17 +855,9 @@
         def _():
             norm_copy(d).start()
 
-    for d in range(4):
-        s = lax.rem(x + d, 4)
-        sum_forward(s, d).wait()
-        b.send_y[s, c] = (b.send_y[s, c].astype(F32) + b.pair_y[s].astype(F32)).astype(BF16)
-        if d:
-            sum_copy(d).start()
-
     e_first = [e_z_copy(step) for step in FAR_FIRST]
     e_first += [e_y_copy(step, to) for step in FAR_FIRST for to in range(4)]
     e_next = scatter_second(links, e_first, e_part, e_got, e_last, e_cut)
-
     d_base = links.take(8)
 
     def d_landing(j):
@@ -834,6 +881,10 @@
             to_blocks(j, b.dense, pl.ds(part * 384, 384), part * 384)
         d_give(j).start()
 
+    s_next = scatter_second(
+        links, s_first, s_sum, (b.s_got0, b.s_got1), (b.s_last0, b.s_last1), s_cut
+    )
+
     @pl.loop(0, 8)
     def _(j):
         d_give(j).wait()
@@ -841,9 +892,15 @@
         b.dense[pl.ds(2 * j, 2), c] = total.astype(BF16)
 
     d_first = scatter_first(links, d_part, (b.d_got0, b.d_got1), d_cut)
-    s_next = scatter_second(
-        links, s_first, s_sum, (b.s_got0, b.s_got1), (b.s_last0, b.s_last1), s_cut
-    )
+
+    for d in (2, 1, 3, 0):
+        s = lax.rem(x + d, 4)
+        sum_forward(s, d).wait()
+        b.send_y[s, c] = (b.send_y[s, c].astype(F32) + b.pair_y[s].astype(F32)).astype(BF16)
+        if d == 2:
+            sum_ring.start_far()
+        elif d:
+            sum_ring.near(d, True).start()
 
     for step in NEAR_FIRST:
         norm_copy(step).wait()
@@ -859,26 +916,16 @@
         * (inverse_one * inverse_one * inverse_one)
         * jnp.mean(scaled * inputs, axis=1, keepdims=True)
     )
-    for step in NEAR_FIRST:
-        sum_copy(step).wait()
-    result = b.hidden[...] + b.send_y[x, c].astype(F32)
-    for step in range(3):
-        result = result + b.got_y[step].astype(F32)
-    b.block_out[...] = result.astype(BF16)
-
-    received(e_next)
-    for part in range(2):
-        rows = slice(48 * part, 48 * part + 48)
-        total = scatter_end(links, e_got, e_last, part)
-        b.g_ein[rows] = total[:, 0:1024]
-        b.g_eout[rows] = total[:, 1024:1536]
+
+    sum_ring.pass_on()
+
+    d_next = scatter_second(
+        links, d_first, d_part, (b.d_got0, b.d_got1), (b.d_last0, b.d_last1), d_cut
+    )
     received(s_next)
     for part in range(2):
         total = scatter_end(links, (b.s_got0, b.s_got1), (b.s_last0, b.s_last1), part)
         b.back[:, W_ATT + 384 * part : W_ATT + 384 * part + 384] = total.astype(BF16)
-    d_next = scatter_second(
-        links, d_first, d_part, (b.d_got0, b.d_got1), (b.d_last0, b.d_last1), d_cut
-    )
     received(d_next)
     for part, cols in ((0, slice(0, 640)), (1, slice(640, 1152))):
         total = scatter_end(links, (b.d_got0, b.d_got1), (b.d_last0, b.d_last1), part)
@@ -891,13 +938,18 @@
         for step in FAR_FIRST
     ]
     b.arrived[x] = b.pack[x]
-
-    sent(normed_sends + e_first + s_first + d_first)
-    for ring in (rows_ring, low_ring):
-        for step in (1, 3):
-            ring.near(step).wait_send()
-        for h in range(2):
-            ring.far(h).wait_send()
+    received(e_next)
+    for part in range(2):
+        rows = slice(48 * part, 48 * part + 48)
+        total = scatter_end(links, e_got, e_last, part)
+        b.g_ein[rows] = total[:, 0:1024]
+        b.g_eout[rows] = total[:, 1024:1536]
+    result = sum_ring.total(b.hidden[...] + b.send_y[x, c].astype(F32))
+    b.block_out[...] = result.astype(BF16)
+
+    sent(e_first + s_first + d_first)
+    for ring in (normed_ring, rows_ring, low_ring):
+        ring.sent()
     for d in range(4):
         forward_rows(lax.rem(x + d, 4), d).wait_send()
     sent(e_next + s_next + d_next)

time: 182 us -> 168 us (0.923)
  Pallas kernels: 180 us -> 165 us
    pallas_call x1, Pallas kernels: 177 us -> 162 us  [local(): pl.pallas_call(kernel, out_shape=[jax.ShapeDtypeStruct(shape, dtype) for...]
where the time goes in v3:
time: 168 us; the launch traced here: 166 us
  Pallas kernels  165 us (98%)
    pallas_call x1, Pallas kernels, local(): pl.pallas_call(kernel, out_shape=[jax.ShapeDtypeStruct(shape, dtype) for...  162 us

profile of v3, /device:TPU:8, one launch (start us, length us, event | category | flops | bytes accessed | tf_op | source)
XLA Modules:
  0.0 165.9 jit_solution(16196815022980194682)
XLA Ops:
  0.6 162.2 %block.1 = (bf16[128,1536]{1,0:T(8,128)(2,1)}, f32[128,1536]{1,0:T(8,128)}, f32[1,12]{1,0:T(1,128)}, f32[12,2560]{1,0:T(8,128)}, f32[12,1536]{1,0:T(8,128)}, /*i...) custom-call(bf16[128,1536]{1,0:T(8,128)(2,1)} %refs_0_.1, ...), custom_call_target="tpu_custom_call" | custom-call | flops 23000000512 | bytes 10000000 | tf_op jit(solution)/shard_map/block/pallas_call | solution.py:1002
  162.9 3.0 %hand_over.1 = (bf16[128,1536]{1,0:T(8,128)(2,1)}, f32[128,1536]{1,0:T(8,128)}, f32[1,12]{1,0:T(1,128)}, f32[12,2560]{1,0:T(8,128)}, f32[12,1536]{1,0:T(8,128)},...) custom-call(bf16[128,1536]{1,0:T(8,128)(2,1)} %get-tuple-element.33., ...), custom_call_target="tpu_custom_call" | custom-call | tf_op jit(solution)/shard_map/hand_over/pallas_call | solution.py:1033

commit v4 on v3

--- a/solution.py
+++ b/solution.py
@@ -150,11 +150,13 @@
             piece = part(z * 4 + lax.rem(links.y + 4 - step, 4), cut[1])
             self.far.append(links.send(piece, piece, "y", step))
 
-    def arrive(self):
+    def arrive_near(self):
         passed = (("z", 1, 0), ("z", 3, 1), ("y", 1, 0), ("y", 1, 1), ("y", 3, 2), ("y", 3, 3))
         for key, copy in self.near.items():
             if key not in passed:
                 copy.wait_recv()
+
+    def arrive(self):
         received(self.far)
         sent(self.near.values())
         sent(self.far)
@@ -239,6 +241,98 @@
         self.far(0).wait_send()
         self.far(1).wait_send()
         return own + self.got[0].astype(F32) + self.got[2].astype(F32)
+
+
+class PlaneSum:
+    def __init__(self, links, full, got):
+        self.links, self.full, self.got = links, full, got
+        self.first = links.take(24)
+
+    def z_copy(self, step, q, far):
+        at = lax.rem(self.links.z + (2 if far else step), 4) * 4 + 2 * q
+        return self.links.copy(
+            self.full.at[pl.ds(at, 2), pl.ds(0, 48)],
+            self.got[0].at[1 if far else step - 1, pl.ds(2 * q, 2)],
+            "z",
+            step,
+            self.first + 2 * (0 if far else step) + q,
+        )
+
+    def y_copy(self, step, z, far):
+        at = z * 4 + lax.rem(self.links.y + (2 if far else step), 4)
+        return self.links.copy(
+            self.full.at[at, pl.ds(48, 48)],
+            self.got[1].at[1 if far else step - 1, z],
+            "y",
+            step,
+            self.first + 8 + 4 * (0 if far else step) + z,
+        )
+
+    def start(self, low):
+        for z in (low, low + 2):
+            through = 1 if z < 2 else 3
+            self.y_copy(through, z, True).start()
+            self.y_copy(4 - through, z, False).start()
+
+        @pl.when(lax.rem(self.links.z, 2) == low)
+        def _():
+            self.z_copy(1, 0, True).start()
+            self.z_copy(3, 1, True).start()
+
+        @pl.when(lax.rem(self.links.z, 2) != low)
+        def _():
+            self.z_copy(1, 1, False).start()
+            self.z_copy(3, 0, False).start()
+
+    def pass_on(self):
+        for q, step in ((0, 1), (1, 3)):
+            self.z_copy(step, q, True).wait_recv()
+            at = lax.rem(self.links.z + step, 4) * 4 + 2 * q
+            for k in range(2):
+                self.add(at + k, pl.ds(0, 48), self.got[0].at[1, 2 * q + k])
+            self.z_copy(step, q, False).start()
+        for z in range(4):
+            step = 1 if z < 2 else 3
+            self.y_copy(step, z, True).wait_recv()
+            at = z * 4 + lax.rem(self.links.y + step, 4)
+            self.add(at, pl.ds(48, 48), self.got[1].at[1, z])
+            self.y_copy(step, z, False).start()
+
+    def add(self, at, rows, what):
+        self.full[at, rows] = (self.full[at, rows].astype(F32) + what[...].astype(F32)).astype(BF16)
+
+    def second(self, last):
+        links, second = self.links, []
+        for step in (1, 3):
+            for q in range(2):
+                self.z_copy(step, q, False).wait()
+            for z in range(4):
+                self.y_copy(step, z, False).wait()
+        for half, axis in ((0, "y"), (1, "z")):
+            here = links.z if half else links.y
+
+            @pl.loop(0, 4)
+            def _(k):
+                slot = k * 4 + links.y if half else links.z * 4 + k
+                total = self.full[slot, pl.ds(48 * half, 48)].astype(F32)
+                for step in (0, 2):
+                    total = total + self.got[half][step, k].astype(F32)
+                self.got[half][0, k] = total.astype(BF16)
+
+            for step in FAR_FIRST:
+                second.append(
+                    links.send(
+                        self.got[half].at[0, lax.rem(here + step, 4)],
+                        last[half].at[step - 1],
+                        axis,
+                        step,
+                    )
+                )
+        for q, step in ((0, 1), (1, 3)):
+            self.z_copy(step, q, True).wait_send()
+        for z in range(4):
+            self.y_copy(1 if z < 2 else 3, z, True).wait_send()
+        return second
 
 
 def scatter_first(links, part, got, cut):
@@ -336,8 +430,8 @@
     "chosen": ((SEQ, 128), F32),
     "rows": ((4, 2, SEQ, WIDE), BF16),
     "cot": ((4, 2, SEQ, D), BF16),
-    "gated": ((4, 256, 640), BF16),
-    "joint": ((4, 256, 1280), BF16),
+    "gated": ((4, 2, SEQ, 640), BF16),
+    "joint": ((4, 2, SEQ, 1280), BF16),
     "low": ((4, SEQ, D), BF16),
     "dsh": ((16, 2, 48, 384), BF16),
     "back": ((48, W_ALL), BF16),
@@ -354,7 +448,7 @@
     "s_last0": ((3, 48, 384), BF16),
     "s_last1": ((3, 48, 384), BF16),
 }
-SEMS = 320
+SEMS = 400
 
 
 class Bag:
@@ -375,7 +469,7 @@
     col = lax.broadcasted_iota(jnp.int32, (SEQ, SEQ), 1)
     scores = jnp.where(col <= row, scores, -1e30)
     exponent = jnp.exp(scores - jnp.max(scores, axis=1, keepdims=True))
-    return exponent / jnp.sum(exponent, axis=1, keepdims=True)
+    return exponent * (1.0 / jnp.sum(exponent, axis=1, keepdims=True))
 
 
 def kernel(*refs):
@@ -429,7 +523,8 @@
         links.send(b.pack.at[lax.rem(x + step, 4)], b.arrived.at[x], "x", step)
         for step in FAR_FIRST
     ]
-    e_first = gather_first(links, b.got.at[here], e_part, here, e_cut)
+    e_cols = lambda cols: tuple((rows, cols) for (rows,) in e_cut)
+    e_first = gather_first(links, b.got.at[here], e_part, here, e_cols(pl.ds(0, 1024)))
     inputs = b.tokens[...].astype(F32)
     inverse_one = lax.rsqrt(jnp.mean(inputs * inputs, axis=1, keepdims=True) + epsilon)
     b.normed[x] = (inputs * inverse_one).astype(BF16)
@@ -450,10 +545,12 @@
 
     d_first = gather_first(links, b.dense.at[here, c], d_part, here, d_cut)
     d_ring = PlaneRing(links, d_first, d_part, d_cut)
-    s_first = gather_first(links, b.shared.at[here, c], s_part, here, s_cut)
     normed_ring.pass_on()
     cot_ring.start()
     d_ring.pass_on()
+    s_first = gather_first(links, b.shared.at[here, c], s_part, here, s_cut)
+    e_first += gather_first(links, b.got.at[here], e_part, here, e_cols(pl.ds(1024, 512)))
+    d_ring.arrive_near()
     d_ring.arrive()
     sent(d_first)
     d_pair = links.take(8)
@@ -492,12 +589,10 @@
         for part in range(3):
             to_rows(j, b.dense, pl.ds(part * 384, 384), part * 384)
 
-    for at, width in ((0, 256), (256, 256), (512, 128)):
-        result = dot(b.normed[...].reshape(512, D), b.nat[:, at : at + width])
-        b.qkv[:, :, at : at + width] = result.astype(BF16).reshape(4, SEQ, width)
     mix_ring = SumRing(links, lambda s, rows: b.send_y.at[s, 0, rows], b.got_y)
 
     def attend(s):
+        b.qkv[s] = dot(b.normed[s], b.nat[:, 0:640]).astype(BF16)
         key, value = b.qkv[s, :, 384:512], b.qkv[s, :, 512:640]
         for h in range(3):
             head = slice(h * HD, (h + 1) * HD)
@@ -552,17 +647,46 @@
     )
     forward_cot = lambda s, d: links.copy(b.cot.at[s, c], b.cot.at[s, c], "c", 1, pair_cot + d)
     forward_rows(x, 0).start()
+    e_hands = []
+    lower, upper = pl.ds(0, 48), pl.ds(48, 48)
+    for k in range(2):
+        for half, to_other in ((other, True), (c, False)):
+            at = 2 * half + k
+            pieces = [
+                (at == lax.rem(z + 2, 4), b.got.at[pl.ds(at * 4, 4), lower], pl.ds(4 * k, 4), lower)
+            ]
+            for to in range(4):
+                pieces.append(
+                    (to == lax.rem(y + 2, 4), b.got.at[at * 4 + to, upper], 4 * k + to, upper)
+                )
+            for is_far, source, slots, rows in pieces:
+                target = b.full.at[slots, c, rows]
+                if to_other:
+                    copy = links.copy(source, target, "c", 1, links.take(1))
+                else:
+                    copy = pltpu.make_async_copy(source, target, links.send_sem.at[links.take(1)])
+                e_hands.append((is_far, copy))
+
+    def e_hand(far_ones):
+        for is_far, copy in e_hands:
+
+            @pl.when(is_far == far_ones)
+            def _():
+                copy.start()
+
+    e_ring.arrive_near()
+    e_hand(False)
     e_ring.arrive()
+    e_hand(True)
     sent(e_first + s_first)
-    e_pair = links.send(b.got.at[pl.ds(8 * other, 8)], b.full.at[:, c], "c", 1)
-    e_own = links.local(b.got.at[pl.ds(8 * c, 8)], b.full.at[:, c])
+    s_ring.arrive_near()
     s_ring.arrive()
     half = pl.ds(pl.multiple_of(other * 384, 128), 384)
     s_pair = links.send(b.shared.at[:, c, :, half], b.shared.at[:, c, :, half], "c", 1)
 
     s_pair.wait()
-    e_pair.wait()
-    e_own.wait()
+    for _, copy in e_hands:
+        copy.wait()
 
     @pl.loop(0, 8)
     def _(j):
@@ -588,40 +712,59 @@
     sum_ring = SumRing(links, lambda s, rows: b.send_y.at[s, c, rows], b.got_y)
     cot_pair.wait()
 
-    rows_ring.pass_on()
-    for d in (1, 3):
-        forward_rows(lax.rem(x + d, 4), d).start()
     cot_ring.arrive()
     for d in range(1, 4):
         forward_cot(lax.rem(x + d, 4), d).start()
+    forward_rows(x, 0).wait_recv()
+
+    def which(i, core):
+        sides = ((i == 1) & (core == 0)) | ((i == 2) & (core == 1))
+        return ((0, i == 0), (1, sides), (3, sides), (2, i == 3))
+
+    def give_pair(i, n):
+        for d, now in which(i, other):
+
+            @pl.when(now)
+            def _():
+                back_forward(lax.rem(x + d, 4), d, n).start()
 
     def add_pair(i):
-        d = near(i)
-        s = lax.rem(x + d, 4)
-        for n in range(2):
-            back_forward(s, d, n).wait_recv()
-            b.send_x[s, c, :, parts[n]] = (
-                b.send_x[s, c, :, parts[n]].astype(F32) + b.pair_x[s, :, parts[n]].astype(F32)
-            ).astype(BF16)
-
-            @pl.when(i > 0)
+        for d, now in which(i, c):
+            s = lax.rem(x + d, 4)
+
+            @pl.when(now)
             def _():
-                back_copy(d, n).start()
+                for n in range(2):
+                    back_forward(s, d, n).wait_recv()
+                    b.send_x[s, c, :, parts[n]] = (
+                        b.send_x[s, c, :, parts[n]].astype(F32)
+                        + b.pair_x[s, :, parts[n]].astype(F32)
+                    ).astype(BF16)
+                    if d:
+                        back_copy(d, n).start()
 
     @pl.loop(0, 4)
     def _(i):
-        d = near(i)
-        s = lax.rem(x + d, 4)
-
-        @pl.when(i > 0)
-        def _():
-            forward_cot(s, d).wait_recv()
-
-        forward_rows(s, d).wait_recv()
-        tokens = b.rows[s, :, :, 0:D].reshape(256, D)
-        grads = b.cot[s].reshape(256, D)
+        one = (lax.rem(x + jnp.where(i == 0, 0, jnp.where(i == 3, 2, 1)), 4), jnp.where(i == 2, 1, 0))
+        two = (lax.rem(x + jnp.where(i == 0, 0, jnp.where(i == 3, 2, 3)), 4), jnp.where(i == 1, 0, 1))
+        both = lambda ref, cols: jnp.concatenate([ref[(*one, slice(None), cols)], ref[(*two, slice(None), cols)]], axis=0)
+
+        def keep(ref, cols, value):
+            ref[(*one, slice(None), cols)] = value[0:SEQ]
+            ref[(*two, slice(None), cols)] = value[SEQ:256]
+
+        for k, far_ones in ((1, (1, 3)), (3, (2,))):
+
+            @pl.when(i == k)
+            def _():
+                for d in far_ones:
+                    forward_cot(lax.rem(x + d, 4), d).wait_recv()
+                    forward_rows(lax.rem(x + d, 4), d).wait_recv()
+
+        tokens = both(b.rows, slice(0, D))
+        grads = both(b.cot, slice(0, D))
         lanes = lax.broadcasted_iota(jnp.int32, (256, 128), 1)
-        gate = b.rows[s, :, :, D:WIDE].reshape(256, 128).astype(F32)
+        gate = both(b.rows, slice(D, WIDE)).astype(F32)
         gate = jnp.where((lanes == mine) | (lanes == mine + 8), gate, 0.0)
         gate = jnp.sum(gate, axis=1, keepdims=True)
         gate_grad = jnp.zeros((256, 1), F32)
@@ -646,65 +789,60 @@
                 gate_grad = gate_grad + jnp.sum(act.astype(F32) * a, axis=1, keepdims=True)
                 act = (act.astype(F32) * scale).astype(BF16)
                 a = a * scale
-            b.gated[s, :, at : at + width] = act
-            b.joint[s, :, first : first + width] = (
-                a * u * (sg * (1.0 + g * (1.0 - sg)))
-            ).astype(BF16)
-            b.joint[s, :, second : second + width] = (a * g * sg).astype(BF16)
+            keep(b.gated, slice(at, at + width), act)
+            keep(
+                b.joint,
+                slice(first, first + width),
+                (a * u * (sg * (1.0 + g * (1.0 - sg)))).astype(BF16),
+            )
+            keep(b.joint, slice(second, second + width), (a * g * sg).astype(BF16))
             if part == 0:
 
                 @pl.when(i > 0)
                 def _():
                     add_pair(i - 1)
 
-                @pl.when(i == 1)
+                @pl.when(i == 2)
                 def _():
                     rows_ring.arrive()
                     forward_rows(lax.rem(x + 2, 4), 2).start()
 
+
+        @pl.when(i == 0)
+        def _():
+            rows_ring.pass_on()
+            for d in (1, 3):
+                forward_rows(lax.rem(x + d, 4), d).start()
+
         gate_high = gate_grad.astype(BF16).astype(F32)
         spread = jnp.where(lanes == mine, gate_high, 0.0)
         spread = spread + jnp.where(lanes == mine + 8, gate_grad - gate_high, 0.0)
-        b.send_x[s, :, :, D:WIDE] = spread.astype(BF16).reshape(2, SEQ, 128)
+        keep(b.send_x, slice(D, WIDE), spread.astype(BF16))
+        slopes = both(b.joint, slice(0, 1280))
         for n in range(2):
             rows = slice(n * 768, (n + 1) * 768)
             result = dot_nt(
-                b.joint[s, :, 0:1024], b.full[4 * n : 4 * n + 4, :, :, 0:1024].reshape(768, 1024)
-            ) + dot_nt(b.joint[s, :, 1024:1280], b.nat[rows, 1152:1408])
-            b.send_x[s, :, :, rows] = result.astype(BF16).reshape(2, SEQ, 768)
-            back_forward(s, d, n).start()
-
-    add_pair(jnp.int32(3))
+                slopes[:, 0:1024], b.full[4 * n : 4 * n + 4, :, :, 0:1024].reshape(768, 1024)
+            ) + dot_nt(slopes[:, 1024:1280], b.nat[rows, 1152:1408])
+            keep(b.send_x, rows, result.astype(BF16))
+            give_pair(i, n)
+
+    add_pair(3)
 
     e_got, e_last = (b.e_got0, b.e_got1), (b.e_last0, b.e_last1)
-    e_z = links.take(4)
-    e_y = links.take(16)
-    e_z_copy = lambda step: links.copy(
-        b.got.at[pl.ds(lax.rem(z + step, 4) * 4, 4), pl.ds(0, 48)],
-        b.e_got0.at[step - 1],
-        "z",
-        step,
-        e_z + step,
-    )
-    e_y_copy = lambda step, to: links.copy(
-        b.got.at[to * 4 + lax.rem(y + step, 4), pl.ds(48, 48)],
-        b.e_got1.at[step - 1, to],
-        "y",
-        step,
-        e_y + 4 * step + to,
-    )
+    e_sum = PlaneSum(links, b.got, e_got)
     e_moves = []
     for low in range(2):
         for n in (2 * low, 2 * low + 1):
             cols = slice(n * 384, (n + 1) * 384)
             tokens = b.rows[:, :, :, cols].reshape(1024, 384)
             for at in (0, 512):
-                result = dot_tn(tokens, b.joint[:, :, at : at + 512].reshape(1024, 512))
+                result = dot_tn(tokens, b.joint[:, :, :, at : at + 512].reshape(1024, 512))
                 b.full[2 * n : 2 * n + 2, :, :, at : at + 512] = result.astype(BF16).reshape(
                     2, 2, 96, 512
                 )
             grads = b.cot[:, :, :, cols].reshape(1024, 384)
-            result = dot_tn(grads, b.gated[:, :, 0:512].reshape(1024, 512))
+            result = dot_tn(grads, b.gated[:, :, :, 0:512].reshape(1024, 512))
             result = result.astype(BF16).reshape(2, 2, 2, 48, 512)
             for h in range(2):
                 b.dense[8 * h + 2 * n : 8 * h + 2 * n + 2, :, :, 0:512] = result[:, :, h]
@@ -727,14 +865,7 @@
 
     def e_start(low):
         finish(e_moves[low])
-        for step in FAR_FIRST:
-
-            @pl.when(lax.rem(z + step, 2) == low)
-            def _():
-                e_z_copy(step).start()
-
-            for to in (low, low + 2):
-                e_y_copy(step, to).start()
+        e_sum.start(low)
 
     e_start(0)
     e_start(1)
@@ -779,18 +910,18 @@
         for n in range(2):
             rows = slice(n * 768, (n + 1) * 768)
             result = dot_nt(
-                b.gated[s, :, 0:512], b.full[4 * n : 4 * n + 4, :, :, 1024:1536].reshape(768, 512)
-            ) + dot_nt(b.gated[s, :, 512:640], b.nat[rows, 1408:1536])
+                b.gated[s, :, :, 0:512].reshape(256, 512), b.full[4 * n : 4 * n + 4, :, :, 1024:1536].reshape(768, 512)
+            ) + dot_nt(b.gated[s, :, :, 512:640].reshape(256, 128), b.nat[rows, 1408:1536])
             b.send_y[s, :, :, rows] = result.astype(BF16).reshape(2, SEQ, 768)
         sum_forward(s, d).start()
 
     for n in range(4):
         cols = slice(n * 384, (n + 1) * 384)
         tokens = b.rows[:, :, :, cols].reshape(1024, 384)
-        result = dot_tn(tokens, b.joint[:, :, 1024:1280].reshape(1024, 256))
+        result = dot_tn(tokens, b.joint[:, :, :, 1024:1280].reshape(1024, 256))
         b.nat[cols, 1152:1408] = result.astype(BF16)
         grads = b.cot[:, :, :, cols].reshape(1024, 384)
-        result = dot_tn(grads, b.gated[:, :, 512:640].reshape(1024, 128))
+        result = dot_tn(grads, b.gated[:, :, :, 512:640].reshape(1024, 128))
         b.nat[cols, 1408:1536] = result.astype(BF16)
 
     @pl.loop(0, 8)
@@ -805,6 +936,7 @@
     s_keep = links.local(b.dsh.at[:, c], b.shared.at[:, 0, :, half])
     s_sum = lambda slots, half: b.shared.at[(slots, 0, *half)]
 
+    e_sum.pass_on()
     s_give.wait()
     s_keep.wait()
     s_first = scatter_first(links, s_sum, (b.s_got0, b.s_got1), s_cut)
@@ -855,9 +987,6 @@
         def _():
             norm_copy(d).start()
 
-    e_first = [e_z_copy(step) for step in FAR_FIRST]
-    e_first += [e_y_copy(step, to) for step in FAR_FIRST for to in range(4)]
-    e_next = scatter_second(links, e_first, e_part, e_got, e_last, e_cut)
     d_base = links.take(8)
 
     def d_landing(j):
@@ -874,6 +1003,8 @@
         b.nat[cols, 0:640] = result.astype(BF16)
         result = dot_tn(b.low[:, :, cols].reshape(512, 384), b.mix[...].reshape(512, 384))
         b.nat[cols, 640:1024] = result.astype(BF16)
+
+    e_next = e_sum.second(e_last)
 
     @pl.loop(0, 8)
     def _(j):
@@ -947,7 +1078,7 @@
     result = sum_ring.total(b.hidden[...] + b.send_y[x, c].astype(F32))
     b.block_out[...] = result.astype(BF16)
 
-    sent(e_first + s_first + d_first)
+    sent(s_first + d_first)
     for ring in (normed_ring, rows_ring, low_ring):
         ring.sent()
     for d in range(4):

time: 168 us -> 160 us (0.952)
  Pallas kernels: 165 us -> 158 us
    pallas_call x1, Pallas kernels: 162 us -> 155 us  [local(): pl.pallas_call(kernel, out_shape=[jax.ShapeDtypeStruct(shape, dtype) for...]
where the time goes in v4:
time: 160 us; the launch traced here: 158 us
  Pallas kernels  158 us (99%)
    pallas_call x1, Pallas kernels, local(): pl.pallas_call(kernel, out_shape=[jax.ShapeDtypeStruct(shape, dtype) for...  155 us

profile of v4, /device:TPU:8, one launch (start us, length us, event | category | flops | bytes accessed | tf_op | source)
XLA Modules:
  0.0 158.5 jit_solution(16051149837984231869)
XLA Ops:
  0.6 154.8 %block.1 = (bf16[128,1536]{1,0:T(8,128)(2,1)}, f32[128,1536]{1,0:T(8,128)}, f32[1,12]{1,0:T(1,128)}, f32[12,2560]{1,0:T(8,128)}, f32[12,1536]{1,0:T(8,128)}, /*i...) custom-call(bf16[128,1536]{1,0:T(8,128)(2,1)} %refs_0_.1, ...), custom_call_target="tpu_custom_call" | custom-call | flops 23000000512 | bytes 10000000 | tf_op jit(solution)/shard_map/block/pallas_call | solution.py:1133
  155.4 3.0 %hand_over.1 = (bf16[128,1536]{1,0:T(8,128)(2,1)}, f32[128,1536]{1,0:T(8,128)}, f32[1,12]{1,0:T(1,128)}, f32[12,2560]{1,0:T(8,128)}, f32[12,1536]{1,0:T(8,128)},...) custom-call(bf16[128,1536]{1,0:T(8,128)(2,1)} %get-tuple-element.33., ...), custom_call_target="tpu_custom_call" | custom-call | tf_op jit(solution)/shard_map/hand_over/pallas_call | solution.py:1164

commit v5 on v4

--- a/solution.py
+++ b/solution.py
@@ -40,7 +40,8 @@
     def __init__(self, send_sem, recv_sem):
         self.me = lax.axis_index("fsdp")
         self.send_sem, self.recv_sem = send_sem, recv_sem
-        self.count = 0
+        self.count = self.locals = 0
+        self.again, self.kept = None, 12
         self.x, self.y, self.z, self.c = (place(self.me, axis) for axis in "xyzc")
 
     def take(self, number):
@@ -48,11 +49,18 @@
         self.count += number
         return first
 
+    def left(self):
+        self.again = self.count
+
+    def sender(self, sem):
+        again = self.again is not None and (not isinstance(sem, int) or sem >= self.again)
+        return self.send_sem.at[sem - self.again + self.kept if again else sem]
+
     def copy(self, src, dst, axis, step, sem):
         return pltpu.make_async_remote_copy(
             src_ref=src,
             dst_ref=dst,
-            send_sem=self.send_sem.at[sem],
+            send_sem=self.sender(sem),
             recv_sem=self.recv_sem.at[sem],
             device_id=(peer(self.me, axis, step),),
             device_id_type=MESH,
@@ -64,9 +72,13 @@
         return copy
 
     def local(self, src, dst):
-        copy = pltpu.make_async_copy(src, dst, self.send_sem.at[self.take(1)])
+        copy = self.local_copy(src, dst)
         copy.start()
         return copy
+
+    def local_copy(self, src, dst):
+        self.locals += 1
+        return pltpu.make_async_copy(src, dst, self.send_sem.at[SENDS - self.locals])
 
     def greet(self, axes):
         barrier = pltpu.get_barrier_semaphore()
@@ -129,7 +141,7 @@
     def __init__(self, links, first, part, cut):
         self.links, self.part, self.cut = links, part, cut
         received(first)
-        self.near, self.far = {}, []
+        self.near, self.far, self.left = {}, [], False
         for step, order in ((1, (0, 1)), (3, (1, 0))):
             for h in order:
                 piece = part(pl.ds(links.z * 4 + 2 * h, 2), cut[0])
@@ -159,13 +171,19 @@
     def arrive(self):
         received(self.far)
         sent(self.near.values())
+        if not self.left:
+            sent(self.far)
+            self.left = True
+
+    def leave(self):
         sent(self.far)
+        self.left = True
 
 
 class RowRing:
-    def __init__(self, links, part):
+    def __init__(self, links, part, first=None):
         self.links, self.part = links, part
-        self.first = links.take(4)
+        self.first = links.take(4) if first is None else first
 
     def near(self, step):
         piece = self.part(self.links.x, pl.ds(0, SEQ))
@@ -244,140 +262,126 @@
 
 
 class PlaneSum:
-    def __init__(self, links, full, got):
-        self.links, self.full, self.got = links, full, got
+    def __init__(self, links, part, got, last):
+        self.links, self.part, self.got, self.last = links, part, got, last
         self.first = links.take(24)
+
+    def last_copy(self, half, step):
+        here = self.links.z if half else self.links.y
+        return self.links.copy(
+            self.got[half].at[0, lax.rem(here + step, 4)],
+            self.last[half].at[step - 1],
+            "z" if half else "y",
+            step,
+            self.first + 17 + 3 * half + step,
+        )
 
     def z_copy(self, step, q, far):
         at = lax.rem(self.links.z + (2 if far else step), 4) * 4 + 2 * q
         return self.links.copy(
-            self.full.at[pl.ds(at, 2), pl.ds(0, 48)],
+            self.part(pl.ds(at, 2), 0),
             self.got[0].at[1 if far else step - 1, pl.ds(2 * q, 2)],
             "z",
             step,
-            self.first + 2 * (0 if far else step) + q,
+            self.first + 2 * (0 if far else (step + 1) // 2) + q,
         )
 
     def y_copy(self, step, z, far):
         at = z * 4 + lax.rem(self.links.y + (2 if far else step), 4)
         return self.links.copy(
-            self.full.at[at, pl.ds(48, 48)],
+            self.part(at, 1),
             self.got[1].at[1 if far else step - 1, z],
             "y",
             step,
-            self.first + 8 + 4 * (0 if far else step) + z,
+            self.first + 6 + 4 * (0 if far else (step + 1) // 2) + z,
         )
 
-    def start(self, low):
+    def start_far(self, low):
         for z in (low, low + 2):
-            through = 1 if z < 2 else 3
-            self.y_copy(through, z, True).start()
-            self.y_copy(4 - through, z, False).start()
+            self.y_copy(1 if z < 2 else 3, z, True).start()
 
         @pl.when(lax.rem(self.links.z, 2) == low)
         def _():
             self.z_copy(1, 0, True).start()
             self.z_copy(3, 1, True).start()
 
-        @pl.when(lax.rem(self.links.z, 2) != low)
-        def _():
-            self.z_copy(1, 1, False).start()
-            self.z_copy(3, 0, False).start()
+    def start_near(self):
+        self.z_copy(1, 1, False).start()
+        self.z_copy(3, 0, False).start()
+        for z in range(4):
+            self.y_copy(3 if z < 2 else 1, z, False).start()
+
+    def start(self):
+        self.z_copy(1, 0, True).start()
+        self.z_copy(3, 1, True).start()
+        for z in range(4):
+            self.y_copy(1 if z < 2 else 3, z, True).start()
+        self.start_near()
+
+    def start_direct(self):
+        for step in FAR_FIRST:
+            for q in range(2):
+                self.z_copy(step, q, step == 2).start()
+            for z in range(4):
+                self.y_copy(step, z, step == 2).start()
 
     def pass_on(self):
         for q, step in ((0, 1), (1, 3)):
             self.z_copy(step, q, True).wait_recv()
             at = lax.rem(self.links.z + step, 4) * 4 + 2 * q
             for k in range(2):
-                self.add(at + k, pl.ds(0, 48), self.got[0].at[1, 2 * q + k])
+                self.add(self.part(at + k, 0), self.got[0].at[1, 2 * q + k])
             self.z_copy(step, q, False).start()
         for z in range(4):
             step = 1 if z < 2 else 3
             self.y_copy(step, z, True).wait_recv()
             at = z * 4 + lax.rem(self.links.y + step, 4)
-            self.add(at, pl.ds(48, 48), self.got[1].at[1, z])
+            self.add(self.part(at, 1), self.got[1].at[1, z])
             self.y_copy(step, z, False).start()
 
-    def add(self, at, rows, what):
-        self.full[at, rows] = (self.full[at, rows].astype(F32) + what[...].astype(F32)).astype(BF16)
-
-    def second(self, last):
-        links, second = self.links, []
-        for step in (1, 3):
-            for q in range(2):
-                self.z_copy(step, q, False).wait()
+    def add(self, target, what):
+        target[...] = (target[...].astype(F32) + what[...].astype(F32)).astype(BF16)
+
+    def second(self, direct=False):
+        links, steps = self.links, FAR_FIRST if direct else (1, 3)
+        for half in range(2):
+            for step in steps:
+                if half:
+                    for z in range(4):
+                        self.y_copy(step, z, step == 2).wait_recv()
+                else:
+                    for q in range(2):
+                        self.z_copy(step, q, step == 2).wait_recv()
+            for k in range(4):
+                slot = k * 4 + links.y if half else links.z * 4 + k
+                total = self.part(slot, half)[...].astype(F32)
+                for step in steps:
+                    total = total + self.got[half][step - 1, k].astype(F32)
+                self.got[half][0, k] = total.astype(BF16)
+
+            for step in FAR_FIRST:
+                self.last_copy(half, step).start()
+
+    def total(self, half):
+        here = self.links.z if half else self.links.y
+        received([self.last_copy(half, step) for step in FAR_FIRST])
+        total = self.got[half][0, here].astype(F32)
+        for step in range(3):
+            total = total + self.last[half][step].astype(F32)
+        return total
+
+    def sent(self):
+        for far in (True, False):
+            for q, step in ((0, 1), (1, 3)):
+                self.z_copy(step, q, far).wait_send()
+                if not far:
+                    self.z_copy(4 - step, q, far).wait_send()
             for z in range(4):
-                self.y_copy(step, z, False).wait()
-        for half, axis in ((0, "y"), (1, "z")):
-            here = links.z if half else links.y
-
-            @pl.loop(0, 4)
-            def _(k):
-                slot = k * 4 + links.y if half else links.z * 4 + k
-                total = self.full[slot, pl.ds(48 * half, 48)].astype(F32)
-                for step in (0, 2):
-                    total = total + self.got[half][step, k].astype(F32)
-                self.got[half][0, k] = total.astype(BF16)
-
-            for step in FAR_FIRST:
-                second.append(
-                    links.send(
-                        self.got[half].at[0, lax.rem(here + step, 4)],
-                        last[half].at[step - 1],
-                        axis,
-                        step,
-                    )
-                )
-        for q, step in ((0, 1), (1, 3)):
-            self.z_copy(step, q, True).wait_send()
-        for z in range(4):
-            self.y_copy(1 if z < 2 else 3, z, True).wait_send()
-        return second
-
-
-def scatter_first(links, part, got, cut):
-    first = []
-    for step in FAR_FIRST:
-        to = lax.rem(links.z + step, 4) * 4
-        first.append(links.send(part(pl.ds(to, 4), cut[0]), got[0].at[step - 1], "z", step))
-    for step in FAR_FIRST:
-        to = lax.rem(links.y + step, 4)
-        for z in range(4):
-            first.append(
-                links.send(part(z * 4 + to, cut[1]), got[1].at[step - 1, z], "y", step)
-            )
-    return first
-
-
-def scatter_second(links, first, part, got, last, cut):
-    second = []
-    for half, axis in ((0, "y"), (1, "z")):
-        received(first[3:] if half else first[:3])
-        here = links.z if half else links.y
-
-        @pl.loop(0, 4)
-        def _(k):
-            slot = k * 4 + links.y if half else links.z * 4 + k
-            total = part(slot, cut[half])[...].astype(F32)
-            for step in range(3):
-                total = total + got[half][step, k].astype(F32)
-            got[half][0, k] = total.astype(BF16)
-
-        for step in FAR_FIRST:
-            second.append(
-                links.send(
-                    got[half].at[0, lax.rem(here + step, 4)], last[half].at[step - 1], axis, step
-                )
-            )
-    return second
-
-
-def scatter_end(links, got, last, half):
-    here = links.z if half else links.y
-    total = got[half][0, here].astype(F32)
-    for step in range(3):
-        total = total + last[half][step].astype(F32)
-    return total
+                step = 1 if z < 2 else 3
+                self.y_copy(step, z, far).wait_send()
+                if not far:
+                    self.y_copy(4 - step, z, far).wait_send()
+        sent([self.last_copy(half, step) for half in range(2) for step in FAR_FIRST])
 
 
 INS = (
@@ -448,19 +452,12 @@
     "s_last0": ((3, 48, 384), BF16),
     "s_last1": ((3, 48, 384), BF16),
 }
-SEMS = 400
+SENDS, RECEIVES = 164, 254
+PAIRS = (((0, 0), (0, 1)), ((1, 0), (3, 0)), ((2, 0), (2, 1)), ((1, 1), (3, 1)))
 
 
 class Bag:
     pass
-
-
-def near(i):
-    return jnp.where(i == 2, 3, jnp.where(i == 3, 2, i))
-
-
-def far(i):
-    return jnp.where(i == 0, 2, jnp.where(i == 3, 0, jnp.where(i == 2, 3, 1)))
 
 
 def causal_probs(q, k):
@@ -474,12 +471,19 @@
 
 def kernel(*refs):
     b = Bag()
-    names = [*INS, *OUTS, *SCRATCH]
+    names = [*INS, *(name + "_result" for name in OUTS), *OUTS, *SCRATCH]
     for name, ref in zip(names, refs):
         setattr(b, name, ref)
     links = Links(*refs[len(names) :])
     x, y, z, c = links.x, links.y, links.z, links.c
     other = 1 - c
+    results = []
+    kept = links.take(links.kept)
+
+    def deliver(*ready):
+        for name in ready:
+            results.append(links.local(getattr(b, name), getattr(b, name + "_result")))
+
     here = z * 4 + y
     mine = 2 * x + c
     every = pl.ds(0, 48)
@@ -519,10 +523,16 @@
             b.pack[k, 0:ROWS, at + 128 : at + 256] = b.w_sin[:, SH + unit : SH + unit + 128]
             b.pack[k, 0:ROWS, at + 256 : at + 384] = b.w_sout[:, unit : unit + 128]
     greeted()
-    exchange = [
-        links.send(b.pack.at[lax.rem(x + step, 4)], b.arrived.at[x], "x", step)
-        for step in FAR_FIRST
-    ]
+
+    def exchange(cols):
+        return [
+            links.send(
+                b.pack.at[lax.rem(x + step, 4), :, cols], b.arrived.at[x, :, cols], "x", step
+            )
+            for step in FAR_FIRST
+        ]
+
+    exchanged = exchange(pl.ds(0, W_ATT))
     e_cols = lambda cols: tuple((rows, cols) for (rows,) in e_cut)
     e_first = gather_first(links, b.got.at[here], e_part, here, e_cols(pl.ds(0, 1024)))
     inputs = b.tokens[...].astype(F32)
@@ -531,28 +541,31 @@
     b.cot[x, c] = b.out_grad[...]
     cot_pair = links.send(b.cot.at[x, c], b.cot.at[x, c], "c", 1)
     b.arrived[x] = b.pack[x]
-    finish(exchange)
+    finish(exchanged)
+    exchanged = exchange(pl.ds(W_ATT, W_SHARED))
     normed_ring = RowRing(links, lambda s, rows: b.normed.at[s, rows])
     cot_ring = RowRing(links, lambda s, rows: b.cot.at[s, c, rows])
     normed_ring.start()
     pick = pick_matrix((48, 64), lambda row: row // ROWS * 16 + row % ROWS)
-    for col in range(0, W_ALL, 384):
+    for col in range(0, W_ATT, 384):
         block = moved(pick, b.arrived[:, :, col : col + 384].reshape(64, 384))
-        if col < W_ATT:
-            b.dense[here, c, :, col : col + 384] = block
-        else:
-            b.shared[here, c, :, col - W_ATT : col - W_ATT + 384] = block
+        b.dense[here, c, :, col : col + 384] = block
 
     d_first = gather_first(links, b.dense.at[here, c], d_part, here, d_cut)
+    sent(d_first)
+    e_first += gather_first(links, b.got.at[here], e_part, here, e_cols(pl.ds(1024, 512)))
     d_ring = PlaneRing(links, d_first, d_part, d_cut)
     normed_ring.pass_on()
     cot_ring.start()
     d_ring.pass_on()
+    d_ring.leave()
+    finish(exchanged)
+    for col in range(W_ATT, W_ALL, 384):
+        block = moved(pick, b.arrived[:, :, col : col + 384].reshape(64, 384))
+        b.shared[here, c, :, col - W_ATT : col - W_ATT + 384] = block
     s_first = gather_first(links, b.shared.at[here, c], s_part, here, s_cut)
-    e_first += gather_first(links, b.got.at[here], e_part, here, e_cols(pl.ds(1024, 512)))
     d_ring.arrive_near()
     d_ring.arrive()
-    sent(d_first)
     d_pair = links.take(8)
 
     def d_forward(j):
@@ -569,84 +582,53 @@
         (192, 192), lambda row: row % 48 // ROWS * 48 + row // 48 * ROWS + row % ROWS
     )
 
-    def to_rows(j, source, start, at):
-        piece = source[pl.ds(2 * j, 2), :, :, start].reshape(192, 384)
+    def to_rows(j, source, start, at, width):
+        piece = source[pl.ds(2 * j, 2), :, :, start].reshape(192, width)
         piece = moved(order, piece)
         for k in range(4):
             row = pl.multiple_of(k * 384 + j * 48, 16)
-            b.nat[pl.ds(row, 48), at : at + 384] = piece[k * 48 : k * 48 + 48]
-
-    def to_blocks(j, target, start, at):
+            b.nat[pl.ds(row, 48), at : at + width] = piece[k * 48 : k * 48 + 48]
+
+    def to_blocks(j, target, at, width):
         pieces = [
-            b.nat[pl.ds(pl.multiple_of(k * 384 + j * 48, 16), 48), at : at + 384] for k in range(4)
+            b.nat[pl.ds(pl.multiple_of(k * 384 + j * 48, 16), 48), at : at + width]
+            for k in range(4)
         ]
         piece = moved(order, jnp.concatenate(pieces, axis=0))
-        target[pl.ds(2 * j, 2), :, :, start] = piece.reshape(2, 2, 48, 384)
+        target[pl.ds(2 * j, 2)] = piece.reshape(2, 2, 48, width)
 
     @pl.loop(0, 8)
     def _(j):
         d_forward(j).wait()
-        for part in range(3):
-            to_rows(j, b.dense, pl.ds(part * 384, 384), part * 384)
+        to_rows(j, b.dense, pl.ds(0, W_ATT), 0, W_ATT)
 
     mix_ring = SumRing(links, lambda s, rows: b.send_y.at[s, 0, rows], b.got_y)
 
-    def attend(s):
-        b.qkv[s] = dot(b.normed[s], b.nat[:, 0:640]).astype(BF16)
-        key, value = b.qkv[s, :, 384:512], b.qkv[s, :, 512:640]
+    def attend(sequences):
+        for s in sequences:
+            b.qkv[s] = dot(b.normed[s], b.nat[:, 0:640]).astype(BF16)
         for h in range(3):
             head = slice(h * HD, (h + 1) * HD)
-            probs = causal_probs(b.qkv[s, :, head], key)
-            b.mix[s, :, head] = dot(probs.astype(BF16), value).astype(BF16)
-        for n in range(2):
-            rows = slice(n * 768, (n + 1) * 768)
-            b.send_y[s, 0, :, rows] = dot_nt(b.mix[s], b.nat[rows, 640:1024]).astype(BF16)
-
-    @pl.loop(0, 4)
-    def _(i):
-        @pl.when(i == 3)
-        def _():
-            mix_ring.pass_on()
-
-        attend(lax.rem(x + far(i), 4))
-
-        @pl.when(i == 0)
-        def _():
-            mix_ring.start_far()
-
-        for k, step in ((1, 1), (2, 3)):
-
-            @pl.when(i == k)
-            def _():
-                mix_ring.near(step, True).start()
+            for s in sequences:
+                probs = causal_probs(b.qkv[s, :, head], b.qkv[s, :, 384:512])
+                b.mix[s, :, head] = dot(probs.astype(BF16), b.qkv[s, :, 512:640]).astype(BF16)
+        for s in sequences:
+            for n in range(2):
+                rows = slice(n * 768, (n + 1) * 768)
+                b.send_y[s, 0, :, rows] = dot_nt(b.mix[s], b.nat[rows, 640:1024]).astype(BF16)
+
+    right, left, far = (lax.rem(x + step, 4) for step in (1, 3, 2))
+    attend([far])
+    mix_ring.start_far()
+    attend([right, left])
+    mix_ring.near(1, True).start()
+    mix_ring.near(3, True).start()
+    mix_ring.pass_on()
+    attend([x])
 
     e_ring.pass_on()
     s_ring.pass_on()
     cot_ring.pass_on()
-
-    hidden = mix_ring.total(b.tokens[...].astype(F32) + b.send_y[x, 0].astype(F32))
-    b.hidden[...] = hidden
-    inverse_two = lax.rsqrt(jnp.mean(hidden * hidden, axis=1, keepdims=True) + epsilon)
-    lane8 = lax.broadcasted_iota(jnp.int32, (8, 128), 1)
-    gain_two = dot_nt((lane8 == 8).astype(BF16), b.nat[:, 1024:1152])[0:1]
-    moe_in = (hidden * inverse_two * gain_two).astype(BF16)
-    b.rows[x, c, :, 0:D] = moe_in
-    logits = jnp.where(lane < EXPERTS, dot(moe_in, b.nat[:, 1024:1152]), -1e30)
-    exponent = jnp.exp(logits - jnp.max(logits, axis=1, keepdims=True))
-    router_probs = exponent / jnp.sum(exponent, axis=1, keepdims=True)
-    b.probs[...] = router_probs
-    gates = b.chosen[...] * router_probs
-    high = gates.astype(BF16).astype(F32)
-    b.rows[x, c, :, D:WIDE] = (high + pltpu.roll(gates - high, 8, 1)).astype(BF16)
-    rows_ring = RowRing(links, lambda s, rows: b.rows.at[s, c, rows])
-    rows_ring.start()
-    pair_rows = links.take(4)
-    pair_cot = links.take(4)
-    forward_rows = lambda s, d: links.copy(
-        b.rows.at[s, c], b.rows.at[s, c], "c", 1, pair_rows + d
-    )
-    forward_cot = lambda s, d: links.copy(b.cot.at[s, c], b.cot.at[s, c], "c", 1, pair_cot + d)
-    forward_rows(x, 0).start()
     e_hands = []
     lower, upper = pl.ds(0, 48), pl.ds(48, 48)
     for k in range(2):
@@ -664,7 +646,7 @@
                 if to_other:
                     copy = links.copy(source, target, "c", 1, links.take(1))
                 else:
-                    copy = pltpu.make_async_copy(source, target, links.send_sem.at[links.take(1)])
+                    copy = links.local_copy(source, target)
                 e_hands.append((is_far, copy))
 
     def e_hand(far_ones):
@@ -676,6 +658,29 @@
 
     e_ring.arrive_near()
     e_hand(False)
+
+    hidden = mix_ring.total(b.tokens[...].astype(F32) + b.send_y[x, 0].astype(F32))
+    b.hidden[...] = hidden
+    inverse_two = lax.rsqrt(jnp.mean(hidden * hidden, axis=1, keepdims=True) + epsilon)
+    lane8 = lax.broadcasted_iota(jnp.int32, (8, 128), 1)
+    gain_two = dot_nt((lane8 == 8).astype(BF16), b.nat[:, 1024:1152])[0:1]
+    moe_in = (hidden * inverse_two * gain_two).astype(BF16)
+    b.rows[x, c, :, 0:D] = moe_in
+    logits = jnp.where(lane < EXPERTS, dot(moe_in, b.nat[:, 1024:1152]), -1e30)
+    exponent = jnp.exp(logits - jnp.max(logits, axis=1, keepdims=True))
+    router_probs = exponent / jnp.sum(exponent, axis=1, keepdims=True)
+    b.probs[...] = router_probs
+    gates = b.chosen[...] * router_probs
+    high = gates.astype(BF16).astype(F32)
+    b.rows[x, c, :, D:WIDE] = (high + pltpu.roll(gates - high, 8, 1)).astype(BF16)
+    rows_ring = RowRing(links, lambda s, rows: b.rows.at[s, c, rows], kept)
+    rows_ring.start()
+    pair_rows, pair_cot = kept + 4, kept + 8
+    forward_rows = lambda s, d: links.copy(
+        b.rows.at[s, c], b.rows.at[s, c], "c", 1, pair_rows + d
+    )
+    forward_cot = lambda s, d: links.copy(b.cot.at[s, c], b.cot.at[s, c], "c", 1, pair_cot + d)
+    forward_rows(x, 0).start()
     e_ring.arrive()
     e_hand(True)
     sent(e_first + s_first)
@@ -684,16 +689,18 @@
     half = pl.ds(pl.multiple_of(other * 384, 128), 384)
     s_pair = links.send(b.shared.at[:, c, :, half], b.shared.at[:, c, :, half], "c", 1)
 
-    s_pair.wait()
     for _, copy in e_hands:
         copy.wait()
 
-    @pl.loop(0, 8)
-    def _(j):
-        to_rows(j, b.shared, pl.ds(pl.multiple_of(c * 384, 128), 384), W_ATT)
-
+    def shared_rows():
+        s_pair.wait()
+
+        @pl.loop(0, 8)
+        def _(j):
+            to_rows(j, b.shared, pl.ds(pl.multiple_of(c * 384, 128), 384), W_ATT, 384)
+
+    links.left()
     back_pair = links.take(8)
-    back_base = links.take(8)
     sum_pair = links.take(4)
     parts = (pl.ds(0, 768), pl.ds(768, WIDE - 768))
     back_forward = lambda s, d, n: links.copy(
@@ -702,24 +709,20 @@
     sum_forward = lambda s, d: links.copy(
         b.send_y.at[s, other], b.pair_y.at[s], "c", 1, sum_pair + d
     )
-    back_copy = lambda step, n: links.copy(
-        b.send_x.at[lax.rem(x + step, 4), c, :, parts[n]],
-        b.got_x.at[step - 1, :, parts[n]],
-        "x",
-        step,
-        back_base + 2 * step + n,
-    )
+    back_ring = SumRing(links, lambda s, rows: b.send_x.at[s, c, rows], b.got_x)
     sum_ring = SumRing(links, lambda s, rows: b.send_y.at[s, c, rows], b.got_y)
     cot_pair.wait()
 
+    normed_ring.sent()
+    cot_ring.sent()
     cot_ring.arrive()
     for d in range(1, 4):
         forward_cot(lax.rem(x + d, 4), d).start()
     forward_rows(x, 0).wait_recv()
 
     def which(i, core):
-        sides = ((i == 1) & (core == 0)) | ((i == 2) & (core == 1))
-        return ((0, i == 0), (1, sides), (3, sides), (2, i == 3))
+        sides = ((i == 1) & (core == 0)) | ((i == 3) & (core == 1))
+        return ((0, i == 0), (1, sides), (3, sides), (2, i == 2))
 
     def give_pair(i, n):
         for d, now in which(i, other):
@@ -728,32 +731,57 @@
             def _():
                 back_forward(lax.rem(x + d, 4), d, n).start()
 
-    def add_pair(i):
+    def add_pair(i, n):
         for d, now in which(i, c):
             s = lax.rem(x + d, 4)
 
             @pl.when(now)
             def _():
-                for n in range(2):
-                    back_forward(s, d, n).wait_recv()
-                    b.send_x[s, c, :, parts[n]] = (
-                        b.send_x[s, c, :, parts[n]].astype(F32)
-                        + b.pair_x[s, :, parts[n]].astype(F32)
-                    ).astype(BF16)
-                    if d:
-                        back_copy(d, n).start()
+                back_forward(s, d, n).wait_recv()
+                b.send_x[s, c, :, parts[n]] = (
+                    b.send_x[s, c, :, parts[n]].astype(F32) + b.pair_x[s, :, parts[n]].astype(F32)
+                ).astype(BF16)
+                if n and d == 2:
+                    back_ring.start_far()
+                elif n and d:
+                    back_ring.near(d, True).start()
+
+    def pair_of(i):
+        def chosen(k, what):
+            values = [PAIRS[step][k][what] for step in range(4)]
+            result = values[3]
+            for step in range(3):
+                result = jnp.where(i == step, values[step], result)
+            return result
+
+        return [(lax.rem(x + chosen(k, 0), 4), chosen(k, 1)) for k in range(2)]
+
+    def both(i, ref, cols):
+        return jnp.concatenate([ref[s, core, :, cols] for s, core in pair_of(i)], axis=0)
+
+    def keep(i, ref, cols, value):
+        for k, (s, core) in enumerate(pair_of(i)):
+            ref[s, core, :, cols] = value[k * SEQ : (k + 1) * SEQ]
+
+    def row_grads(i):
+        slopes = both(i, b.joint, slice(0, 1280))
+        for n in range(2):
+            rows = slice(n * 768, (n + 1) * 768)
+            result = dot_nt(
+                slopes[:, 0:1024], b.full[4 * n : 4 * n + 4, :, :, 0:1024].reshape(768, 1024)
+            ) + dot_nt(slopes[:, 1024:1280], b.nat[rows, 1152:1408])
+            keep(i, b.send_x, rows, result.astype(BF16))
+            give_pair(i, n)
+            if n == 0:
+
+                @pl.when(i == 1)
+                def _():
+                    rows_ring.arrive()
+                    forward_rows(lax.rem(x + 2, 4), 2).start()
 
     @pl.loop(0, 4)
     def _(i):
-        one = (lax.rem(x + jnp.where(i == 0, 0, jnp.where(i == 3, 2, 1)), 4), jnp.where(i == 2, 1, 0))
-        two = (lax.rem(x + jnp.where(i == 0, 0, jnp.where(i == 3, 2, 3)), 4), jnp.where(i == 1, 0, 1))
-        both = lambda ref, cols: jnp.concatenate([ref[(*one, slice(None), cols)], ref[(*two, slice(None), cols)]], axis=0)
-
-        def keep(ref, cols, value):
-            ref[(*one, slice(None), cols)] = value[0:SEQ]
-            ref[(*two, slice(None), cols)] = value[SEQ:256]
-
-        for k, far_ones in ((1, (1, 3)), (3, (2,))):
+        for k, far_ones in ((1, (1, 3)), (2, (2,))):
 
             @pl.when(i == k)
             def _():
@@ -761,10 +789,14 @@
                     forward_cot(lax.rem(x + d, 4), d).wait_recv()
                     forward_rows(lax.rem(x + d, 4), d).wait_recv()
 
-        tokens = both(b.rows, slice(0, D))
-        grads = both(b.cot, slice(0, D))
+        @pl.when(i > 0)
+        def _():
+            add_pair(i - 1, 0)
+
+        tokens = both(i, b.rows, slice(0, D))
+        grads = both(i, b.cot, slice(0, D))
         lanes = lax.broadcasted_iota(jnp.int32, (256, 128), 1)
-        gate = both(b.rows, slice(D, WIDE)).astype(F32)
+        gate = both(i, b.rows, slice(D, WIDE)).astype(F32)
         gate = jnp.where((lanes == mine) | (lanes == mine + 8), gate, 0.0)
         gate = jnp.sum(gate, axis=1, keepdims=True)
         gate_grad = jnp.zeros((256, 1), F32)
@@ -776,6 +808,11 @@
                 a = dot(grads, b.full[:, :, :, at + 1024 : at + 1280].reshape(D, 256))
                 first, second, scale = at, at + 512, gate
             else:
+
+                @pl.when(i == 0)
+                def _():
+                    shared_rows()
+
                 at, width = 512, 128
                 gu = dot(tokens, b.nat[:, 1152:1408])
                 g, u = gu[:, 0:128], gu[:, 128:256]
@@ -789,24 +826,22 @@
                 gate_grad = gate_grad + jnp.sum(act.astype(F32) * a, axis=1, keepdims=True)
                 act = (act.astype(F32) * scale).astype(BF16)
                 a = a * scale
-            keep(b.gated, slice(at, at + width), act)
+            keep(i, b.gated, slice(at, at + width), act)
             keep(
+                i,
                 b.joint,
                 slice(first, first + width),
                 (a * u * (sg * (1.0 + g * (1.0 - sg)))).astype(BF16),
             )
-            keep(b.joint, slice(second, second + width), (a * g * sg).astype(BF16))
-            if part == 0:
-
-                @pl.when(i > 0)
-                def _():
-                    add_pair(i - 1)
-
-                @pl.when(i == 2)
-                def _():
-                    rows_ring.arrive()
-                    forward_rows(lax.rem(x + 2, 4), 2).start()
-
+            keep(i, b.joint, slice(second, second + width), (a * g * sg).astype(BF16))
+        gate_high = gate_grad.astype(BF16).astype(F32)
+        spread = jnp.where(lanes == mine, gate_high, 0.0)
+        spread = spread + jnp.where(lanes == mine + 8, gate_grad - gate_high, 0.0)
+        keep(i, b.send_x, slice(D, WIDE), spread.astype(BF16))
+
+        @pl.when(i > 0)
+        def _():
+            add_pair(i - 1, 1)
 
         @pl.when(i == 0)
         def _():
@@ -814,26 +849,28 @@
             for d in (1, 3):
                 forward_rows(lax.rem(x + d, 4), d).start()
 
-        gate_high = gate_grad.astype(BF16).astype(F32)
-        spread = jnp.where(lanes == mine, gate_high, 0.0)
-        spread = spread + jnp.where(lanes == mine + 8, gate_grad - gate_high, 0.0)
-        keep(b.send_x, slice(D, WIDE), spread.astype(BF16))
-        slopes = both(b.joint, slice(0, 1280))
-        for n in range(2):
-            rows = slice(n * 768, (n + 1) * 768)
-            result = dot_nt(
-                slopes[:, 0:1024], b.full[4 * n : 4 * n + 4, :, :, 0:1024].reshape(768, 1024)
-            ) + dot_nt(slopes[:, 1024:1280], b.nat[rows, 1152:1408])
-            keep(b.send_x, rows, result.astype(BF16))
-            give_pair(i, n)
-
-    add_pair(3)
-
-    e_got, e_last = (b.e_got0, b.e_got1), (b.e_last0, b.e_last1)
-    e_sum = PlaneSum(links, b.got, e_got)
+        row_grads(i)
+
+    add_pair(3, 0)
+    add_pair(3, 1)
+
+
+    e_sum = PlaneSum(
+        links,
+        lambda slots, half: b.got.at[slots, pl.ds(48 * half, 48)],
+        (b.e_got0, b.e_got1),
+        (b.e_last0, b.e_last1),
+    )
     e_moves = []
+
+    def e_start(low):
+        finish(e_moves[low])
+        e_sum.start_far(low)
+
     for low in range(2):
         for n in (2 * low, 2 * low + 1):
+            if n == 3:
+                e_start(0)
             cols = slice(n * 384, (n + 1) * 384)
             tokens = b.rows[:, :, :, cols].reshape(1024, 384)
             for at in (0, 512):
@@ -862,20 +899,12 @@
                 links.local(b.dense.at[slots, c, :, pl.ds(0, 512)], b.got.at[target, rows, slim]),
             ]
         e_moves.append(moves)
-
-    def e_start(low):
-        finish(e_moves[low])
-        e_sum.start(low)
-
-    e_start(0)
+        if not low:
+            back_ring.pass_on()
+
     e_start(1)
 
-    for step in NEAR_FIRST:
-        back_copy(step, 0).wait()
-        back_copy(step, 1).wait()
-    moe_back = b.send_x[x, c].astype(F32)
-    for step in range(3):
-        moe_back = moe_back + b.got_x[step].astype(F32)
+    moe_back = back_ring.total(b.send_x[x, c].astype(F32))
     raw = moe_back[:, D:WIDE]
     router_probs = b.probs[...]
     prob_grad = b.chosen[...] * (raw + pltpu.roll(raw, 120, 1))
@@ -899,6 +928,7 @@
     b.low[x] = hidden_grad.astype(BF16)
     low_ring = RowRing(links, lambda s, rows: b.low.at[s, rows])
     low_ring.start()
+    e_sum.start_near()
     misc_grad = dot_tn(b.rows[x, c, :, 0:D], logit_grad) + dot_tn(
         (moe_in_grad * hidden * inverse_two).astype(BF16), (lane == 8).astype(BF16)
     )
@@ -926,103 +956,74 @@
 
     @pl.loop(0, 8)
     def _(j):
-        to_blocks(j, b.dsh, pl.ds(0, 384), W_ATT)
+        to_blocks(j, b.dsh, W_ATT, 384)
 
     half = pl.ds(pl.multiple_of(c * 384, 128), 384)
-    cot_ring.sent()
     for d in range(1, 4):
         forward_cot(lax.rem(x + d, 4), d).wait_send()
     s_give = links.send(b.dsh.at[:, other], b.shared.at[:, 0, :, half], "c", 1)
     s_keep = links.local(b.dsh.at[:, c], b.shared.at[:, 0, :, half])
-    s_sum = lambda slots, half: b.shared.at[(slots, 0, *half)]
+    s_sum = PlaneSum(
+        links,
+        lambda slots, half: b.shared.at[slots, 0, :, pl.ds(384 * half, 384)],
+        (b.s_got0, b.s_got1),
+        (b.s_last0, b.s_last1),
+    )
 
     e_sum.pass_on()
-    s_give.wait()
-    s_keep.wait()
-    s_first = scatter_first(links, s_sum, (b.s_got0, b.s_got1), s_cut)
-    low_ring.pass_on()
-    norm_base = links.take(4)
-    norm_copy = lambda step: links.copy(
-        b.send_x.at[lax.rem(x + step, 4), 0, :, pl.ds(0, D)],
-        b.got_x.at[step - 1, :, pl.ds(0, D)],
-        "x",
-        step,
-        norm_base + step,
+    norm_ring = SumRing(
+        links,
+        lambda s, rows: b.send_x.at[s, 0, rows, pl.ds(0, D)],
+        b.got_x.at[:, :, pl.ds(0, D)],
     )
     for d in range(4):
         for n in range(2):
             back_forward(lax.rem(x + d, 4), d, n).wait_send()
 
-    @pl.loop(0, 4)
-    def _(i):
-        d = near(i)
-        s = lax.rem(x + d, 4)
-
-        @pl.when(i == 3)
-        def _():
-            low_ring.arrive()
-
-        mix_grad = dot(b.low[s], b.nat[:, 640:1024]).astype(BF16)
-        key, value = b.qkv[s, :, 384:512], b.qkv[s, :, 512:640]
-        key_grad = jnp.zeros((SEQ, HD), F32)
-        value_grad = jnp.zeros((SEQ, HD), F32)
+    def attend_back(sequences):
+        mix_grads, parts_of = [], []
+        for s in sequences:
+            mix_grads.append(dot(b.low[s], b.nat[:, 640:1024]).astype(BF16))
+            parts_of.append((jnp.zeros((SEQ, HD), F32), jnp.zeros((SEQ, HD), F32)))
         for h in range(3):
             head = slice(h * HD, (h + 1) * HD)
-            query = b.qkv[s, :, head]
-            mixed = mix_grad[:, head]
-            probs = causal_probs(query, key)
-            dprob = dot_nt(mixed, value)
-            value_grad = value_grad + dot_tn(probs.astype(BF16), mixed)
-            delta = jnp.sum(probs * dprob, axis=1, keepdims=True)
-            score_grad = (probs * (dprob - delta)).astype(BF16)
-            b.qkv[s, :, head] = (dot(score_grad, key) * HD**-0.5).astype(BF16)
-            key_grad = key_grad + dot_tn(score_grad, query)
-        b.qkv[s, :, 384:512] = (key_grad * HD**-0.5).astype(BF16)
-        b.qkv[s, :, 512:640] = value_grad.astype(BF16)
-        for n in range(2):
-            rows = slice(n * 768, (n + 1) * 768)
-            b.send_x[s, 0, :, rows] = dot_nt(b.qkv[s], b.nat[rows, 0:640]).astype(BF16)
-
-        @pl.when(i > 0)
-        def _():
-            norm_copy(d).start()
-
-    d_base = links.take(8)
-
-    def d_landing(j):
-        rows = pl.ds(pl.multiple_of(lax.div(j, 4) * 48, 16), 48)
-        return b.cot.at[lax.rem(j, 4), :, rows, pl.ds(0, W_ATT)]
-
-    d_give = lambda j: links.copy(
-        b.dense.at[pl.ds(2 * j, 2), other], d_landing(j), "c", 1, d_base + j
-    )
-
-    for n in range(4):
-        cols = slice(n * 384, (n + 1) * 384)
-        result = dot_tn(b.normed[:, :, cols].reshape(512, 384), b.qkv[...].reshape(512, 640))
-        b.nat[cols, 0:640] = result.astype(BF16)
-        result = dot_tn(b.low[:, :, cols].reshape(512, 384), b.mix[...].reshape(512, 384))
-        b.nat[cols, 640:1024] = result.astype(BF16)
-
-    e_next = e_sum.second(e_last)
-
-    @pl.loop(0, 8)
-    def _(j):
-        for part in range(3):
-            to_blocks(j, b.dense, pl.ds(part * 384, 384), part * 384)
-        d_give(j).start()
-
-    s_next = scatter_second(
-        links, s_first, s_sum, (b.s_got0, b.s_got1), (b.s_last0, b.s_last1), s_cut
-    )
-
-    @pl.loop(0, 8)
-    def _(j):
-        d_give(j).wait()
-        total = b.dense[pl.ds(2 * j, 2), c].astype(F32) + d_landing(j)[...].astype(F32)
-        b.dense[pl.ds(2 * j, 2), c] = total.astype(BF16)
-
-    d_first = scatter_first(links, d_part, (b.d_got0, b.d_got1), d_cut)
+            for k, s in enumerate(sequences):
+                key_grad, value_grad = parts_of[k]
+                key, value = b.qkv[s, :, 384:512], b.qkv[s, :, 512:640]
+                query = b.qkv[s, :, head]
+                mixed = mix_grads[k][:, head]
+                probs = causal_probs(query, key)
+                dprob = dot_nt(mixed, value)
+                value_grad = value_grad + dot_tn(probs.astype(BF16), mixed)
+                delta = jnp.sum(probs * dprob, axis=1, keepdims=True)
+                score_grad = (probs * (dprob - delta)).astype(BF16)
+                b.qkv[s, :, head] = (dot(score_grad, key) * HD**-0.5).astype(BF16)
+                parts_of[k] = (key_grad + dot_tn(score_grad, query), value_grad)
+        for k, s in enumerate(sequences):
+            key_grad, value_grad = parts_of[k]
+            b.qkv[s, :, 384:512] = (key_grad * HD**-0.5).astype(BF16)
+            b.qkv[s, :, 512:640] = value_grad.astype(BF16)
+
+    def normed_back(sequences):
+        for s in sequences:
+            for n in range(2):
+                rows = slice(n * 768, (n + 1) * 768)
+                b.send_x[s, 0, :, rows] = dot_nt(b.qkv[s], b.nat[rows, 0:640]).astype(BF16)
+
+    attend_back([x])
+    low_ring.pass_on()
+    normed_back([x])
+    attend_back([right, left])
+    normed_back([right, left])
+    norm_ring.near(1, True).start()
+    norm_ring.near(3, True).start()
+    s_give.wait()
+    s_keep.wait()
+    s_sum.start()
+    low_ring.arrive()
+    attend_back([far])
+    normed_back([far])
+    norm_ring.start_far()
 
     for d in (2, 1, 3, 0):
         s = lax.rem(x + d, 4)
@@ -1032,12 +1033,49 @@
             sum_ring.start_far()
         elif d:
             sum_ring.near(d, True).start()
-
-    for step in NEAR_FIRST:
-        norm_copy(step).wait()
-    scaled = b.send_x[x, 0, :, 0:D].astype(F32)
-    for step in range(3):
-        scaled = scaled + b.got_x[step, :, 0:D].astype(F32)
+    e_sum.second()
+    d_base = links.take(8)
+
+    def d_landing(j):
+        rows = pl.ds(pl.multiple_of(lax.div(j, 4) * 48, 16), 48)
+        return b.cot.at[lax.rem(j, 4), :, rows, pl.ds(0, W_ATT)]
+
+    d_give = lambda j: links.copy(
+        b.dense.at[pl.ds(2 * j, 2), other], d_landing(j), "c", 1, d_base + j
+    )
+
+    for n in range(4):
+        cols = slice(n * 384, (n + 1) * 384)
+        result = dot_tn(b.normed[:, :, cols].reshape(512, 384), b.qkv[...].reshape(512, 640))
+        b.nat[cols, 0:640] = result.astype(BF16)
+        result = dot_tn(b.low[:, :, cols].reshape(512, 384), b.mix[...].reshape(512, 384))
+        b.nat[cols, 640:1024] = result.astype(BF16)
+
+    @pl.loop(0, 8)
+    def _(j):
+        to_blocks(j, b.dense, 0, W_ATT)
+        d_give(j).start()
+
+    s_sum.pass_on()
+
+    @pl.loop(0, 8)
+    def _(j):
+        d_give(j).wait()
+        total = b.dense[pl.ds(2 * j, 2), c].astype(F32) + d_landing(j)[...].astype(F32)
+        b.dense[pl.ds(2 * j, 2), c] = total.astype(BF16)
+
+    d_sum = PlaneSum(
+        links,
+        lambda slots, half: d_part(slots, d_cut[half]),
+        (b.d_got0, b.d_got1),
+        (b.d_last0, b.d_last1),
+    )
+    d_sum.start_direct()
+
+    s_sum.second()
+    norm_ring.pass_on()
+
+    scaled = norm_ring.total(b.send_x[x, 0, :, 0:D].astype(F32))
     inputs = b.tokens[...].astype(F32)
     inverse_one = lax.rsqrt(jnp.mean(inputs * inputs, axis=1, keepdims=True) + epsilon)
     b.tokens_grad[...] = (
@@ -1047,44 +1085,38 @@
         * (inverse_one * inverse_one * inverse_one)
         * jnp.mean(scaled * inputs, axis=1, keepdims=True)
     )
-
+    deliver("tokens_grad")
+
+
+    d_sum.second(direct=True)
     sum_ring.pass_on()
-
-    d_next = scatter_second(
-        links, d_first, d_part, (b.d_got0, b.d_got1), (b.d_last0, b.d_last1), d_cut
-    )
-    received(s_next)
     for part in range(2):
-        total = scatter_end(links, (b.s_got0, b.s_got1), (b.s_last0, b.s_last1), part)
-        b.back[:, W_ATT + 384 * part : W_ATT + 384 * part + 384] = total.astype(BF16)
-    received(d_next)
+        at = W_ATT + 384 * part
+        b.back[:, at : at + 384] = s_sum.total(part).astype(BF16)
     for part, cols in ((0, slice(0, 640)), (1, slice(640, 1152))):
-        total = scatter_end(links, (b.d_got0, b.d_got1), (b.d_last0, b.d_last1), part)
-        b.back[:, cols] = total.astype(BF16)
+        b.back[:, cols] = d_sum.total(part).astype(BF16)
     pick = pick_matrix((64, 48), lambda row: jnp.where(row % 16 < ROWS, row // 16 * ROWS + row % 16, -1))
     for col in range(0, W_ALL, 384):
         b.pack[:, :, col : col + 384] = moved(pick, b.back[:, col : col + 384]).reshape(4, 16, 384)
-    exchange = [
-        links.send(b.pack.at[lax.rem(x + step, 4)], b.arrived.at[x], "x", step)
-        for step in FAR_FIRST
-    ]
+    exchanged = exchange(pl.ds(0, W_ALL))
     b.arrived[x] = b.pack[x]
-    received(e_next)
     for part in range(2):
         rows = slice(48 * part, 48 * part + 48)
-        total = scatter_end(links, e_got, e_last, part)
+        total = e_sum.total(part)
         b.g_ein[rows] = total[:, 0:1024]
         b.g_eout[rows] = total[:, 1024:1536]
+    deliver("g_ein", "g_eout")
     result = sum_ring.total(b.hidden[...] + b.send_y[x, c].astype(F32))
     b.block_out[...] = result.astype(BF16)
-
-    sent(s_first + d_first)
-    for ring in (normed_ring, rows_ring, low_ring):
+    deliver("block_out")
+
+    for ring in (rows_ring, low_ring):
         ring.sent()
     for d in range(4):
         forward_rows(lax.rem(x + d, 4), d).wait_send()
-    sent(e_next + s_next + d_next)
-    received(exchange)
+    for plane_sum in (e_sum, s_sum, d_sum):
+        plane_sum.sent()
+    received(exchanged)
     gain_grad = jnp.zeros((ROWS, 1), F32)
     misc = jnp.zeros((ROWS, 128), F32)
     for k in range(4):
@@ -1107,13 +1139,22 @@
     b.g_router[...] = small[0:EXPERTS, 0:ROWS]
     b.g_gain_two[...] = small[8:9, 0:ROWS]
     b.g_gain_one[...] = small[9:10, 0:ROWS]
-    sent(exchange)
+    sent(exchanged)
+    deliver("g_gain_one", "g_qkv", "g_out", "g_gain_two", "g_router", "g_sin", "g_sout")
+    finish(results)
 
 
 def hand_over(*refs):
     n = len(OUTS)
-    for source, target in zip(refs[:n], refs[n:]):
-        target[...] = source[...]
+    sources, targets, held, sems = refs[:n], refs[n : 2 * n], refs[2 * n : 3 * n], refs[3 * n]
+    reads = [pltpu.make_async_copy(sources[i], held[i], sems.at[0, i]) for i in range(n)]
+    writes = [pltpu.make_async_copy(held[i], targets[i], sems.at[1, i]) for i in range(n)]
+    for read in reads:
+        read.start()
+    for read, write in zip(reads, writes):
+        read.wait()
+        write.start()
+    finish(writes)
 
 
 def local(
@@ -1134,11 +1175,12 @@
         kernel,
         out_shape=[jax.ShapeDtypeStruct(shape, dtype) for shape, dtype in OUTS.values()],
         in_specs=[pl.BlockSpec(memory_space=pltpu.VMEM)] * len(INS),
-        out_specs=[pl.BlockSpec(memory_space=pltpu.VMEM)] * len(OUTS),
+        out_specs=[pl.BlockSpec(memory_space=pl.ANY)] * len(OUTS),
         scratch_shapes=[
+            *[pltpu.VMEM(shape, dtype) for shape, dtype in OUTS.values()],
             *[pltpu.VMEM(shape, dtype) for shape, dtype in SCRATCH.values()],
-            pltpu.SemaphoreType.DMA((SEMS,)),
-            pltpu.SemaphoreType.DMA((SEMS,)),
+            pltpu.SemaphoreType.DMA((SENDS,)),
+            pltpu.SemaphoreType.DMA((RECEIVES,)),
         ],
         compiler_params=pltpu.CompilerParams(
             collective_id=1, has_side_effects=True, vmem_limit_bytes=(64 << 20) - (1 << 16)
@@ -1164,8 +1206,12 @@
     results = pl.pallas_call(
         hand_over,
         out_shape=[jax.ShapeDtypeStruct(shape, dtype) for shape, dtype in OUTS.values()],
-        in_specs=[pl.BlockSpec(memory_space=pltpu.VMEM)] * len(OUTS),
-        out_specs=[pl.BlockSpec(memory_space=pltpu.VMEM)] * len(OUTS),
+        in_specs=[pl.BlockSpec(memory_space=pl.ANY)] * len(OUTS),
+        out_specs=[pl.BlockSpec(memory_space=pl.ANY)] * len(OUTS),
+        scratch_shapes=[
+            *[pltpu.VMEM(shape, dtype) for shape, dtype in OUTS.values()],
+            pltpu.SemaphoreType.DMA((2, len(OUTS))),
+        ],
         name="hand_over",
     )(*results)
     block_out, tokens_grad, gain_one, qkv, out, gain_two, router, sin, sout, ein, eout = results

time: 160 us -> 154 us (0.963)
  Pallas kernels: 158 us -> 151 us
    pallas_call x1, Pallas kernels: 155 us -> 149 us  [local(): pl.pallas_call(kernel, out_shape=[jax.ShapeDtypeStruct(shape, dtype) for...]
where the time goes in v5:
time: 154 us; the launch traced here: 152 us
  Pallas kernels  151 us (98%)
    pallas_call x1, Pallas kernels, local(): pl.pallas_call(kernel, out_shape=[jax.ShapeDtypeStruct(shape, dtype) for...  149 us

profile of v5, /device:TPU:8, one launch (start us, length us, event | category | flops | bytes accessed | tf_op | source)
XLA Modules:
  0.0 152.3 jit_solution(15072395859666628335)
XLA Ops:
  0.6 148.8 %block.1 = (bf16[128,1536]{1,0:T(8,128)(2,1)}, f32[128,1536]{1,0:T(8,128)}, f32[1,12]{1,0:T(1,128)}, f32[12,2560]{1,0:T(8,128)}, f32[12,1536]{1,0:T(8,128)}, /*i...) custom-call(bf16[128,1536]{1,0:T(8,128)(2,1)} %refs_0_.1, ...), custom_call_target="tpu_custom_call" | custom-call | flops 23000000512 | bytes 10000000 | tf_op jit(solution)/shard_map/block/pallas_call | solution.py:1174
  149.4 2.7 %hand_over.1 = (bf16[128,1536]{1,0:T(8,128)(2,1)}, f32[128,1536]{1,0:T(8,128)}, f32[1,12]{1,0:T(1,128)}, f32[12,2560]{1,0:T(8,128)}, f32[12,1536]{1,0:T(8,128)},...) custom-call(bf16[128,1536]{1,0:T(8,128)(2,1)} %get-tuple-element.33., ...), custom_call_target="tpu_custom_call" | custom-call | tf_op jit(solution)/shard_map/hand_over/pallas_call | solution.py:1206

commit v6 on v5

--- a/solution.py
+++ b/solution.py
@@ -398,6 +398,17 @@
     "e_out",
     "out_grad",
 )
+HELD = {
+    "tokens": ((SEQ, D), BF16),
+    "ids": ((TOP, SEQ), jnp.int32),
+    "gain_one": ((1, ROWS), BF16),
+    "w_qkv": ((ROWS, 2560), BF16),
+    "w_out": ((ROWS, D), BF16),
+    "w_router": ((EXPERTS, ROWS), BF16),
+    "gain_two": ((1, ROWS), BF16),
+    "w_sin": ((ROWS, 2 * SH), BF16),
+    "w_sout": ((ROWS, SH), BF16),
+}
 OUTS = {
     "block_out": ((SEQ, D), BF16),
     "tokens_grad": ((SEQ, D), F32),
@@ -471,7 +482,13 @@
 
 def kernel(*refs):
     b = Bag()
-    names = [*INS, *(name + "_result" for name in OUTS), *OUTS, *SCRATCH]
+    names = [
+        *(name + "_given" for name in INS),
+        *(name + "_result" for name in OUTS),
+        *OUTS,
+        *HELD,
+        *SCRATCH,
+    ]
     for name, ref in zip(names, refs):
         setattr(b, name, ref)
     links = Links(*refs[len(names) :])
@@ -495,10 +512,16 @@
     e_part = lambda slots, half: b.got.at[(slots, *half)]
 
     greeted = links.greet("xyzc")
-    b.got[here, :, 0:1024] = b.e_in[...]
-    b.got[here, :, 1024:1536] = b.e_out[...]
+    loads = [links.local(getattr(b, name + "_given"), getattr(b, name)) for name in HELD]
+    loads += [
+        links.local(b.e_in_given, b.got.at[here, :, pl.ds(0, 1024)]),
+        links.local(b.e_out_given, b.got.at[here, :, pl.ds(1024, 512)]),
+        links.local(b.out_grad_given, b.cot.at[x, c]),
+    ]
     b.pack[...] = jnp.zeros_like(b.pack)
     b.small[...] = jnp.zeros_like(b.small)
+    finish(loads)
+    links.locals = 0
     b.small[0:EXPERTS, 0:ROWS] = b.w_router[...].astype(F32)
     b.small[8:9, 0:ROWS] = b.gain_two[...].astype(F32)
     b.small[9:10, 0:ROWS] = b.gain_one[...].astype(F32)
@@ -538,7 +561,6 @@
     inputs = b.tokens[...].astype(F32)
     inverse_one = lax.rsqrt(jnp.mean(inputs * inputs, axis=1, keepdims=True) + epsilon)
     b.normed[x] = (inputs * inverse_one).astype(BF16)
-    b.cot[x, c] = b.out_grad[...]
     cot_pair = links.send(b.cot.at[x, c], b.cot.at[x, c], "c", 1)
     b.arrived[x] = b.pack[x]
     finish(exchanged)
@@ -575,7 +597,6 @@
     for j in range(8):
         d_forward(j).start()
     e_ring = PlaneRing(links, e_first, e_part, e_cut)
-    s_ring = PlaneRing(links, s_first, s_part, s_cut)
     normed_ring.arrive()
 
     order = pick_matrix(
@@ -601,6 +622,8 @@
     def _(j):
         d_forward(j).wait()
         to_rows(j, b.dense, pl.ds(0, W_ATT), 0, W_ATT)
+
+    s_ring = PlaneRing(links, s_first, s_part, s_cut)
 
     mix_ring = SumRing(links, lambda s, rows: b.send_y.at[s, 0, rows], b.got_y)
 
@@ -627,7 +650,6 @@
     attend([x])
 
     e_ring.pass_on()
-    s_ring.pass_on()
     cot_ring.pass_on()
     e_hands = []
     lower, upper = pl.ds(0, 48), pl.ds(48, 48)
@@ -681,6 +703,7 @@
     )
     forward_cot = lambda s, d: links.copy(b.cot.at[s, c], b.cot.at[s, c], "c", 1, pair_cot + d)
     forward_rows(x, 0).start()
+    s_ring.pass_on()
     e_ring.arrive()
     e_hand(True)
     sent(e_first + s_first)
@@ -918,7 +941,7 @@
     inverse_two = lax.rsqrt(jnp.mean(hidden * hidden, axis=1, keepdims=True) + epsilon)
     scaled = gain_two * moe_in_grad
     hidden_grad = (
-        b.out_grad[...].astype(F32)
+        b.cot[x, c].astype(F32)
         + inverse_two * scaled
         - hidden
         * (inverse_two * inverse_two * inverse_two)
@@ -1174,11 +1197,13 @@
     results = pl.pallas_call(
         kernel,
         out_shape=[jax.ShapeDtypeStruct(shape, dtype) for shape, dtype in OUTS.values()],
-        in_specs=[pl.BlockSpec(memory_space=pltpu.VMEM)] * len(INS),
+        in_specs=[pl.BlockSpec(memory_space=pl.ANY)] * len(INS),
         out_specs=[pl.BlockSpec(memory_space=pl.ANY)] * len(OUTS),
         scratch_shapes=[
-            *[pltpu.VMEM(shape, dtype) for shape, dtype in OUTS.values()],
-            *[pltpu.VMEM(shape, dtype) for shape, dtype in SCRATCH.values()],
+            *[
+                pltpu.VMEM(shape, dtype)
+                for shape, dtype in (*OUTS.values(), *HELD.values(), *SCRATCH.values())
+            ],
             pltpu.SemaphoreType.DMA((SENDS,)),
             pltpu.SemaphoreType.DMA((RECEIVES,)),
         ],

time: 154 us -> 153 us (level)
  no operation moved by 1% of the time
where the time goes in v6:
time: 153 us; the launch traced here: 151 us
  Pallas kernels  150 us (98%)
    pallas_call x1, Pallas kernels, local(): pl.pallas_call(kernel, out_shape=[jax.ShapeDtypeStruct(shape, dtype) for...  148 us

profile of v6, /device:TPU:8, one launch (start us, length us, event | category | flops | bytes accessed | tf_op | source)
XLA Modules:
  0.0 151.2 jit_solution(9103711900147616980)
XLA Ops:
  0.6 147.7 %block.1 = (bf16[128,1536]{1,0:T(8,128)(2,1)}, f32[128,1536]{1,0:T(8,128)}, f32[1,12]{1,0:T(1,128)}, f32[12,2560]{1,0:T(8,128)}, f32[12,1536]{1,0:T(8,128)}, /*i...) custom-call(bf16[128,1536]{1,0:T(8,128)(2,1)} %refs_0_.1, ...), custom_call_target="tpu_custom_call" | custom-call | flops 23000000512 | bytes 10000000 | tf_op jit(solution)/shard_map/block/pallas_call | solution.py:1197
  148.4 2.7 %hand_over.1 = (bf16[128,1536]{1,0:T(8,128)(2,1)}, f32[128,1536]{1,0:T(8,128)}, f32[1,12]{1,0:T(1,128)}, f32[12,2560]{1,0:T(8,128)}, f32[12,1536]{1,0:T(8,128)},...) custom-call(bf16[128,1536]{1,0:T(8,128)(2,1)} %get-tuple-element.33., ...), custom_call_target="tpu_custom_call" | custom-call | tf_op jit(solution)/shard_map/hand_over/pallas_call | solution.py:1231

commit v7 on v6

--- a/solution.py
+++ b/solution.py
@@ -398,17 +398,7 @@
     "e_out",
     "out_grad",
 )
-HELD = {
-    "tokens": ((SEQ, D), BF16),
-    "ids": ((TOP, SEQ), jnp.int32),
-    "gain_one": ((1, ROWS), BF16),
-    "w_qkv": ((ROWS, 2560), BF16),
-    "w_out": ((ROWS, D), BF16),
-    "w_router": ((EXPERTS, ROWS), BF16),
-    "gain_two": ((1, ROWS), BF16),
-    "w_sin": ((ROWS, 2 * SH), BF16),
-    "w_sout": ((ROWS, SH), BF16),
-}
+FETCHED = ("tokens", "e_in", "e_out", "out_grad")
 OUTS = {
     "block_out": ((SEQ, D), BF16),
     "tokens_grad": ((SEQ, D), F32),
@@ -483,10 +473,10 @@
 def kernel(*refs):
     b = Bag()
     names = [
-        *(name + "_given" for name in INS),
+        *(name + "_given" if name in FETCHED else name for name in INS),
         *(name + "_result" for name in OUTS),
         *OUTS,
-        *HELD,
+        "tokens",
         *SCRATCH,
     ]
     for name, ref in zip(names, refs):
@@ -512,16 +502,14 @@
     e_part = lambda slots, half: b.got.at[(slots, *half)]
 
     greeted = links.greet("xyzc")
-    loads = [links.local(getattr(b, name + "_given"), getattr(b, name)) for name in HELD]
-    loads += [
+    loads = [
+        links.local(b.tokens_given, b.tokens),
         links.local(b.e_in_given, b.got.at[here, :, pl.ds(0, 1024)]),
         links.local(b.e_out_given, b.got.at[here, :, pl.ds(1024, 512)]),
         links.local(b.out_grad_given, b.cot.at[x, c]),
     ]
     b.pack[...] = jnp.zeros_like(b.pack)
     b.small[...] = jnp.zeros_like(b.small)
-    finish(loads)
-    links.locals = 0
     b.small[0:EXPERTS, 0:ROWS] = b.w_router[...].astype(F32)
     b.small[8:9, 0:ROWS] = b.gain_two[...].astype(F32)
     b.small[9:10, 0:ROWS] = b.gain_one[...].astype(F32)
@@ -545,6 +533,8 @@
             b.pack[k, 0:ROWS, at : at + 128] = b.w_sin[:, unit : unit + 128]
             b.pack[k, 0:ROWS, at + 128 : at + 256] = b.w_sin[:, SH + unit : SH + unit + 128]
             b.pack[k, 0:ROWS, at + 256 : at + 384] = b.w_sout[:, unit : unit + 128]
+    finish(loads)
+    links.locals = 0
     greeted()
 
     def exchange(cols):
@@ -1197,12 +1187,14 @@
     results = pl.pallas_call(
         kernel,
         out_shape=[jax.ShapeDtypeStruct(shape, dtype) for shape, dtype in OUTS.values()],
-        in_specs=[pl.BlockSpec(memory_space=pl.ANY)] * len(INS),
+        in_specs=[
+            pl.BlockSpec(memory_space=pl.ANY if name in FETCHED else pltpu.VMEM) for name in INS
+        ],
         out_specs=[pl.BlockSpec(memory_space=pl.ANY)] * len(OUTS),
         scratch_shapes=[
             *[
                 pltpu.VMEM(shape, dtype)
-                for shape, dtype in (*OUTS.values(), *HELD.values(), *SCRATCH.values())
+                for shape, dtype in (*OUTS.values(), ((SEQ, D), BF16), *SCRATCH.values())
             ],
             pltpu.SemaphoreType.DMA((SENDS,)),
             pltpu.SemaphoreType.DMA((RECEIVES,)),

time: 153 us -> 153 us (level)
  no operation moved by 1% of the time
where the time goes in v7:
time: 153 us; the launch traced here: 152 us
  Pallas kernels  151 us (99%)
    pallas_call x1, Pallas kernels, local(): pl.pallas_call(kernel, out_shape=[jax.ShapeDtypeStruct(shape, dtype) for...  148 us

profile of v7, /device:TPU:8, one launch (start us, length us, event | category | flops | bytes accessed | tf_op | source)
XLA Modules:
  0.0 151.9 jit_solution(3409270865859210926)
XLA Ops:
  0.6 148.4 %block.1 = (bf16[128,1536]{1,0:T(8,128)(2,1)}, f32[128,1536]{1,0:T(8,128)}, f32[1,12]{1,0:T(1,128)}, f32[12,2560]{1,0:T(8,128)}, f32[12,1536]{1,0:T(8,128)}, /*i...) custom-call(bf16[128,1536]{1,0:T(8,128)(2,1)} %refs_0_.1, ...), custom_call_target="tpu_custom_call" | custom-call | flops 23000000512 | bytes 10000000 | tf_op jit(solution)/shard_map/block/pallas_call | solution.py:1187
  149.0 2.7 %hand_over.1 = (bf16[128,1536]{1,0:T(8,128)(2,1)}, f32[128,1536]{1,0:T(8,128)}, f32[1,12]{1,0:T(1,128)}, f32[12,2560]{1,0:T(8,128)}, f32[12,1536]{1,0:T(8,128)},...) custom-call(bf16[128,1536]{1,0:T(8,128)(2,1)} %get-tuple-element.33., ...), custom_call_target="tpu_custom_call" | custom-call | tf_op jit(solution)/shard_map/hand_over/pallas_call | solution.py:1223
